TPU v7x, 32 devices: a whole 2x2x4 slice. The times are simulated.
32 devices in a mesh: row: 4 (over y, x), col: 8 (over z, core).
Axes of the slice: x: 2, y: 2, z: 4, core: 2. Of those that a mesh axis runs over, the one named last changes fastest.
Arguments:
- layer_input: bfloat16 [640, 8192], P('col', 'row'), may hold values from -6 to 6
- w_query: bfloat16 [8192, 8192], P('row', 'col'), may hold values from -0.0625 to 0.0625
- w_key: bfloat16 [8192, 1024], P('row', 'col'), may hold values from -0.0625 to 0.0625
- w_value: bfloat16 [8192, 1024], P('row', 'col'), may hold values from -0.0625 to 0.0625
- rotated_query_state: bfloat16 [640, 8192], P('row', 'col'), may hold values from -156 to 156
- rotated_key_state: bfloat16 [640, 1024], P('row', 'col'), may hold values from -6 to 6
- saved_value_state: bfloat16 [640, 1024], P('row', 'col'), may hold values from -6 to 6
- context_gradient: bfloat16 [640, 8192], P('row', 'col'), may hold values from -24 to 24
- positions: int32 [640], P('row'), may hold values from 0 to 542, as said below
- segment_ids: int32 [640], P('row'), may hold values from 0 to 1, as said below
Outputs:
- grad_input: bfloat16 [640, 8192], P('col', 'row')
- grad_wq: float32 [8192, 8192], P('row', 'col')
- grad_wk: float32 [8192, 1024], P('row', 'col')
- grad_wv: float32 [8192, 1024], P('row', 'col')
Inputs may be any that keep to these rules, and one draw needn't show every extreme that they name: `segment_ids`: never falls along the tokens; each of the 2 rollouts holds at least one token. `positions`: rises by one from each token to the next within a rollout.
All inputs are finite; a program needn't handle non-finite values.
Results may differ from a plain program's by a relative error of at most 0.025.
Values may be sent and summed in bfloat16 or wider, within the bound.
No kernel may reach another device: no remote copies, remote signals or barrier semaphores. Data moves between devices by JAX's collectives and lax.ppermute only.
A program may use at most 128 MiB of HBM per device.

v0:
```python
import math

import jax
import jax.numpy as jnp
from jax import lax
from jax.sharding import PartitionSpec as P

KEY_VALUE_HEADS = 8
HEAD_SIZE = 128


rope_base = 500000.0


def as_sent(shard):
    return jax.tree.map(lambda a: a.astype(jnp.bfloat16) if a.dtype == jnp.float32 else a, shard)


def partner_2(value, axis, apart):
    mask = 2**apart
    pairs = [(source, source ^ mask) for source in range(lax.axis_size(axis))]
    return lax.ppermute(value, axis, pairs)


def contract(left, right, left_dim, right_dim):
    return lax.dot_general(
        left, right, (((left_dim,), (right_dim,)), ((), ())), preferred_element_type=jnp.float32
    )


def rope_tables(positions):
    half_width = HEAD_SIZE // 2
    freq = jnp.exp(
        -(2.0 * jnp.arange(half_width, dtype=jnp.float32) / HEAD_SIZE) * math.log(rope_base)
    )
    angle = positions.astype(jnp.float32)[:, None] * freq[None, :]
    return (jnp.cos(angle), jnp.sin(angle))


def unrotate(gradient, cosine, sine):
    half_width = gradient.shape[-1] // 2
    first = gradient[..., :half_width]
    second = gradient[..., half_width:]
    return jnp.concatenate(
        [first * cosine + second * sine, second * cosine - first * sine], axis=-1
    )


def join_halves(mine, partner, bit_level, col_index):
    upper_bit = col_index >> bit_level & 1
    low_first = jnp.concatenate([mine, partner], axis=2)
    high_first = jnp.concatenate([partner, mine], axis=2)
    return jnp.where(upper_bit == 0, low_first, high_first)


def head_rows(states, head_count):
    count_rows = states.shape[0]
    return (
        states.reshape(count_rows, head_count, HEAD_SIZE)
        .transpose(1, 0, 2)
        .reshape(head_count * count_rows, HEAD_SIZE)
    )


def shards(
    layer_input,
    w_query,
    w_key,
    w_value,
    rotated_query_state,
    rotated_key_state,
    saved_value_state,
    context_gradient,
    positions,
    segment_ids,
):
    score_scale = HEAD_SIZE ** (-0.5)
    local_tokens = rotated_query_state.shape[0]
    head_count = rotated_query_state.shape[1] // HEAD_SIZE
    shared_heads = lax.axis_size("col") // KEY_VALUE_HEADS
    levels = shared_heads.bit_length() - 1
    col_index = lax.axis_index("col")
    labels = lax.all_gather(jnp.stack([positions, segment_ids]), "row", axis=1, tiled=True)
    key_count = labels.shape[1]
    visible = (segment_ids[:, None] == labels[1][None, :]) & (
        labels[0][None, :] <= positions[:, None]
    )
    key_pair = jnp.stack([rotated_key_state, saved_value_state], axis=1)
    key_pair = lax.all_gather(key_pair, "row", axis=0, tiled=True)
    for bit_level in range(levels):
        partner = partner_2(as_sent(key_pair), "col", bit_level).astype(key_pair.dtype)
        key_pair = join_halves(key_pair, partner, bit_level, col_index)
    key_full = key_pair[:, 0]
    value_full = key_pair[:, 1]
    query_rows = head_rows(rotated_query_state, head_count)
    grad_rows = head_rows(context_gradient, head_count)
    scores = (contract(query_rows, key_full, 1, 1) * score_scale).reshape(
        head_count, local_tokens, key_count
    )
    row_peak = jnp.max(jnp.where(visible[None], scores, -1e30), axis=-1, keepdims=True)
    exponent_terms = jnp.where(visible[None], jnp.exp(scores - row_peak), 0.0)
    row_total = jnp.sum(exponent_terms, axis=-1, keepdims=True)
    weights = exponent_terms / row_total
    dweights = contract(grad_rows, value_full, 1, 1).reshape(head_count, local_tokens, key_count)
    row_delta = jnp.sum(weights * dweights, axis=-1, keepdims=True)
    dscores = (weights * (dweights - row_delta) * score_scale).astype(jnp.bfloat16)
    flat_dscores = dscores.reshape(head_count * local_tokens, key_count)
    dquery_rot = (
        contract(flat_dscores, key_full, 1, 0)
        .reshape(head_count, local_tokens, HEAD_SIZE)
        .transpose(1, 0, 2)
    )
    cosine, sine = rope_tables(positions)
    dquery = (
        unrotate(dquery_rot, cosine[:, None], sine[:, None])
        .reshape(local_tokens, head_count * HEAD_SIZE)
        .astype(jnp.bfloat16)
    )
    weights_low = weights.astype(jnp.bfloat16).reshape(head_count * local_tokens, key_count)
    dkey_part = contract(flat_dscores, query_rows, 0, 0)
    dvalue_part = contract(weights_low, grad_rows, 0, 0)
    pair_grads = lax.psum_scatter(
        jnp.stack([dkey_part, dvalue_part], axis=1).astype(jnp.bfloat16),
        "row",
        scatter_dimension=0,
        tiled=True,
    ).astype(jnp.float32)
    key_unrotated = unrotate(pair_grads[:, 0], cosine, sine)
    pair_grads = jnp.stack([key_unrotated, pair_grads[:, 1]], axis=1)
    for bit_level in reversed(range(levels)):
        half_width = pair_grads.shape[2] // 2
        upper_bit = col_index >> bit_level & 1
        lower_part = pair_grads[:, :, :half_width]
        upper_part = pair_grads[:, :, half_width:]
        kept_half = jnp.where(upper_bit == 0, lower_part, upper_part)
        sent_half = jnp.where(upper_bit == 0, upper_part, lower_part)
        pair_grads = kept_half + partner_2(as_sent(sent_half), "col", bit_level).astype(
            sent_half.dtype
        )
    local_grads = jnp.concatenate(
        [dquery, pair_grads[:, 0].astype(jnp.bfloat16), pair_grads[:, 1].astype(jnp.bfloat16)],
        axis=1,
    )
    grads_full = lax.all_gather(local_grads, "row", axis=0, tiled=True)
    weights_all = jnp.concatenate([w_query, w_key, w_value], axis=1)
    matching = grads_full
    weight_grads = contract(lax.all_gather(layer_input, "col", axis=0, tiled=True), matching, 0, 0)
    matching = grads_full
    grad_input = lax.psum_scatter(
        contract(matching, weights_all, 1, 1).astype(jnp.bfloat16),
        "col",
        scatter_dimension=0,
        tiled=True,
    )
    query_cols = w_query.shape[1]
    key_cols = w_key.shape[1]
    grad_wq = weight_grads[:, :query_cols]
    grad_wk = weight_grads[:, query_cols : query_cols + key_cols]
    grad_wv = weight_grads[:, query_cols + key_cols :]
    return (grad_input, grad_wq, grad_wk, grad_wv)


def solution(mesh):
    return jax.shard_map(
        shards,
        mesh=mesh,
        in_specs=(
            P("col", "row"),
            P("row", "col"),
            P("row", "col"),
            P("row", "col"),
            P("row", "col"),
            P("row", "col"),
            P("row", "col"),
            P("row", "col"),
            P("row"),
            P("row"),
        ),
        out_specs=(P("col", "row"), P("row", "col"), P("row", "col"), P("row", "col")),
        check_vma=False,
    )
```

profile of v0, /device:TPU:0, one launch (start us, length us, event | category | flops | bytes accessed | tf_op | source)
XLA Modules:
  0.0 196.4 jit_solution(13045474186146518474)
XLA Ops:
  7.2 0.0 reduce-scatter.3.cloned.1.call-start
  7.2 0.7 add_bitcast_fusion
  8.0 9.5 %all-gather = s32[4,160,2]{1,2,0:T(2,128)S(1)} all-gather(s32[1,160,2]{1,2,0:T(2,128)S(1)} %add_bitcast_fusion), channel_id=1, replica_groups=mesh['row'=4,'col'=8] {'row'}, dimensions={0}, use_global_device_ids=true | all-gather | bytes 6400 | tf_op jit(solution)/shard_map/all_gather | solution.py:83
  17.5 0.1 reshape.175
  17.6 0.8 pad_maximum_fusion.1
  18.4 9.2 %all_gather.13 = bf16[640,2,128]{2,0,1:T(8,128)(2,1)S(1)} all-gather(bf16[160,2,128]{2,0,1:T(8,128)(2,1)S(1)} %pad_maximum_fusion.1), channel_id=1, replica_groups=mesh['row'=4,'col'=8] {'row'}, dimensions={0}, use_global_device_ids=true | all-gather | bytes 409600 | tf_op jit(solution)/shard_map/all_gather | solution.py:89
  27.6 1.0 copy_bitcast_fusion.2
  28.7 0.8 compare_and_fusion
  29.5 0.2 broadcast_in_dim.33
  29.8 0.9 copy.37
  30.7 2.4 %select_reduce_fusion = (f32[1280]{0:T(1024)S(1)}, f32[1280,640]{0,1:T(8,128)}) fusion(pred[1280,640]{0,1:T(32,128)(4,1)S(1)} %copy.37, bf16[1280,128]{1,0:T(8,128)(2,1)S(1)} %bitcast.107, bf16[640,2,128]{2,0,1:T(8,128)(2,1)S(1)} %all_gather.13), kind=kOutput, calls=%fused_computation.15 | convolution fusion | flops 212171520 | bytes 4592640 | tf_op jit(solution)/shard_map/dot_general | solution.py:26
  33.1 0.1 sub.43
  33.2 2.7 %fusion.11 = f32[1280]{0:T(1024)S(1)} fusion(pred[1280,640]{0,1:T(32,128)(4,1)S(1)} %copy.37, f32[1280,640]{0,1:T(8,128)} %get-tuple-element.29, f32[1280]{0:T(1024)S(1)} %get-tuple-element.28), kind=kLoop, calls=%fused_computation.18 | loop fusion | flops 2456320 | bytes 4106240 | tf_op jit(solution)/shard_map/reduce_sum | solution.py:102
  35.9 4.6 %copy.41 = f32[1280,640]{1,0:T(8,128)} copy(f32[1280,640]{0,1:T(8,128)} %get-tuple-element.29) | data formatting | bytes 6553600 | tf_op jit(solution)/shard_map/mul | solution.py:97
  40.5 0.1 copy_bitcast_fusion.1
  40.5 0.1 div.26
  40.6 4.6 %multiply_reduce_fusion = (f32[1280]{0:T(1024)S(1)}, f32[1280,640]{0,1:T(8,128)}) fusion(f32[1280]{0:T(1024)S(1)} %fusion.11, pred[1280,640]{0,1:T(32,128)(4,1)S(1)} %copy.37, f32[1280,640]{0,1:T(8,128)} %get-tuple-element.29, f32[1280]{0:T(1024)S(1)} %get-tuple-element.28, bf16[1280,128]{1,0:T(8,128)(2,1)S(1)} %bitcast.108, ...), kind=kOutput, calls=%fused_computation.13 | convolution fusion | flops 213809920 | bytes 7885824 | tf_op jit(solution)/shard_map/dot_general | solution.py:26
  45.2 0.1 sub.46
  45.3 4.6 %copy.42 = f32[1280,640]{1,0:T(8,128)} copy(f32[1280,640]{0,1:T(8,128)} %get-tuple-element.31) | data formatting | bytes 6553600 | tf_op jit(solution)/shard_map/dot_general | solution.py:26
  49.8 3.3 %fusion.26 = bf16[640,1,128]{2,0,1:T(8,128)(2,1)S(1)} fusion(f32[8,160,640]{2,1,0:T(8,128)} %bitcast.103, f32[8,160]{1,0:T(8,128)S(1)} %div.26, f32[8,160]{1,0:T(8,128)S(1)} %sub.43, pred[160,640]{1,0:T(8,128)(4,1)S(1)} %compare_and_fusion, bf16[160,1024]{1,0:T(8,128)(2,1)S(1)} %copy-done), kind=kOutput, calls=%fused_computation.30 | convolution fusion | flops 213073920 | bytes 3880960 | tf_op jit(solution)/shard_map/dot_general | solution.py:26
  53.2 0.6 copy-done.4
  53.7 1.6 fusion.25
  55.4 0.8 pad_maximum_fusion
  56.1 0.0 reduce-scatter.3.cloned.1.call-update
  56.2 0.0 all-gather.4.cloned.1.call-start
  56.2 4.0 %multiply_convert_fusion.1 = bf16[1280,640]{0,1:T(8,128)(2,1)S(1)} fusion(f32[1280,640]{0,1:T(8,128)} %get-tuple-element.31, f32[1280]{0:T(1024)S(1)} %get-tuple-element.30, f32[1280]{0:T(1024)S(1)} %fusion.11, pred[1280,640]{0,1:T(32,128)(4,1)S(1)} %copy.37, f32[1280,640]{0,1:T(8,128)} %get-tuple-element.29, f32[1280]{0:T(1024)S(1)} %get-tuple-element.28), kind=kLoop, calls=%fused_computation.12 | loop fusion | flops 5734400 | bytes 9026560 | tf_op jit(solution)/shard_map/convert_element_type | solution.py:106
  60.3 2.2 %copy.39 = bf16[1280,640]{1,0:T(8,128)(2,1)} copy(bf16[1280,640]{0,1:T(8,128)(2,1)S(1)} %multiply_convert_fusion.1) | data formatting | bytes 3276800 | tf_op jit(solution)/shard_map/convert_element_type | solution.py:106
  62.5 2.0 %convolution_bitcast_fusion.2 = f32[160,8,128]{2,0,1:T(8,128)S(1)} fusion(bf16[8,160,640]{2,1,0:T(8,128)(2,1)} %bitcast.102, bf16[640,2,128]{2,0,1:T(8,128)(2,1)S(1)} %all_gather.13), kind=kOutput, calls=%fused_computation.24 | convolution fusion | flops 209715200 | bytes 2457600 | tf_op jit(solution)/shard_map/dot_general | solution.py:26
  64.6 16.3 %reduce-scatter.3.cloned.1.call-done = bf16[160,2,128]{2,0,1:T(8,128)(2,1)} async-done(((bf16[640,2,128]{2,0,1:T(8,128)(2,1)}), bf16[160,2,128]{2,0,1:T(8,128)(2,1)}) %reduce-scatter.3.cloned.1.call-update) | async-done | bytes 81936 | tf_op jit(solution)/shard_map/reduce_scatter | solution.py:122
  80.9 0.8 slice_bitcast_fusion.2
  81.7 0.4 subtract_convert_fusion.1
  82.1 0.3 add_convert_fusion
  82.4 0.2 copy_bitcast_fusion
  82.6 0.9 concatenate.14
  83.5 0.0 all-gather.6.cloned.1.call-start
  83.5 0.7 all-gather.6.cloned.1.call-update
  84.2 0.2 reduce-scatter.5.cloned.1.call-start
  84.4 30.7 %all-gather.4.cloned.1.call-done = bf16[640,1280]{1,0:T(8,128)(2,1)} async-done(((bf16[160,1280]{1,0:T(8,128)(2,1)}), bf16[640,1280]{1,0:T(8,128)(2,1)}) %all-gather.4.cloned.1.call-update) | async-done | bytes 1638416 | tf_op jit(solution)/shard_map/all_gather | solution.py:144
  115.2 7.9 %fusion.7 = bf16[640,2048]{1,0:T(8,128)(2,1)} fusion(bf16[640,1280]{1,0:T(8,128)(2,1)} %all-gather.4.cloned.1.call-done, bf16[2048,128]{1,0:T(8,128)(2,1)S(1)} %copy-done.8, bf16[2048,128]{1,0:T(8,128)(2,1)S(1)} %copy-done.9, bf16[2048,1024]{1,0:T(8,128)(2,1)} %param.11), kind=kOutput, calls=%fused_computation.16 | convolution fusion | flops 3372482560 | bytes 9502720 | tf_op jit(solution)/shard_map/dot_general | solution.py:26
  123.1 27.6 %all-gather.6.cloned.1.call-done = bf16[640,2048]{1,0:T(8,128)(2,1)} async-done(((bf16[80,2048]{1,0:T(8,128)(2,1)}), bf16[640,2048]{1,0:T(8,128)(2,1)}) %all-gather.6.cloned.1.call-update) | async-done | bytes 2621456 | tf_op jit(solution)/shard_map/all_gather | solution.py:147
  150.7 6.0 %convolution_bitcast_fusion = f32[2048,1280]{0,1:T(8,128)S(1)} fusion(bf16[640,1280]{1,0:T(8,128)(2,1)S(1)} %copy-done.7, bf16[640,2048]{1,0:T(8,128)(2,1)} %all-gather.6.cloned.1.call-done), kind=kOutput, calls=%fused_computation | convolution fusion | flops 3355443200 | bytes 14745600 | tf_op jit(solution)/shard_map/dot_general | solution.py:26
  156.8 4.0 %copy-done.2 = f32[2048,1280]{0,1:T(8,128)} copy-done((f32[2048,1280]{0,1:T(8,128)}, f32[2048,1280]{0,1:T(8,128)S(1)}, u32[]{:S(2)}) %copy-start.2) | copy-done | bytes 10485784
  160.8 3.9 %slice.70 = f32[2048,1024]{0,1:T(8,128)} slice(f32[2048,1280]{0,1:T(8,128)S(1)} %convolution_bitcast_fusion), slice={[0:2048], [0:1024]} | slice | bytes 16777216 | tf_op jit(solution)/shard_map/slice | solution.py:157
  164.7 9.3 %copy.43 = f32[2048,1024]{1,0:T(8,128)} copy(f32[2048,1024]{0,1:T(8,128)} %slice.70) | data formatting | bytes 16777216
  174.0 1.7 fusion.40
  175.7 1.3 copy.45
  177.0 1.3 copy.44
  178.3 11.5 %reduce-scatter.5.cloned.1.call-done = bf16[80,2048]{1,0:T(8,128)(2,1)} async-done(((bf16[640,2048]{1,0:T(8,128)(2,1)}), bf16[80,2048]{1,0:T(8,128)(2,1)}) %reduce-scatter.5.cloned.1.call-update) | async-done | bytes 327696 | tf_op jit(solution)/shard_map/reduce_scatter | solution.py:149
  (24 shorter events, 0.1 us)
Async XLA Ops:
  7.2 33.3 %copy-start = (bf16[160,1024]{1,0:T(8,128)(2,1)S(1)}, bf16[160,1024]{1,0:T(8,128)(2,1)}, u32[]{:S(2)}) copy-start(bf16[160,1024]{1,0:T(8,128)(2,1)} %param.17) | copy-start | bytes 983044
  7.2 73.7 %reduce-scatter.3.cloned.1.call-start = ((), (), s32[]{:S(2)}) async-start(), calls=%async_computation.2 | async-start | bytes 409600 | tf_op jit(solution)/shard_map/reduce_scatter | solution.py:122
  49.8 3.3 %copy-start.3 = (f32[1280,640]{1,0:T(8,128)S(1)}, f32[1280,640]{1,0:T(8,128)}, u32[]{:S(2)}) copy-start(f32[1280,640]{1,0:T(8,128)} %copy.41) | copy-start | bytes 9830404
  49.8 3.9 %copy-start.4 = (f32[1280,640]{1,0:T(8,128)S(1)}, f32[1280,640]{1,0:T(8,128)}, u32[]{:S(2)}) copy-start(f32[1280,640]{1,0:T(8,128)} %copy.42) | copy-start | bytes 9830404
  49.8 3.9 %copy-start.5 = (bf16[160,1024]{1,0:T(8,128)(2,1)S(1)}, bf16[160,1024]{1,0:T(8,128)(2,1)}, u32[]{:S(2)}) copy-start(bf16[160,1024]{1,0:T(8,128)(2,1)} %param.14) | copy-start | bytes 983044
  56.2 4.1 %copy-start.6 = (s32[160]{0:T(256)S(1)}, s32[160]{0:T(256)}, u32[]{:S(2)}) copy-start(s32[160]{0:T(256)} %param.18) | copy-start | bytes 1924
  56.2 59.0 %all-gather.4.cloned.1.call-start = ((), (), s32[]{:S(2)}) async-start(), calls=%async_computation.3 | async-start | bytes 2048000 | tf_op jit(solution)/shard_map/all_gather | solution.py:144
  64.5 50.6 %copy-start.8 = (bf16[2048,128]{1,0:T(8,128)(2,1)S(1)}, bf16[2048,128]{1,0:T(8,128)(2,1)}, u32[]{:S(2)}) copy-start(bf16[2048,128]{1,0:T(8,128)(2,1)} %param.13) | copy-start | bytes 1572868
  64.6 50.6 %copy-start.9 = (bf16[2048,128]{1,0:T(8,128)(2,1)S(1)}, bf16[2048,128]{1,0:T(8,128)(2,1)}, u32[]{:S(2)}) copy-start(bf16[2048,128]{1,0:T(8,128)(2,1)} %param.12) | copy-start | bytes 1572868
  83.5 67.3 %all-gather.6.cloned.1.call-start = ((), (), s32[]{:S(2)}) async-start(), calls=%async_computation.5 | async-start | bytes 2949120 | tf_op jit(solution)/shard_map/all_gather | solution.py:147
  84.2 105.7 %reduce-scatter.5.cloned.1.call-start = ((), (), s32[]{:S(2)}) async-start(), calls=%async_computation.4 | async-start | bytes 2949120 | tf_op jit(solution)/shard_map/reduce_scatter | solution.py:149
  115.2 35.6 %copy-start.7 = (bf16[640,1280]{1,0:T(8,128)(2,1)S(1)}, bf16[640,1280]{1,0:T(8,128)(2,1)}, u32[]{:S(2)}) copy-start(bf16[640,1280]{1,0:T(8,128)(2,1)} %all-gather.4.cloned.1.call-done) | copy-start | bytes 4915204
  156.8 4.0 %copy-start.2 = (f32[2048,1280]{0,1:T(8,128)}, f32[2048,1280]{0,1:T(8,128)S(1)}, u32[]{:S(2)}) copy-start(f32[2048,1280]{0,1:T(8,128)S(1)} %convolution_bitcast_fusion) | copy-start | bytes 31457284
  164.7 25.2 %copy-start.1 = (bf16[160,1024]{1,0:T(8,128)(2,1)S(1)}, bf16[160,1024]{1,0:T(8,128)(2,1)}, u32[]{:S(2)}) copy-start(bf16[160,1024]{1,0:T(8,128)(2,1)} %param.17) | copy-start | bytes 983044
Sparse Core Ops, SparseCore 0:
  56.3 24.5 reduce-scatter.2
  83.6 31.5 all-gather.3
  116.8 33.8 all-gather.5
  153.5 36.3 reduce-scatter.4
where the time goes:
time: 197 us; the launch traced here: 196 us
  waiting for transfers between devices  87 us (44%)
  local copies, waits for them, and re-layouts  36.9 us (19%)
  matrix products  28 us (14%)
  blocking collectives  18.7 us (9%)
  between operations  13.9 us (7%)
  other arithmetic  11.6 us (6%)
    all_gather x1, waiting for transfers between devices, shards(): grads_full = lax.all_gather(local_grads, 'row', axis=0, tiled=True)  30.7 us
    dot_general x7, matrix products, contract(): lax.dot_general(left, right, (((left_dim,), (right_dim,)), ((), ())), pre...  28 us
    all_gather x1, waiting for transfers between devices, shards(): lax.all_gather(layer_input, 'col', axis=0, tiled=True)  27.6 us
    unnamed x24, local copies, waits for them, and re-layouts  16.6 us
    reduce_scatter x1, waiting for transfers between devices, shards(): lax.psum_scatter(jnp.stack([dkey_part, dvalue_part], axis=1).astype(jnp.b...  16.3 us
    reduce_scatter x1, waiting for transfers between devices, shards(): lax.psum_scatter(contract(matching, weights_all, 1, 1).astype(jnp.bfloat1...  11.5 us
    all_gather x1, blocking collectives, shards(): lax.all_gather(jnp.stack([positions, segment_ids]), 'row', axis=1, tiled=...  9.51 us
    all_gather x1, blocking collectives, shards(): key_pair = lax.all_gather(key_pair, 'row', axis=0, tiled=True)  9.24 us
  transfers between devices with their start and end apart: 4, of which 4 were waited for; matrix products, arithmetic and copies ran while one was open for 20% of the time, Pallas kernels for 0%

commit v1 on v0

v1 whole, which is shorter than its diff:
```python
import functools
import math

import jax
import jax.numpy as jnp
import numpy as np
from jax import lax
from jax.experimental import pallas as pl
from jax.experimental.pallas import tpu as pltpu
from jax.sharding import PartitionSpec as P

KEY_VALUE_HEADS = 8
HEAD_SIZE = 128
ROPE_BASE = 500000.0
PAD_ROWS = 16
MIB = 1024 * 1024


def contract(left, right, left_dim, right_dim):
    return lax.dot_general(
        left, right, (((left_dim,), (right_dim,)), ((), ())), preferred_element_type=jnp.float32
    )


def swap(value, axis, offset):
    pairs = [(source, source ^ offset) for source in range(lax.axis_size(axis))]
    return lax.ppermute(value, axis, pairs)


def gather_direct(value, axis):
    return [value] + [swap(value, axis, s) for s in range(1, lax.axis_size(axis))]


def add_low(left, right):
    return (left.astype(jnp.float32) + right.astype(jnp.float32)).astype(jnp.bfloat16)


def block_index(position, row, blocks, tokens):
    index = position
    for b in range(blocks):
        index = jnp.where(position >= b * tokens, position + ((row ^ b) - b) * tokens, index)
    return index.astype(jnp.float32)


def unrotate(gradient, cosine, sine):
    return gradient * cosine + pltpu.roll(gradient, HEAD_SIZE // 2, 1) * sine


def pack_kernel(k_ref, v_ref, ids_ref, out_ref):
    tokens = k_ref.shape[0]
    out_ref[:tokens, :HEAD_SIZE] = k_ref[...]
    out_ref[:tokens, HEAD_SIZE:] = v_ref[...]
    width = ids_ref.shape[1]
    row = lax.broadcasted_iota(jnp.int32, (PAD_ROWS, width), 0)
    ids = jnp.ones((PAD_ROWS, width), jnp.float32)
    for i in range(ids_ref.shape[0]):
        ids = jnp.where(row == i, ids_ref[i : i + 1, :].astype(jnp.float32), ids)
    out_ref[tokens:, :] = jnp.ones((PAD_ROWS, out_ref.shape[1]), jnp.bfloat16)
    out_ref[tokens:, :width] = ids.astype(jnp.bfloat16)


def pack(key, value, segment_ids):
    tokens = key.shape[0]
    width = 2 * HEAD_SIZE
    rows = -(-tokens // width)
    ids = segment_ids
    if rows > 1:
        ids = jnp.pad(ids, (0, rows * width - tokens), constant_values=1)
    ids = ids.reshape(rows, -1)
    vmem = pl.BlockSpec(memory_space=pltpu.VMEM)
    return pl.pallas_call(
        pack_kernel,
        out_shape=jax.ShapeDtypeStruct((tokens + PAD_ROWS, width), jnp.bfloat16),
        in_specs=[vmem] * 3,
        out_specs=vmem,
        compiler_params=pltpu.CompilerParams(vmem_limit_bytes=MIB),
        cost_estimate=pl.CostEstimate(
            flops=0, bytes_accessed=8 * tokens * HEAD_SIZE, transcendentals=0
        ),
        name="pack",
    )(
        pltpu.with_memory_space_constraint(key, pltpu.HBM),
        pltpu.with_memory_space_constraint(value, pltpu.HBM),
        pltpu.with_memory_space_constraint(ids, pltpu.HBM),
    )


def prepare_kernel(heads, blocks, row_ref, q_hbm, o_hbm, positions_ref, ids_ref, freq_ref, *refs):
    q_ref, o_ref, cos_ref, sin_ref, sems = refs
    tokens = q_hbm.shape[0]
    row = row_ref[0]
    copies = []
    for h in range(heads):
        rows = slice(h * tokens, (h + 1) * tokens)
        cols = slice(h * HEAD_SIZE, (h + 1) * HEAD_SIZE)
        for i, (source, target) in enumerate(((q_hbm, q_ref), (o_hbm, o_ref))):
            copies.append(
                pltpu.make_async_copy(source.at[:, cols], target.at[rows, :], sems.at[h, i])
            )
            copies[-1].start()

    first = (row * tokens).astype(jnp.float32)
    last = first + (tokens - 1)
    positions = positions_ref[...].astype(jnp.float32)
    cut = first + jnp.sum(1.0 - ids_ref[...].astype(jnp.float32), axis=1, keepdims=True)
    offset_low = positions[:, :1] - first
    offset_high = positions[:, tokens - 1 :] - last
    place = lax.broadcasted_iota(jnp.int32, (blocks * tokens, 1), 0)
    index = block_index(place, row, blocks, tokens)
    angle = (index + jnp.where(index < cut, offset_low, offset_high)) * freq_ref[...]
    lane = lax.broadcasted_iota(jnp.int32, (1, HEAD_SIZE), 1)
    lower = lane < HEAD_SIZE // 2
    table = jnp.cos(angle - jnp.where(lower, 0.0, math.pi / 2))
    turned = pltpu.roll(table, HEAD_SIZE // 2, 1)
    cos_ref[...] = jnp.where(lower, table, turned)
    sin_ref[...] = jnp.where(lower, turned, -table)

    for copy in copies:
        copy.wait()


def prepare(row, blocks, query, out_grad, positions, segment_ids):
    tokens, width = query.shape
    heads = width // HEAD_SIZE
    half_width = HEAD_SIZE // 2
    freq = np.exp(-(2.0 * np.arange(half_width) / HEAD_SIZE) * math.log(ROPE_BASE))
    freq = np.tile(freq, 2)[None].astype(np.float32)
    vmem = pl.BlockSpec(memory_space=pltpu.VMEM)
    hbm = pl.BlockSpec(memory_space=pltpu.HBM)
    return pl.pallas_call(
        functools.partial(prepare_kernel, heads, blocks),
        out_shape=[jax.ShapeDtypeStruct((heads * tokens, HEAD_SIZE), jnp.bfloat16)] * 2
        + [jax.ShapeDtypeStruct((blocks * tokens, HEAD_SIZE), jnp.float32)] * 2,
        in_specs=[pl.BlockSpec(memory_space=pltpu.SMEM), hbm, hbm, vmem, vmem, vmem],
        out_specs=[vmem] * 4,
        scratch_shapes=[pltpu.SemaphoreType.DMA((heads, 2))],
        compiler_params=pltpu.CompilerParams(vmem_limit_bytes=8 * MIB),
        cost_estimate=pl.CostEstimate(
            flops=0,
            bytes_accessed=8 * tokens * width,
            transcendentals=2 * blocks * tokens * HEAD_SIZE,
        ),
        name="prepare",
    )(
        row,
        pltpu.with_memory_space_constraint(query, pltpu.HBM),
        pltpu.with_memory_space_constraint(out_grad, pltpu.HBM),
        pltpu.with_memory_space_constraint(positions.reshape(1, -1), pltpu.HBM),
        pltpu.with_memory_space_constraint(segment_ids.reshape(1, -1), pltpu.HBM),
        pltpu.with_memory_space_constraint(jnp.asarray(freq), pltpu.HBM),
    )


def attention_kernel(heads, blocks, row_ref, q_all, o_all, *refs):
    kv_refs = refs[:blocks]
    cos_ref, sin_ref = refs[blocks : blocks + 2]
    dq_refs, packet_refs = refs[blocks + 2 : blocks + 4], refs[blocks + 4 : blocks + 6]
    k_all, v_all, ds_all, w_all, bias_ref, scores_ref, dweights_ref = refs[blocks + 6 :]
    together = scores_ref.shape[0] // bias_ref.shape[0]
    tokens = q_all.shape[0] // heads
    width = dq_refs[0].shape[1]
    keys = tokens * blocks
    scale = HEAD_SIZE**-0.5
    row = row_ref[0]

    cut = jnp.zeros((1, 1), jnp.float32)
    for b in range(blocks):
        rows = slice(b * tokens, (b + 1) * tokens)
        k_all[rows, :] = kv_refs[b][:tokens, :HEAD_SIZE]
        v_all[rows, :] = kv_refs[b][:tokens, HEAD_SIZE:]
        first = 1.0 - kv_refs[b][tokens:, :].astype(jnp.float32)
        cut += jnp.sum(jnp.sum(first, axis=0, keepdims=True), axis=1, keepdims=True)
    lane = lax.broadcasted_iota(jnp.int32, (1, keys), 1)
    key_index = block_index(lane, row, blocks, tokens)
    query_index = (
        lax.broadcasted_iota(jnp.int32, (tokens, 1), 0) + row * tokens
    ).astype(jnp.float32)
    lowest = jnp.where(query_index < cut, 0.0, cut)
    visible = (key_index <= query_index) & (key_index >= lowest)
    bias_ref[...] = jnp.where(visible, 0.0, -1e30)

    for h in range(heads):
        if h % together == 0:
            rows = slice(h * tokens, (h + together) * tokens)
            scores_ref[...] = contract(q_all[rows, :], k_all[...], 1, 1)
            dweights_ref[...] = contract(o_all[rows, :], v_all[...], 1, 1)
        rows = slice(h % together * tokens, (h % together + 1) * tokens)
        scores = scores_ref[rows, :] + bias_ref[...]
        peak = jnp.max(scores, axis=1, keepdims=True)
        terms = jnp.exp2((scores - peak) * (scale * math.log2(math.e)))
        inverse = 1.0 / jnp.sum(terms, axis=1, keepdims=True)
        dweights = dweights_ref[rows, :]
        weights = terms * inverse
        delta = jnp.sum(weights * dweights, axis=1, keepdims=True)
        dscores = (weights * (dweights - delta) * scale).astype(jnp.bfloat16)
        rows = slice(h * tokens, (h + 1) * tokens)
        w_all[rows, :] = weights.astype(jnp.bfloat16)
        ds_all[rows, :] = dscores
    dq = contract(ds_all[...], k_all[...], 1, 0)
    for h in range(heads):
        side, first = divmod(h * HEAD_SIZE, width)
        cols = slice(first, first + HEAD_SIZE)
        head = dq[h * tokens : (h + 1) * tokens]
        head = unrotate(head, cos_ref[:tokens, :], sin_ref[:tokens, :]).astype(jnp.bfloat16)
        dq_refs[side][:, cols] = head
        packet_refs[side][:, cols] = head
    dk = contract(ds_all[...], q_all[...], 0, 0)
    dk = unrotate(dk, cos_ref[...], sin_ref[...]).astype(jnp.bfloat16)
    dv = contract(w_all[...], o_all[...], 0, 0).astype(jnp.bfloat16)
    for b in range(blocks):
        rows = slice(b * tokens, (b + 1) * tokens)
        cols = slice(width + b * HEAD_SIZE, width + (b + 1) * HEAD_SIZE)
        packet_refs[0][:, cols] = dk[rows]
        packet_refs[1][:, cols] = dv[rows]


def attention_backward(row, query, out_grad, packed, cosine, sine):
    blocks = len(packed)
    keys = cosine.shape[0]
    tokens = keys // blocks
    heads = query.shape[0] // tokens
    width = heads // 2 * HEAD_SIZE
    vmem = pl.BlockSpec(memory_space=pltpu.VMEM)
    return pl.pallas_call(
        functools.partial(attention_kernel, heads, blocks),
        out_shape=[jax.ShapeDtypeStruct((tokens, width), jnp.bfloat16)] * 2
        + [jax.ShapeDtypeStruct((tokens, width + blocks * HEAD_SIZE), jnp.bfloat16)] * 2,
        in_specs=[pl.BlockSpec(memory_space=pltpu.SMEM)] + [vmem] * (blocks + 4),
        out_specs=[vmem] * 4,
        scratch_shapes=[
            pltpu.VMEM((keys, HEAD_SIZE), jnp.bfloat16),
            pltpu.VMEM((keys, HEAD_SIZE), jnp.bfloat16),
            pltpu.VMEM((heads * tokens, keys), jnp.bfloat16),
            pltpu.VMEM((heads * tokens, keys), jnp.bfloat16),
            pltpu.VMEM((tokens, keys), jnp.float32),
            pltpu.VMEM((min(4, heads) * tokens, keys), jnp.float32),
            pltpu.VMEM((min(4, heads) * tokens, keys), jnp.float32),
        ],
        compiler_params=pltpu.CompilerParams(vmem_limit_bytes=32 * MIB),
        cost_estimate=pl.CostEstimate(
            flops=10 * heads * tokens * keys * HEAD_SIZE,
            bytes_accessed=16 * tokens * width + 16 * keys * HEAD_SIZE,
            transcendentals=heads * tokens * keys,
        ),
        name="attention_backward",
    )(row, query, out_grad, *packed, cosine, sine)


def combine_kernel(blocks, offset, columns, width, *refs):
    packet_ref, other_ref, out_ref = refs[0], refs[1], refs[-1]
    for i, first in enumerate(columns):
        out_ref[:, i * width : (i + 1) * width] = refs[2 + i][:, first : first + width]
    for b in range(blocks):
        first = len(columns) * width + b * HEAD_SIZE
        out_ref[:, first : first + HEAD_SIZE] = summed_block(
            packet_ref, other_ref, blocks, b, offset, slice(None)
        )


def summed_block(packet_ref, other_ref, blocks, b, offset, rows):
    first = packet_ref.shape[1] - (blocks - b) * HEAD_SIZE
    total = packet_ref[rows, first : first + HEAD_SIZE].astype(jnp.float32)
    first = other_ref.shape[1] - (blocks - (b ^ offset)) * HEAD_SIZE
    total += other_ref[rows, first : first + HEAD_SIZE].astype(jnp.float32)
    return total.astype(jnp.bfloat16)


def combine(packet, other, pieces, blocks, offset, width):
    tokens = packet.shape[0]
    cols = len(pieces) * width + blocks * HEAD_SIZE
    vmem = pl.BlockSpec(memory_space=pltpu.VMEM)
    return pl.pallas_call(
        functools.partial(combine_kernel, blocks, offset, [c for _, c in pieces], width),
        out_shape=jax.ShapeDtypeStruct((tokens, cols), jnp.bfloat16),
        in_specs=[vmem] * (2 + len(pieces)),
        out_specs=vmem,
        compiler_params=pltpu.CompilerParams(vmem_limit_bytes=4 * MIB),
        cost_estimate=pl.CostEstimate(
            flops=tokens * cols, bytes_accessed=6 * tokens * cols, transcendentals=0
        ),
        name="combine",
    )(packet, other, *[a for a, _ in pieces])


def spread(own, packet, bits, blocks):
    width = own.shape[1]
    held, newest, other, last = {0: (own, 0)}, {}, None, None
    for bit in bits:
        arrived = {}
        if newest:
            for offset, (array, first) in held.items():
                if array.shape[1] != width:
                    array = array[:, first : first + width]
                arrived[offset ^ bit] = (swap(array, "row", bit), 0)
            packet = combine(packet, other, list(newest.values()), blocks, last, width)
        sent = list(newest) if newest else [0]
        other = swap(packet, "row", bit)
        held.update(newest)
        arrived |= {offset ^ bit: (other, i * width) for i, offset in enumerate(sent)}
        newest, last = arrived, bit
    held.update(newest)
    return held, {offset ^ last for offset in sent}, packet, other, last


def turn_kernel(tile, wq_hbm, wk_hbm, wv_hbm, *refs):
    out_ref, wq, wk, wv, sems = refs[-5:]
    steps = wq.shape[0] // tile
    copies = []
    for j in range(steps):
        rows = slice(j * tile, (j + 1) * tile)
        copies.append(
            [
                pltpu.make_async_copy(source.at[rows, :], target.at[rows, :], sems.at[j, i])
                for i, (source, target) in enumerate(
                    ((wq_hbm, wq), (wk_hbm, wk), (wv_hbm, wv))
                )
            ]
        )
        for copy in copies[j]:
            copy.start()
    for j in range(steps):
        rows = slice(j * tile, (j + 1) * tile)
        first = 0
        for copy, weight in zip(copies[j], (wq, wk, wv)):
            copy.wait()
            out_ref[first : first + weight.shape[1], rows] = weight[rows, :].T
            first += weight.shape[1]


def turn_weights(weights, after):
    features = weights[0].shape[0]
    widths = [w.shape[1] for w in weights]
    tile = min(512, features)
    hbm = pl.BlockSpec(memory_space=pltpu.HBM)
    return pl.pallas_call(
        functools.partial(turn_kernel, tile),
        out_shape=pltpu.VMEM((sum(widths), features), jnp.bfloat16),
        in_specs=[hbm] * 3 + [pl.BlockSpec(memory_space=pl.ANY)] * len(after),
        out_specs=pl.BlockSpec(memory_space=pltpu.VMEM),
        scratch_shapes=[pltpu.VMEM((features, width), jnp.bfloat16) for width in widths]
        + [pltpu.SemaphoreType.DMA((features // tile, 3))],
        compiler_params=pltpu.CompilerParams(vmem_limit_bytes=16 * MIB),
        cost_estimate=pl.CostEstimate(
            flops=0, bytes_accessed=4 * features * sum(widths), transcendentals=0
        ),
        name="turn_weights",
    )(*[pltpu.with_memory_space_constraint(w, pltpu.HBM) for w in weights], *after)


def early_kernel(columns, tile, *refs):
    count, width = len(columns[0]), refs[-1].shape[1] // 2
    w_ref, out_ref, gq = refs[2 * count :]
    tokens = refs[0].shape[0]
    for i in range(2):
        for k, first in enumerate(columns[i]):
            gq[k * tokens : (k + 1) * tokens, i * width : (i + 1) * width] = refs[
                i * count + k
            ][:, first : first + width]
    for j in range(w_ref.shape[1] // tile):
        cols = slice(j * tile, (j + 1) * tile)
        out_ref[:, cols] = contract(gq[...], w_ref[: 2 * width, cols], 1, 0).astype(
            jnp.bfloat16
        )


def early_product(pieces, blocks, width, weights):
    arrays = [side[b][0] for side in pieces for b in blocks]
    columns = [[side[b][1] for b in blocks] for side in pieces]
    tokens = arrays[0].shape[0]
    features = weights.shape[1]
    tile = min(1024, features)
    rows = len(blocks) * tokens
    vmem = pl.BlockSpec(memory_space=pltpu.VMEM)
    return pl.pallas_call(
        functools.partial(early_kernel, columns, tile),
        out_shape=jax.ShapeDtypeStruct((rows, features), jnp.bfloat16),
        in_specs=[vmem] * (len(arrays) + 1),
        out_specs=vmem,
        scratch_shapes=[pltpu.VMEM((rows, 2 * width), jnp.bfloat16)],
        compiler_params=pltpu.CompilerParams(vmem_limit_bytes=16 * MIB),
        cost_estimate=pl.CostEstimate(
            flops=4 * rows * features * width,
            bytes_accessed=4 * features * width + 2 * rows * features + 4 * rows * width,
            transcendentals=0,
        ),
        name="early_product",
    )(*arrays, weights)


def put_pair(target_ref, target, first, sums, offsets, blocks, b, start):
    count = target.stop - target.start
    if offsets is None:
        tokens = sums[0].shape[0] // blocks
        rows = pl.ds(pl.multiple_of(b * tokens + start, 16), count)
        target_ref[target, first:] = sums[0][rows, :]
        return
    rows = pl.ds(pl.multiple_of(start, 16), count)
    for i in range(2):
        cols = slice(first + i * HEAD_SIZE, first + (i + 1) * HEAD_SIZE)
        target_ref[target, cols] = summed_block(
            sums[2 * i], sums[2 * i + 1], blocks, b, offsets[i], rows
        )


def by_destination(blocks, half, place_ref, put):
    core, turn = place_ref[0], place_ref[1]
    for q in range(blocks):
        for b in range(blocks):

            @pl.when((q ^ turn) == b)
            def _():
                for side in range(2):
                    first = (side * blocks + q) * half
                    put(q, side, slice(first, first + half), b, (core ^ side) * half)


def last_kernel(early, late, columns, offsets, part, width, spare, place_ref, *refs):
    blocks = len(early) + len(late)
    early_ref, w_ref, refs = refs[0], refs[1], refs[2 + spare :]
    pieces = [refs[i * len(late) : (i + 1) * len(late)] for i in range(2)]
    refs = refs[2 * len(late) :]
    count = 1 if offsets is None else 4
    sums, refs = refs[:count], refs[count:]
    mine_refs, other_ref, gq, gkv, query, pair = refs[:blocks], *refs[blocks:]
    half = mine_refs[0].shape[0]
    tokens = 2 * half
    cols = slice(part * other_ref.shape[1], (part + 1) * other_ref.shape[1])

    for i in range(2):
        for k, first in enumerate(columns[i]):
            gq[k * tokens : (k + 1) * tokens, i * width : (i + 1) * width] = pieces[i][k][
                :, first : first + width
            ]

    def put_rows(q, side, target, b, start):
        put_pair(gkv, target, 0, sums, offsets, blocks, b, start)

    by_destination(blocks, half, place_ref, put_rows)
    query[...] = contract(gq[...], w_ref[: 2 * width, cols], 1, 0).astype(jnp.bfloat16)
    pair[...] = contract(gkv[...], w_ref[2 * width :, cols], 1, 0)

    def put_sum(q, side, target, b, start):
        if b in late:
            rows = pl.ds(pl.multiple_of(late.index(b) * tokens + start, 16), half)
            part_sum = query[rows, :]
        else:
            rows = pl.ds(pl.multiple_of(early.index(b) * tokens + start, 16), half)
            part_sum = early_ref[rows, cols]
        total = (pair[target, :] + part_sum.astype(jnp.float32)).astype(jnp.bfloat16)
        if side:
            other_ref[q * half : (q + 1) * half, :] = total
        else:
            mine_refs[q][...] = total

    by_destination(blocks, half, place_ref, put_sum)


def last_product(place, early, late, early_part, pieces, sums, offsets, weights, width, part, after):
    blocks = len(early) + len(late)
    arrays = [side[b][0] for side in pieces for b in late]
    columns = [[side[b][1] for b in late] for side in pieces]
    tokens = arrays[0].shape[0]
    half, cols = tokens // 2, weights.shape[1] // 2
    pair_cols = weights.shape[0] - 2 * width
    vmem = pl.BlockSpec(memory_space=pltpu.VMEM)
    *mine, other = pl.pallas_call(
        functools.partial(
            last_kernel, early, late, columns, offsets, part, width, len(after)
        ),
        out_shape=[jax.ShapeDtypeStruct((half, cols), jnp.bfloat16)] * blocks
        + [jax.ShapeDtypeStruct((blocks * half, cols), jnp.bfloat16)],
        in_specs=[pl.BlockSpec(memory_space=pltpu.SMEM)]
        + [vmem] * 2
        + [pl.BlockSpec(memory_space=pl.ANY)] * len(after)
        + [vmem] * (len(arrays) + len(sums)),
        out_specs=[vmem] * (blocks + 1),
        scratch_shapes=[
            pltpu.VMEM((len(late) * tokens, 2 * width), jnp.bfloat16),
            pltpu.VMEM((blocks * tokens, pair_cols), jnp.bfloat16),
            pltpu.VMEM((len(late) * tokens, cols), jnp.bfloat16),
            pltpu.VMEM((blocks * tokens, cols), jnp.float32),
        ],
        compiler_params=pltpu.CompilerParams(vmem_limit_bytes=16 * MIB),
        cost_estimate=pl.CostEstimate(
            flops=2 * tokens * cols * (len(late) * 2 * width + blocks * pair_cols),
            bytes_accessed=2 * cols * (2 * width + pair_cols) + 8 * blocks * tokens * cols,
            transcendentals=0,
        ),
        name="last_product",
    )(place, early_part, weights, *after, *arrays, *sums)
    return mine, other


def order_kernel(blocks, columns, offsets, width, place_ref, *refs):
    pieces = [refs[i * blocks : (i + 1) * blocks] for i in range(2)]
    sums, g = refs[2 * blocks : -2], refs[-1]
    half = g.shape[0] // (2 * blocks)

    def put(q, side, target, b, start):
        rows = pl.ds(pl.multiple_of(start, 16), half)
        for i in range(2):
            first = columns[i][b]
            g[target, i * width : (i + 1) * width] = pieces[i][b][rows, first : first + width]
        put_pair(g, target, 2 * width, sums, offsets, blocks, b, start)

    by_destination(blocks, half, place_ref, put)


def order_rows(place, pieces, sums, offsets, width, cols, after):
    blocks = len(pieces[0])
    arrays = [side[b][0] for side in pieces for b in range(blocks)]
    columns = [[side[b][1] for b in range(blocks)] for side in pieces]
    rows = blocks * arrays[0].shape[0]
    vmem = pl.BlockSpec(memory_space=pltpu.VMEM)
    return pl.pallas_call(
        functools.partial(order_kernel, blocks, columns, offsets, width),
        out_shape=jax.ShapeDtypeStruct((rows, cols), jnp.bfloat16),
        in_specs=[pl.BlockSpec(memory_space=pltpu.SMEM)]
        + [vmem] * (len(arrays) + len(sums))
        + [pl.BlockSpec(memory_space=pl.ANY)],
        out_specs=vmem,
        compiler_params=pltpu.CompilerParams(vmem_limit_bytes=8 * MIB),
        cost_estimate=pl.CostEstimate(
            flops=0, bytes_accessed=4 * rows * cols, transcendentals=0
        ),
        name="order_rows",
    )(place, *arrays, *sums, after)


def join_kernel(count, *refs):
    sources, out_ref, sems = refs[:count], refs[count + 1], refs[count + 2]
    rows = sources[0].shape[0]
    copies = [
        pltpu.make_async_copy(source, out_ref.at[i * rows : (i + 1) * rows, :], sems.at[i])
        for i, source in enumerate(sources)
    ]
    for copy in copies:
        copy.start()
    for copy in copies:
        copy.wait()


def join_rows(arrays, after):
    count = len(arrays)
    rows, cols = arrays[0].shape
    return pl.pallas_call(
        functools.partial(join_kernel, count),
        out_shape=jax.ShapeDtypeStruct((count * rows, cols), arrays[0].dtype),
        in_specs=[pl.BlockSpec(memory_space=pl.ANY)] * (count + 1),
        out_specs=pl.BlockSpec(memory_space=pltpu.VMEM),
        scratch_shapes=[pltpu.SemaphoreType.DMA((count,))],
        compiler_params=pltpu.CompilerParams(vmem_limit_bytes=4 * MIB),
        cost_estimate=pl.CostEstimate(
            flops=0, bytes_accessed=4 * count * rows * cols, transcendentals=0
        ),
        name="join_rows",
    )(*arrays, after)


def weight_grad_kernel(places, g_ref, *refs):
    pieces = len(places)
    x_refs = refs[:pieces]
    gwq_ref, gwk_ref, gwv_ref, x_all = refs[pieces:]
    query_cols, key_cols = gwq_ref.shape[1], gwk_ref.shape[1]
    rows = x_refs[0].shape[0]
    for place, x_ref in zip(places, x_refs):
        x_all[place * rows : (place + 1) * rows, :] = x_ref[...]
    x = x_all[...]
    gwq_ref[...] = contract(x, g_ref[:, :query_cols], 0, 0)
    pair = contract(x, g_ref[:, query_cols:], 0, 0)
    gwk_ref[...] = pair[:, :key_cols]
    gwv_ref[...] = pair[:, key_cols:]


def weight_grads(g, x_parts, order, query_cols):
    chips = len(order)
    features = x_parts[0].shape[1]
    piece_tokens = g.shape[0] // (2 * chips)
    places = [core * chips + q for core in range(2) for q in order]
    counts = [part.shape[0] // piece_tokens for part in x_parts]
    key_cols = (g.shape[1] - query_cols) // 2
    tile = min(256, features)
    return pl.pallas_call(
        functools.partial(weight_grad_kernel, places),
        grid=(features // tile,),
        out_shape=[
            jax.ShapeDtypeStruct((features, query_cols), jnp.float32),
            jax.ShapeDtypeStruct((features, key_cols), jnp.float32),
            jax.ShapeDtypeStruct((features, key_cols), jnp.float32),
        ],
        in_specs=[pl.BlockSpec(g.shape, lambda i: (0, 0))]
        + [
            pl.BlockSpec((piece_tokens, tile), lambda i, k=k: (k, i))
            for count in counts
            for k in range(count)
        ],
        out_specs=[
            pl.BlockSpec((tile, query_cols), lambda i: (i, 0)),
            pl.BlockSpec((tile, key_cols), lambda i: (i, 0)),
            pl.BlockSpec((tile, key_cols), lambda i: (i, 0)),
        ],
        scratch_shapes=[pltpu.VMEM((g.shape[0], tile), jnp.bfloat16)],
        compiler_params=pltpu.CompilerParams(vmem_limit_bytes=32 * MIB),
        cost_estimate=pl.CostEstimate(
            flops=2 * g.size * features,
            bytes_accessed=2 * g.size + 2 * g.shape[0] * features + 4 * features * g.shape[1],
            transcendentals=0,
        ),
        name="weight_grads",
    )(g, *[x for x, n in zip(x_parts, counts) for _ in range(n)])


def sum_kernel(count, groups, *refs):
    out_ref = refs[-1]
    for i in range(groups):
        cols = slice(
            i * out_ref.shape[1] // groups, (i + 1) * out_ref.shape[1] // groups
        )
        total = refs[i * count][...].astype(jnp.float32)
        for ref in refs[i * count + 1 : (i + 1) * count]:
            total += ref[...].astype(jnp.float32)
        for ref in refs[groups * count : -2]:
            total += ref[:, cols].astype(jnp.float32)
        out_ref[:, cols] = total.astype(out_ref.dtype)


def sum_rows(groups, whole, after):
    rows, cols = groups[0][0].shape
    terms = [term for group in groups for term in group] + whole
    vmem = pl.BlockSpec(memory_space=pltpu.VMEM)
    return pl.pallas_call(
        functools.partial(sum_kernel, len(groups[0]), len(groups)),
        out_shape=jax.ShapeDtypeStruct((rows, cols * len(groups)), jnp.bfloat16),
        in_specs=[vmem] * len(terms) + [pl.BlockSpec(memory_space=pl.ANY)],
        out_specs=vmem,
        compiler_params=pltpu.CompilerParams(vmem_limit_bytes=4 * MIB),
        cost_estimate=pl.CostEstimate(
            flops=len(terms) * rows * cols,
            bytes_accessed=4 * len(terms) * rows * cols,
            transcendentals=0,
        ),
        name="sum_rows",
    )(*terms, pltpu.with_memory_space_constraint(after, pltpu.HBM))


def shards(
    layer_input,
    w_query,
    w_key,
    w_value,
    rotated_query_state,
    rotated_key_state,
    saved_value_state,
    context_gradient,
    positions,
    segment_ids,
):
    tokens = rotated_query_state.shape[0]
    n_row, n_col = lax.axis_size("row"), lax.axis_size("col")
    chips = n_col // 2
    shared_heads = n_col // KEY_VALUE_HEADS
    row_index = lax.axis_index("row").astype(jnp.int32)
    col_index = lax.axis_index("col").astype(jnp.int32)
    chip_index, core_index = col_index // 2, col_index % 2

    key, value = rotated_key_state, saved_value_state
    if shared_heads > 1:
        pair = jnp.concatenate([key, value], axis=1)
        pair = [pair] + [swap(pair, "col", s) for s in range(1, shared_heads)]
        part = col_index % shared_heads
        stacked = jnp.stack(pair)
        stacked = jnp.take(stacked, jnp.arange(shared_heads) ^ part, axis=0)
        stacked = stacked.reshape(shared_heads, tokens, 2, -1).transpose(1, 2, 0, 3)
        stacked = stacked.reshape(tokens, 2, HEAD_SIZE)
        key, value = stacked[:, 0], stacked[:, 1]
    packed = gather_direct(pack(key, value, segment_ids), "row")

    row = row_index.reshape(1)
    query, out_grad, cosine, sine = prepare(
        row, n_row, rotated_query_state, context_gradient, positions, segment_ids
    )
    first, second, *packets = attention_backward(row, query, out_grad, packed, cosine, sine)
    bits = [1 << i for i in range(n_row.bit_length() - 1)]
    pieces, sums, offsets, late = [], [], [], set()
    for own, packet, order in zip((first, second), packets, (bits, bits[::-1])):
        held, with_last, *last_two, offset = spread(own, packet, order, n_row)
        pieces.append(held)
        late |= with_last
        sums += last_two
        offsets.append(offset)

    if shared_heads > 1:
        dkv = []
        for i in range(2):
            packet, other = (a[:, -n_row * HEAD_SIZE :] for a in sums[2 * i : 2 * i + 2])
            packet, other = (a.reshape(tokens, n_row, HEAD_SIZE) for a in (packet, other))
            dkv.append(add_low(packet, other[:, np.arange(n_row) ^ offsets[i]]))
        dkv = jnp.stack(dkv, axis=2)
        bit = shared_heads // 2
        while bit:
            half = dkv.shape[3] // 2
            upper = (col_index & bit) != 0
            lower_part, upper_part = dkv[..., :half], dkv[..., half:]
            kept = jnp.where(upper, upper_part, lower_part)
            sent = jnp.where(upper, lower_part, upper_part)
            dkv = add_low(kept, swap(sent, "col", bit))
            bit //= 2
        sums, offsets = [dkv.transpose(1, 0, 2, 3).reshape(n_row * tokens, -1)], None

    held, order = layer_input, [0]
    bit = chips // 2
    while bit > 1:
        held = join_rows([held, swap(held, "col", 2 * bit)], first)
        order += [q | bit for q in order]
        bit //= 2
    x_parts = [held, swap(held, "col", 2)]
    order += [q | 1 for q in order]

    place = jnp.stack([core_index, row_index ^ chip_index])
    weights = turn_weights((w_query, w_key, w_value), [sums[0]])
    weights = pltpu.with_memory_space_constraint(weights, pltpu.VMEM)
    width = first.shape[1]
    early = [b for b in range(n_row) if b not in late]
    late = sorted(late)
    early_part = early_product(pieces, early, width, weights)
    half = tokens // 2
    groups, after = [], x_parts
    for part in range(2):
        mine, other = last_product(
            place, early, late, early_part, pieces, sums, offsets, weights, width, part, after
        )
        after = mine[:1]
        other = swap(other, "col", 1)
        group = {
            q: add_low(mine[q], other[q * half : (q + 1) * half]) for q in range(chips)
        }
        groups.append(group)
    x_parts += [swap(part, "col", 1) for part in x_parts]
    cols = weights.shape[0]
    g = order_rows(place, pieces, sums, offsets, width, cols, groups[1][chips - 1])
    terms = [[group.pop(0)] for group in groups]
    whole = []
    bit = 1
    while bit < chips:
        for q in sorted((q for q in groups[0] if q & bit), reverse=True):
            sent = [group.pop(q) for group in groups]
            if q == bit and 2 * bit < chips:
                sent = jnp.concatenate(sent, axis=1)
                sent = lax.optimization_barrier((sent, received))[0]
                whole.append(swap(sent, "col", 2 * bit))
                continue
            for group, term, half_sent in zip(groups, terms, sent):
                received = swap(half_sent, "col", 2 * bit)
                if q == bit:
                    term.append(received)
                else:
                    group[q ^ bit] = add_low(group[q ^ bit], received)
        bit *= 2

    grad_wq, grad_wk, grad_wv = weight_grads(g, x_parts, order, w_query.shape[1])
    grad_input = sum_rows(terms, whole, grad_wk)
    return grad_input, grad_wq, grad_wk, grad_wv


def solution(mesh):
    return jax.shard_map(
        shards,
        mesh=mesh,
        in_specs=(
            P("col", "row"),
            P("row", "col"),
            P("row", "col"),
            P("row", "col"),
            P("row", "col"),
            P("row", "col"),
            P("row", "col"),
            P("row", "col"),
            P("row"),
            P("row"),
        ),
        out_specs=(P("col", "row"), P("row", "col"), P("row", "col"), P("row", "col")),
        check_vma=False,
    )
```

time: 197 us -> 67.4 us (0.34)
  waiting for transfers between devices: 87 us -> 13.2 us
  local copies, waits for them, and re-layouts: 36.9 us -> 0.01 us
  Pallas kernels: 0 us -> 28.5 us
  matrix products: 28 us -> 0 us
  starting transfers between devices: 0.34 us -> 24.1 us
  blocking collectives: 18.7 us -> 0 us
  between operations: 13.9 us -> 0.78 us
  other arithmetic: 11.6 us -> 0.57 us
    all_gather x2 -> x0, waiting for transfers between devices: 58.4 us -> none  [the longest x1 30.7 us: shards(): grads_full = lax.all_gather(local_grads, 'row', axis=0, tiled=True)]
    pallas_call x0 -> x13, Pallas kernels: none -> 28.5 us  [the longest x1 8.14 us: weight_grads(): pl.pallas_call(functools.partial(weight_grad_kernel, places), grid=(featu...]
    dot_general x7 -> x0, matrix products: 28 us -> none  [contract(): lax.dot_general(left, right, (((left_dim,), (right_dim,)), ((), ())), pre...]
    reduce_scatter x2 -> x0, waiting for transfers between devices: 27.9 us -> none  [the longest x1 16.3 us: shards(): lax.psum_scatter(jnp.stack([dkey_part, dvalue_part], axis=1).astype(jnp.b...]
    ppermute x0 -> x20, starting transfers between devices: none -> 24.1 us  [swap(): return lax.ppermute(value, axis, pairs)]
    all_gather x2 -> x0, blocking collectives: 18.7 us -> none  [the longest x1 9.51 us: shards(): lax.all_gather(jnp.stack([positions, segment_ids]), 'row', axis=1, tiled=...]
    unnamed x24 -> x2, local copies, waits for them, and re-layouts: 16.6 us -> 0.01 us
    ppermute x0 -> x20, waiting for transfers between devices: none -> 13.2 us  [swap(): return lax.ppermute(value, axis, pairs)]
  transfers between devices with their start and end apart: 4 -> 20, of which waited for: 4 -> 10; matrix products, arithmetic and copies ran while one was open for 20% -> 1% of each run, Pallas kernels for 0% -> 38%
where the time goes in v1:
time: 67.4 us; the launch traced here: 67.2 us
  Pallas kernels  28.5 us (42%)
  starting transfers between devices  24.1 us (36%)
  waiting for transfers between devices  13.2 us (20%)
  between operations  0.78 us (1%)
    ppermute x20, starting transfers between devices, swap(): return lax.ppermute(value, axis, pairs)  24.1 us
    ppermute x20, waiting for transfers between devices, swap(): return lax.ppermute(value, axis, pairs)  13.2 us
    pallas_call x1, Pallas kernels, weight_grads(): pl.pallas_call(functools.partial(weight_grad_kernel, places), grid=(featu...  8.14 us
    pallas_call x1, Pallas kernels, attention_backward(): pl.pallas_call(functools.partial(attention_kernel, heads, blocks), out_sh...  4.05 us
    pallas_call x2, Pallas kernels, last_product(): pl.pallas_call(functools.partial(last_kernel, early, late, columns, offse...  3.96 us
    pallas_call x1, Pallas kernels, turn_weights(): pl.pallas_call(functools.partial(turn_kernel, tile), out_shape=pltpu.VMEM...  3.44 us
    pallas_call x1, Pallas kernels, early_product(): pl.pallas_call(functools.partial(early_kernel, columns, tile), out_shape=...  3.31 us
    pallas_call x1, Pallas kernels, prepare(): pl.pallas_call(functools.partial(prepare_kernel, heads, blocks), out_shap...  2.25 us
  transfers between devices with their start and end apart: 20, of which 10 were waited for; matrix products, arithmetic and copies ran while one was open for 1% of the time, Pallas kernels for 38%

profile of v1, /device:TPU:0, one launch (start us, length us, event | category | flops | bytes accessed | tf_op | source)
XLA Modules:
  0.0 67.2 jit_solution(8882645642041656672)
XLA Ops:
  0.6 4.1 %collective-permute-start.7 = (bf16[80,2048]{1,0:T(8,128)(2,1)}, bf16[80,2048]{1,0:T(8,128)(2,1)S(1)}, u32[]{:S(2)}, u32[]{:S(2)}) collective-permute-start(bf16[80,2048]{1,0:T(8,128)(2,1)} %refs_0_.1), channel_id=1, source_target_pairs={{0,4},{1,5},{2,6},{3,7},{4,0},{5,1},{6,2},{7,3},{8,12},{9,13},{10,... | collective-permute-start | bytes 983048 | tf_op jit(solution)/shard_map/ppermute | solution.py:27
  4.7 0.8 %pack.1.refs_0_ = bf16[176,256]{1,0:T(8,128)(2,1)S(1)} custom-call(bf16[160,128]{1,0:T(8,128)(2,1)} %k_ref.1, bf16[160,128]{1,0:T(8,128)(2,1)} %v_ref.1, s32[1,160]{1,0:T(1,128)} %bitcast.5), custom_call_target="tpu_custom_call" | custom-call | bytes 163840 | tf_op jit(solution)/shard_map/pack/pallas_call | solution.py:71
  5.6 2.5 %collective-permute-start.2 = (bf16[176,256]{1,0:T(8,128)(2,1)S(1)}, bf16[176,256]{1,0:T(8,128)(2,1)S(1)}, u32[]{:S(2)}, u32[]{:S(2)}) collective-permute-start(bf16[176,256]{1,0:T(8,128)(2,1)S(1)} %pack.1.refs_0_), channel_id=1, source_target_pairs={{0,24},{8,16},{16,8},{24,0},{1,25},{9,17},{17,9},{25,1},{2,26},{10... | collective-permute-start | bytes 270344 | tf_op jit(solution)/shard_map/ppermute | solution.py:27
  8.1 0.5 collective-permute-start.1
  8.6 0.5 collective-permute-start
  9.1 2.2 %prepare.1 = (bf16[1280,128]{1,0:T(8,128)(2,1)S(1)}, bf16[1280,128]{1,0:T(8,128)(2,1)S(1)}, f32[640,128]{1,0:T(8,128)S(1)}, f32[640,128]{1,0:T(8,128)S(1)}) custom-call(s32[1]{0:T(128)} %bitcast.2.row_ref, bf16[160,1024]{1,0:T(8,128)(2,1)} %q_hbm.1, bf16[160,1024]{1,0:T(8,128)(2,1)} %o_hbm.1, s32[1,160]{1,0:T(1,128)} %bitcast.7, s32[1,160]{1,0:T(1,128)} %bitcast.6, ...), custom_call_target="tpu_custom_call" | custom-call | bytes 1310720 | tf_op jit(solution)/shard_map/prepare/pallas_call | solution.py:130
  11.4 1.5 %collective-permute-done.1.refs_2_ = bf16[176,256]{1,0:T(8,128)(2,1)S(1)} collective-permute-done((bf16[176,256]{1,0:T(8,128)(2,1)S(1)}, bf16[176,256]{1,0:T(8,128)(2,1)S(1)}, u32[]{:S(2)}, u32[]{:S(2)}) %collective-permute-start.1) | collective-permute-done | bytes 90144 | tf_op jit(solution)/shard_map/ppermute | solution.py:27
  12.8 0.3 collective-permute-done.refs_1_
  13.1 4.0 %attention_backward.1 = (bf16[160,512]{1,0:T(8,128)(2,1)S(1)}, bf16[160,512]{1,0:T(8,128)(2,1)}, bf16[160,1024]{1,0:T(8,128)(2,1)S(1)}, bf16[160,1024]{1,0:T(8,128)(2,1)S(1)}) custom-call(s32[1]{0:T(128)} %bitcast.2.row_ref, bf16[1280,128]{1,0:T(8,128)(2,1)S(1)} %get-tuple-element.26.q_all, bf16[1280,128]{1,0:T(8,128)(2,1)S(1)} %get-tuple-element.27.o_all, ...), custom_call_target="tpu_custom_call" | custom-call | flops 1048576000 | bytes 2621440 | tf_op jit(solution)/shard_map/attention_backward/pallas_call | solution.py:224
  17.2 1.0 %collective-permute-start.3 = (bf16[160,1024]{1,0:T(8,128)(2,1)S(1)}, bf16[160,1024]{1,0:T(8,128)(2,1)S(1)}, u32[]{:S(2)}, u32[]{:S(2)}) collective-permute-start(bf16[160,1024]{1,0:T(8,128)(2,1)S(1)} %get-tuple-element.31.refs_0_), channel_id=1, source_target_pairs={{0,8},{8,0},{16,24},{24,16},{1,9},{9,1},{17,25},{25,17},{2,10},{10... | collective-permute-start | bytes 983048 | tf_op jit(solution)/shard_map/ppermute | solution.py:27
  18.1 1.1 %collective-permute-start.6 = (bf16[160,1024]{1,0:T(8,128)(2,1)S(1)}, bf16[160,1024]{1,0:T(8,128)(2,1)S(1)}, u32[]{:S(2)}, u32[]{:S(2)}) collective-permute-start(bf16[160,1024]{1,0:T(8,128)(2,1)S(1)} %get-tuple-element.33.refs_0_), channel_id=1, source_target_pairs={{0,16},{8,24},{16,0},{24,8},{1,17},{9,25},{17,1},{25,9},{2,18},{10... | collective-permute-start | bytes 983048 | tf_op jit(solution)/shard_map/ppermute | solution.py:27
  19.2 0.5 collective-permute-done.7.refs_1_
  19.7 0.2 join_rows.1.refs_2_.refs_0_.refs_1_
  19.9 1.2 %collective-permute-start.8 = (bf16[160,2048]{1,0:T(8,128)(2,1)S(1)}, bf16[160,2048]{1,0:T(8,128)(2,1)S(1)}, u32[]{:S(2)}, u32[]{:S(2)}) collective-permute-start(bf16[160,2048]{1,0:T(8,128)(2,1)S(1)} %join_rows.1.refs_2_.refs_0_.refs_1_), channel_id=1, source_target_pairs={{0,2},{1,3},{2,0},{3,1},{4,6},{5,7},{6,4},{7,5},{8,10},{9,11},{10,... | collective-permute-start | bytes 1966088 | tf_op jit(solution)/shard_map/ppermute | solution.py:27
  21.1 1.5 %collective-permute-start.5 = (bf16[160,512]{1,0:T(8,128)(2,1)}, bf16[160,512]{1,0:T(8,128)(2,1)}, u32[]{:S(2)}, u32[]{:S(2)}) collective-permute-start(bf16[160,512]{1,0:T(8,128)(2,1)} %get-tuple-element.32.refs_3_.refs_4_), channel_id=1, source_target_pairs={{0,8},{8,0},{16,24},{24,16},{1,9},{9,1},{17,25},{25,17},{2,10},{10... | collective-permute-start | bytes 491528 | tf_op jit(solution)/shard_map/ppermute | solution.py:27
  22.6 1.2 %collective-permute-start.4 = (bf16[160,512]{1,0:T(8,128)(2,1)S(1)}, bf16[160,512]{1,0:T(8,128)(2,1)}, u32[]{:S(2)}, u32[]{:S(2)}) collective-permute-start(bf16[160,512]{1,0:T(8,128)(2,1)S(1)} %get-tuple-element.30.refs_0_.refs_2_), channel_id=1, source_target_pairs={{0,16},{8,24},{16,0},{24,8},{1,17},{9,25},{17,1},{25,9},{2,18},{10... | collective-permute-start | bytes 491528 | tf_op jit(solution)/shard_map/ppermute | solution.py:27
  23.8 4.0 %collective-permute-done.3.refs_1_.refs_2_ = bf16[160,1024]{1,0:T(8,128)(2,1)S(1)} collective-permute-done((bf16[160,1024]{1,0:T(8,128)(2,1)S(1)}, bf16[160,1024]{1,0:T(8,128)(2,1)S(1)}, u32[]{:S(2)}, u32[]{:S(2)}) %collective-permute-start.3) | collective-permute-done | bytes 327712 | tf_op jit(solution)/shard_map/ppermute | solution.py:27
  27.8 0.1 combine.2.refs_0_.refs_6_.refs_5_.refs_8_
  27.9 0.9 %collective-permute-start.9 = (bf16[160,1024]{1,0:T(8,128)(2,1)S(1)}, bf16[160,1024]{1,0:T(8,128)(2,1)S(1)}, u32[]{:S(2)}, u32[]{:S(2)}) collective-permute-start(bf16[160,1024]{1,0:T(8,128)(2,1)S(1)} %combine.2.refs_0_.refs_6_.refs_5_.refs_8_), channel_id=1, source_target_pairs={{0,16},{8,24},{16,0},{24,8},{1,17},{9,25},{17,1},{25,9},{2,18},{10... | collective-permute-start | bytes 983048 | tf_op jit(solution)/shard_map/ppermute | solution.py:27
  28.7 0.1 collective-permute-done.6.refs_5_.refs_1_.refs_2_.refs_6_
  28.8 0.1 combine.3.refs_8_.refs_7_.refs_10_
  28.9 1.1 %collective-permute-start.10 = (bf16[160,1024]{1,0:T(8,128)(2,1)S(1)}, bf16[160,1024]{1,0:T(8,128)(2,1)S(1)}, u32[]{:S(2)}, u32[]{:S(2)}) collective-permute-start(bf16[160,1024]{1,0:T(8,128)(2,1)S(1)} %combine.3.refs_8_.refs_7_.refs_10_), channel_id=1, source_target_pairs={{0,8},{8,0},{16,24},{24,16},{1,9},{9,1},{17,25},{25,17},{2,10},{10... | collective-permute-start | bytes 983048 | tf_op jit(solution)/shard_map/ppermute | solution.py:27
  30.0 0.1 pad_add_fusion.place_ref
  30.0 3.4 %turn_weights.1.refs_6_.refs_1_ = bf16[1280,2048]{1,0:T(8,128)(2,1)S(1)} custom-call(bf16[2048,1024]{1,0:T(8,128)(2,1)} %wq_hbm.1, bf16[2048,128]{1,0:T(8,128)(2,1)} %wk_hbm.1, bf16[2048,128]{1,0:T(8,128)(2,1)} %wv_hbm.1, bf16[160,1024]{1,0:T(8,128)(2,1)S(1)} %combine.2.refs_0_.refs_6_.refs_5_.refs_8_), custom_call_target="tpu_custom_call" | custom-call | bytes 10485760 | tf_op jit(solution)/shard_map/turn_weights/pallas_call | solution.py:335
  33.5 3.3 %early_product.1.refs_0_ = bf16[480,2048]{1,0:T(8,128)(2,1)S(1)} custom-call(bf16[160,512]{1,0:T(8,128)(2,1)S(1)} %get-tuple-element.30.refs_0_.refs_2_, bf16[160,1024]{1,0:T(8,128)(2,1)S(1)} %collective-permute-done.3.refs_1_.refs_2_, bf16[160,512]{1,0:T(8,128)(2,1)} %collective-permute-done.4.refs_2_, bf16[160,512]{1,0:T(8,128)(2,1)} %get-tuple-element.32.refs_3_.refs_4_, ...), custom_call_target="tpu_custom_call" | custom-call | flops 2013265920 | bytes 7143424 | tf_op jit(solution)/shard_map/early_product/pallas_call | solution.py:374
  36.8 0.3 collective-permute-done.9.refs_4_.refs_7_.refs_3_.refs_6_.refs_9_
  37.1 1.9 %last_product.2 = (bf16[80,1024]{1,0:T(8,128)(2,1)S(1)}, bf16[80,1024]{1,0:T(8,128)(2,1)S(1)}, bf16[80,1024]{1,0:T(8,128)(2,1)S(1)}, bf16[80,1024]{1,0:T(8,128)(2,1)S(1)}, bf16[320,1024]{1,0:T(8,128)(2,1)S(1)}) custom-call(s32[2]{0:T(128)S(1)} %pad_add_fusion.place_ref, bf16[480,2048]{1,0:T(8,128)(2,1)S(1)} %early_product.1.refs_0_, ...), custom_call_target="tpu_custom_call" | custom-call | flops 671088640 | bytes 7864320 | tf_op jit(solution)/shard_map/last_product/pallas_call | solution.py:466
  39.0 0.1 collective-permute-start.11
  39.1 2.1 %last_product.3 = (bf16[80,1024]{1,0:T(8,128)(2,1)S(1)}, bf16[80,1024]{1,0:T(8,128)(2,1)S(1)}, bf16[80,1024]{1,0:T(8,128)(2,1)S(1)}, bf16[80,1024]{1,0:T(8,128)(2,1)S(1)}, bf16[320,1024]{1,0:T(8,128)(2,1)S(1)}) custom-call(s32[2]{0:T(128)S(1)} %pad_add_fusion.place_ref, bf16[480,2048]{1,0:T(8,128)(2,1)S(1)} %early_product.1.refs_0_, ...), custom_call_target="tpu_custom_call" | custom-call | flops 671088640 | bytes 7864320 | tf_op jit(solution)/shard_map/last_product/pallas_call | solution.py:466
  41.2 0.6 collective-permute-start.14
  41.7 0.1 collective-permute-start.18
  41.8 0.4 collective-permute-start.19
  42.2 0.2 add_convert_fusion.1
  42.4 1.7 %collective-permute-start.12 = (bf16[80,1024]{1,0:T(8,128)(2,1)S(1)}, bf16[80,1024]{1,0:T(8,128)(2,1)S(1)}, u32[]{:S(2)}, u32[]{:S(2)}) collective-permute-start(bf16[80,1024]{1,0:T(8,128)(2,1)S(1)} %get-tuple-element.49), channel_id=1, source_target_pairs={{0,2},{1,3},{2,0},{3,1},{4,6},{5,7},{6,4},{7,5},{8,10},{9,11},{10,... | collective-permute-start | bytes 491528 | tf_op jit(solution)/shard_map/ppermute | solution.py:27
  44.1 0.2 add_convert_fusion
  44.3 1.0 %collective-permute-start.15 = (bf16[80,1024]{1,0:T(8,128)(2,1)S(1)}, bf16[80,1024]{1,0:T(8,128)(2,1)S(1)}, u32[]{:S(2)}, u32[]{:S(2)}) collective-permute-start(bf16[80,1024]{1,0:T(8,128)(2,1)S(1)} %get-tuple-element.52.refs_12_), channel_id=1, source_target_pairs={{0,2},{1,3},{2,0},{3,1},{4,6},{5,7},{6,4},{7,5},{8,10},{9,11},{10,... | collective-permute-start | bytes 491528 | tf_op jit(solution)/shard_map/ppermute | solution.py:27
  45.3 1.3 %order_rows.1.g_ref = bf16[640,1280]{1,0:T(8,128)(2,1)S(1)} custom-call(s32[2]{0:T(128)S(1)} %pad_add_fusion.place_ref, bf16[160,512]{1,0:T(8,128)(2,1)S(1)} %get-tuple-element.30.refs_0_.refs_2_, bf16[160,1024]{1,0:T(8,128)(2,1)S(1)} %collective-permute-done.3.refs_1_.refs_2_, bf16[160,512]{1,0:T(8,128)(2,1)} %collective-permute-done.4.refs_2_, ...), custom_call_target="tpu_custom_call" | custom-call | bytes 3276800 | tf_op jit(solution)/shard_map/order_rows/pallas_call | solution.py:515
  46.7 2.9 %collective-permute-done.12 = bf16[80,1024]{1,0:T(8,128)(2,1)S(1)} collective-permute-done((bf16[80,1024]{1,0:T(8,128)(2,1)S(1)}, bf16[80,1024]{1,0:T(8,128)(2,1)S(1)}, u32[]{:S(2)}, u32[]{:S(2)}) %collective-permute-start.12) | collective-permute-done | bytes 163872 | tf_op jit(solution)/shard_map/ppermute | solution.py:27
  49.5 0.1 add_convert_fusion.6
  49.6 1.9 %collective-permute-start.13 = (bf16[80,1024]{1,0:T(8,128)(2,1)S(1)}, bf16[80,1024]{1,0:T(8,128)(2,1)S(1)}, u32[]{:S(2)}, u32[]{:S(2)}) collective-permute-start(bf16[80,1024]{1,0:T(8,128)(2,1)S(1)} %add_convert_fusion.6), channel_id=1, source_target_pairs={{0,4},{1,5},{2,6},{3,7},{4,0},{5,1},{6,2},{7,3},{8,12},{9,13},{10,... | collective-permute-start | bytes 491528 | tf_op jit(solution)/shard_map/ppermute | solution.py:27
  51.6 2.3 %collective-permute-done.15 = bf16[80,1024]{1,0:T(8,128)(2,1)S(1)} collective-permute-done((bf16[80,1024]{1,0:T(8,128)(2,1)S(1)}, bf16[80,1024]{1,0:T(8,128)(2,1)S(1)}, u32[]{:S(2)}, u32[]{:S(2)}) %collective-permute-start.15) | collective-permute-done | bytes 163872 | tf_op jit(solution)/shard_map/ppermute | solution.py:27
  53.9 0.8 %collective-permute-start.17 = (bf16[80,2048]{1,0:T(8,128)(2,1)S(1)}, bf16[80,2048]{1,0:T(8,128)(2,1)S(1)}, u32[]{:S(2)}, u32[]{:S(2)}) collective-permute-start(bf16[80,2048]{1,0:T(8,128)(2,1)S(1)} %pad_maximum_fusion), channel_id=1, source_target_pairs={{0,2},{1,3},{2,0},{3,1},{4,6},{5,7},{6,4},{7,5},{8,10},{9,11},{10,... | collective-permute-start | bytes 983048 | tf_op jit(solution)/shard_map/ppermute | solution.py:27
  54.7 0.1 add_convert_fusion.2
  54.7 2.0 %collective-permute-start.16 = (bf16[80,1024]{1,0:T(8,128)(2,1)S(1)}, bf16[80,1024]{1,0:T(8,128)(2,1)S(1)}, u32[]{:S(2)}, u32[]{:S(2)}) collective-permute-start(bf16[80,1024]{1,0:T(8,128)(2,1)S(1)} %add_convert_fusion.2), channel_id=1, source_target_pairs={{0,4},{1,5},{2,6},{3,7},{4,0},{5,1},{6,2},{7,3},{8,12},{9,13},{10,... | collective-permute-start | bytes 491528 | tf_op jit(solution)/shard_map/ppermute | solution.py:27
  56.7 8.1 %weight_grads.1 = (f32[2048,1024]{1,0:T(8,128)}, f32[2048,128]{1,0:T(8,128)}, f32[2048,128]{1,0:T(8,128)}) custom-call(bf16[640,1280]{1,0:T(8,128)(2,1)S(1)} %order_rows.1.g_ref, bf16[160,2048]{1,0:T(8,128)(2,1)S(1)} %join_rows.1.refs_2_.refs_0_.refs_1_, bf16[160,2048]{1,0:T(8,128)(2,1)S(1)} %join_rows.1.refs_2_.refs_0_.refs_1_, ...), custom_call_target="tpu_custom_call" | custom-call | flops 3355443200 | bytes 14745600 | tf_op jit(solution)/shard_map/weight_grads/pallas_call | solution.py:583
  64.8 0.5 collective-permute-done.16.refs_3_
  65.4 0.9 %collective-permute-done.17.refs_4_ = bf16[80,2048]{1,0:T(8,128)(2,1)S(1)} collective-permute-done((bf16[80,2048]{1,0:T(8,128)(2,1)S(1)}, bf16[80,2048]{1,0:T(8,128)(2,1)S(1)}, u32[]{:S(2)}, u32[]{:S(2)}) %collective-permute-start.17) | collective-permute-done | bytes 327712 | tf_op jit(solution)/shard_map/ppermute | solution.py:27
  66.3 0.8 %sum_rows.1 = bf16[80,2048]{1,0:T(8,128)(2,1)} custom-call(bf16[80,1024]{1,0:T(8,128)(2,1)S(1)} %get-tuple-element.50.refs_0_, bf16[80,1024]{1,0:T(8,128)(2,1)S(1)} %collective-permute-done.13.refs_1_, bf16[80,1024]{1,0:T(8,128)(2,1)S(1)} %get-tuple-element.53.refs_2_, bf16[80,1024]{1,0:T(8,128)(2,1)S(1)} %collective-permute-done.16.refs_3_, ...), custom_call_target="tpu_custom_call" | custom-call | flops 409600 | bytes 1638400 | tf_op jit(solution)/shard_map/sum_rows/pallas_call | solution.py:631
  (13 shorter events, 0.1 us)
Async XLA Ops:
  0.6 19.1 %copy-start = (bf16[80,2048]{1,0:T(8,128)(2,1)S(1)}, bf16[80,2048]{1,0:T(8,128)(2,1)}, u32[]{:S(2)}) copy-start(bf16[80,2048]{1,0:T(8,128)(2,1)} %refs_0_.1) | copy-start | bytes 983044
  0.6 19.0 %collective-permute-start.7 = (bf16[80,2048]{1,0:T(8,128)(2,1)}, bf16[80,2048]{1,0:T(8,128)(2,1)S(1)}, u32[]{:S(2)}, u32[]{:S(2)}) collective-permute-start(bf16[80,2048]{1,0:T(8,128)(2,1)} %refs_0_.1), channel_id=1, source_target_pairs={{0,4},{1,5},{2,6},{3,7},{4,0},{5,1},{6,2},{7,3},{8,12},{9,13},{10,... | collective-permute-start | bytes 983048 | tf_op jit(solution)/shard_map/ppermute | solution.py:27
  5.6 5.8 %collective-permute-start.2 = (bf16[176,256]{1,0:T(8,128)(2,1)S(1)}, bf16[176,256]{1,0:T(8,128)(2,1)S(1)}, u32[]{:S(2)}, u32[]{:S(2)}) collective-permute-start(bf16[176,256]{1,0:T(8,128)(2,1)S(1)} %pack.1.refs_0_), channel_id=1, source_target_pairs={{0,24},{8,16},{16,8},{24,0},{1,25},{9,17},{17,9},{25,1},{2,26},{10... | collective-permute-start | bytes 270344 | tf_op jit(solution)/shard_map/ppermute | solution.py:27
  8.1 4.8 %collective-permute-start.1 = (bf16[176,256]{1,0:T(8,128)(2,1)S(1)}, bf16[176,256]{1,0:T(8,128)(2,1)S(1)}, u32[]{:S(2)}, u32[]{:S(2)}) collective-permute-start(bf16[176,256]{1,0:T(8,128)(2,1)S(1)} %pack.1.refs_0_), channel_id=1, source_target_pairs={{0,16},{8,24},{16,0},{24,8},{1,17},{9,25},{17,1},{25,9},{2,18},{10... | collective-permute-start | bytes 270344 | tf_op jit(solution)/shard_map/ppermute | solution.py:27
  8.6 4.5 %collective-permute-start = (bf16[176,256]{1,0:T(8,128)(2,1)S(1)}, bf16[176,256]{1,0:T(8,128)(2,1)S(1)}, u32[]{:S(2)}, u32[]{:S(2)}) collective-permute-start(bf16[176,256]{1,0:T(8,128)(2,1)S(1)} %pack.1.refs_0_), channel_id=1, source_target_pairs={{0,8},{8,0},{16,24},{24,16},{1,9},{9,1},{17,25},{25,17},{2,10},{10... | collective-permute-start | bytes 270344 | tf_op jit(solution)/shard_map/ppermute | solution.py:27
  17.2 10.6 %collective-permute-start.3 = (bf16[160,1024]{1,0:T(8,128)(2,1)S(1)}, bf16[160,1024]{1,0:T(8,128)(2,1)S(1)}, u32[]{:S(2)}, u32[]{:S(2)}) collective-permute-start(bf16[160,1024]{1,0:T(8,128)(2,1)S(1)} %get-tuple-element.31.refs_0_), channel_id=1, source_target_pairs={{0,8},{8,0},{16,24},{24,16},{1,9},{9,1},{17,25},{25,17},{2,10},{10... | collective-permute-start | bytes 983048 | tf_op jit(solution)/shard_map/ppermute | solution.py:27
  18.1 10.7 %collective-permute-start.6 = (bf16[160,1024]{1,0:T(8,128)(2,1)S(1)}, bf16[160,1024]{1,0:T(8,128)(2,1)S(1)}, u32[]{:S(2)}, u32[]{:S(2)}) collective-permute-start(bf16[160,1024]{1,0:T(8,128)(2,1)S(1)} %get-tuple-element.33.refs_0_), channel_id=1, source_target_pairs={{0,16},{8,24},{16,0},{24,8},{1,17},{9,25},{17,1},{25,9},{2,18},{10... | collective-permute-start | bytes 983048 | tf_op jit(solution)/shard_map/ppermute | solution.py:27
  19.9 17.2 %collective-permute-start.8 = (bf16[160,2048]{1,0:T(8,128)(2,1)S(1)}, bf16[160,2048]{1,0:T(8,128)(2,1)S(1)}, u32[]{:S(2)}, u32[]{:S(2)}) collective-permute-start(bf16[160,2048]{1,0:T(8,128)(2,1)S(1)} %join_rows.1.refs_2_.refs_0_.refs_1_), channel_id=1, source_target_pairs={{0,2},{1,3},{2,0},{3,1},{4,6},{5,7},{6,4},{7,5},{8,10},{9,11},{10,... | collective-permute-start | bytes 1966088 | tf_op jit(solution)/shard_map/ppermute | solution.py:27
  21.1 12.4 %collective-permute-start.5 = (bf16[160,512]{1,0:T(8,128)(2,1)}, bf16[160,512]{1,0:T(8,128)(2,1)}, u32[]{:S(2)}, u32[]{:S(2)}) collective-permute-start(bf16[160,512]{1,0:T(8,128)(2,1)} %get-tuple-element.32.refs_3_.refs_4_), channel_id=1, source_target_pairs={{0,8},{8,0},{16,24},{24,16},{1,9},{9,1},{17,25},{25,17},{2,10},{10... | collective-permute-start | bytes 491528 | tf_op jit(solution)/shard_map/ppermute | solution.py:27
  22.6 10.9 %collective-permute-start.4 = (bf16[160,512]{1,0:T(8,128)(2,1)S(1)}, bf16[160,512]{1,0:T(8,128)(2,1)}, u32[]{:S(2)}, u32[]{:S(2)}) collective-permute-start(bf16[160,512]{1,0:T(8,128)(2,1)S(1)} %get-tuple-element.30.refs_0_.refs_2_), channel_id=1, source_target_pairs={{0,16},{8,24},{16,0},{24,8},{1,17},{9,25},{17,1},{25,9},{2,18},{10... | collective-permute-start | bytes 491528 | tf_op jit(solution)/shard_map/ppermute | solution.py:27
  27.9 9.2 %collective-permute-start.9 = (bf16[160,1024]{1,0:T(8,128)(2,1)S(1)}, bf16[160,1024]{1,0:T(8,128)(2,1)S(1)}, u32[]{:S(2)}, u32[]{:S(2)}) collective-permute-start(bf16[160,1024]{1,0:T(8,128)(2,1)S(1)} %combine.2.refs_0_.refs_6_.refs_5_.refs_8_), channel_id=1, source_target_pairs={{0,16},{8,24},{16,0},{24,8},{1,17},{9,25},{17,1},{25,9},{2,18},{10... | collective-permute-start | bytes 983048 | tf_op jit(solution)/shard_map/ppermute | solution.py:27
  28.9 8.3 %collective-permute-start.10 = (bf16[160,1024]{1,0:T(8,128)(2,1)S(1)}, bf16[160,1024]{1,0:T(8,128)(2,1)S(1)}, u32[]{:S(2)}, u32[]{:S(2)}) collective-permute-start(bf16[160,1024]{1,0:T(8,128)(2,1)S(1)} %combine.3.refs_8_.refs_7_.refs_10_), channel_id=1, source_target_pairs={{0,8},{8,0},{16,24},{24,16},{1,9},{9,1},{17,25},{25,17},{2,10},{10... | collective-permute-start | bytes 983048 | tf_op jit(solution)/shard_map/ppermute | solution.py:27
  39.0 3.2 %collective-permute-start.11 = (bf16[320,1024]{1,0:T(8,128)(2,1)S(1)}, bf16[320,1024]{1,0:T(8,128)(2,1)S(1)}, u32[]{:S(2)}, u32[]{:S(2)}) collective-permute-start(bf16[320,1024]{1,0:T(8,128)(2,1)S(1)} %get-tuple-element.35), channel_id=1, source_target_pairs={{0,1},{1,0},{2,3},{3,2},{4,5},{5,4},{6,7},{7,6},{8,9},{9,8},{10,11... | collective-permute-start | bytes 1966088 | tf_op jit(solution)/shard_map/ppermute | solution.py:27
  41.2 2.9 %collective-permute-start.14 = (bf16[320,1024]{1,0:T(8,128)(2,1)S(1)}, bf16[320,1024]{1,0:T(8,128)(2,1)S(1)}, u32[]{:S(2)}, u32[]{:S(2)}) collective-permute-start(bf16[320,1024]{1,0:T(8,128)(2,1)S(1)} %get-tuple-element.39), channel_id=1, source_target_pairs={{0,1},{1,0},{2,3},{3,2},{4,5},{5,4},{6,7},{7,6},{8,9},{9,8},{10,11... | collective-permute-start | bytes 1966088 | tf_op jit(solution)/shard_map/ppermute | solution.py:27
  41.7 15.0 %collective-permute-start.18 = (bf16[160,2048]{1,0:T(8,128)(2,1)S(1)}, bf16[160,2048]{1,0:T(8,128)(2,1)S(1)}, u32[]{:S(2)}, u32[]{:S(2)}) collective-permute-start(bf16[160,2048]{1,0:T(8,128)(2,1)S(1)} %join_rows.1.refs_2_.refs_0_.refs_1_), channel_id=1, source_target_pairs={{0,1},{1,0},{2,3},{3,2},{4,5},{5,4},{6,7},{7,6},{8,9},{9,8},{10,11... | collective-permute-start | bytes 1966088 | tf_op jit(solution)/shard_map/ppermute | solution.py:27
  41.8 14.9 %collective-permute-start.19 = (bf16[160,2048]{1,0:T(8,128)(2,1)S(1)}, bf16[160,2048]{1,0:T(8,128)(2,1)S(1)}, u32[]{:S(2)}, u32[]{:S(2)}) collective-permute-start(bf16[160,2048]{1,0:T(8,128)(2,1)S(1)} %collective-permute-done.8.refs_3_.refs_2_), channel_id=1, source_target_pairs={{0,1},{1,0},{2,3},{3,2},{4,5},{5,4},{6,7},{7,6},{8,9},{9,8},{10,11... | collective-permute-start | bytes 1966088 | tf_op jit(solution)/shard_map/ppermute | solution.py:27
  42.4 7.1 %collective-permute-start.12 = (bf16[80,1024]{1,0:T(8,128)(2,1)S(1)}, bf16[80,1024]{1,0:T(8,128)(2,1)S(1)}, u32[]{:S(2)}, u32[]{:S(2)}) collective-permute-start(bf16[80,1024]{1,0:T(8,128)(2,1)S(1)} %get-tuple-element.49), channel_id=1, source_target_pairs={{0,2},{1,3},{2,0},{3,1},{4,6},{5,7},{6,4},{7,5},{8,10},{9,11},{10,... | collective-permute-start | bytes 491528 | tf_op jit(solution)/shard_map/ppermute | solution.py:27
  44.3 9.6 %collective-permute-start.15 = (bf16[80,1024]{1,0:T(8,128)(2,1)S(1)}, bf16[80,1024]{1,0:T(8,128)(2,1)S(1)}, u32[]{:S(2)}, u32[]{:S(2)}) collective-permute-start(bf16[80,1024]{1,0:T(8,128)(2,1)S(1)} %get-tuple-element.52.refs_12_), channel_id=1, source_target_pairs={{0,2},{1,3},{2,0},{3,1},{4,6},{5,7},{6,4},{7,5},{8,10},{9,11},{10,... | collective-permute-start | bytes 491528 | tf_op jit(solution)/shard_map/ppermute | solution.py:27
  49.6 15.2 %collective-permute-start.13 = (bf16[80,1024]{1,0:T(8,128)(2,1)S(1)}, bf16[80,1024]{1,0:T(8,128)(2,1)S(1)}, u32[]{:S(2)}, u32[]{:S(2)}) collective-permute-start(bf16[80,1024]{1,0:T(8,128)(2,1)S(1)} %add_convert_fusion.6), channel_id=1, source_target_pairs={{0,4},{1,5},{2,6},{3,7},{4,0},{5,1},{6,2},{7,3},{8,12},{9,13},{10,... | collective-permute-start | bytes 491528 | tf_op jit(solution)/shard_map/ppermute | solution.py:27
  53.9 12.4 %collective-permute-start.17 = (bf16[80,2048]{1,0:T(8,128)(2,1)S(1)}, bf16[80,2048]{1,0:T(8,128)(2,1)S(1)}, u32[]{:S(2)}, u32[]{:S(2)}) collective-permute-start(bf16[80,2048]{1,0:T(8,128)(2,1)S(1)} %pad_maximum_fusion), channel_id=1, source_target_pairs={{0,2},{1,3},{2,0},{3,1},{4,6},{5,7},{6,4},{7,5},{8,10},{9,11},{10,... | collective-permute-start | bytes 983048 | tf_op jit(solution)/shard_map/ppermute | solution.py:27
  54.7 10.7 %collective-permute-start.16 = (bf16[80,1024]{1,0:T(8,128)(2,1)S(1)}, bf16[80,1024]{1,0:T(8,128)(2,1)S(1)}, u32[]{:S(2)}, u32[]{:S(2)}) collective-permute-start(bf16[80,1024]{1,0:T(8,128)(2,1)S(1)} %add_convert_fusion.2), channel_id=1, source_target_pairs={{0,4},{1,5},{2,6},{3,7},{4,0},{5,1},{6,2},{7,3},{8,12},{9,13},{10,... | collective-permute-start | bytes 491528 | tf_op jit(solution)/shard_map/ppermute | solution.py:27

commit v2 on v1

--- a/solution.py
+++ b/solution.py
@@ -749,12 +749,13 @@
                 sent = lax.optimization_barrier((sent, received))[0]
                 whole.append(swap(sent, "col", 2 * bit))
                 continue
-            for group, term, half_sent in zip(groups, terms, sent):
-                received = swap(half_sent, "col", 2 * bit)
+            arrived = [swap(half_sent, "col", 2 * bit) for half_sent in sent]
+            received = arrived[0]
+            for group, term, half in zip(groups, terms, arrived):
                 if q == bit:
-                    term.append(received)
+                    term.append(half)
                 else:
-                    group[q ^ bit] = add_low(group[q ^ bit], received)
+                    group[q ^ bit] = add_low(group[q ^ bit], half)
         bit *= 2
 
     grad_wq, grad_wk, grad_wv = weight_grads(g, x_parts, order, w_query.shape[1])

time: 67.4 us -> 67.3 us (level)
  no operation moved by 1% of the time
where the time goes in v2:
time: 67.3 us; the launch traced here: 67.1 us
  Pallas kernels  28.5 us (42%)
  starting transfers between devices  23.7 us (35%)
  waiting for transfers between devices  13.5 us (20%)
  between operations  0.78 us (1%)
    ppermute x20, starting transfers between devices, swap(): return lax.ppermute(value, axis, pairs)  23.7 us
    ppermute x20, waiting for transfers between devices, swap(): return lax.ppermute(value, axis, pairs)  13.5 us
    pallas_call x1, Pallas kernels, weight_grads(): pl.pallas_call(functools.partial(weight_grad_kernel, places), grid=(featu...  8.14 us
    pallas_call x1, Pallas kernels, attention_backward(): pl.pallas_call(functools.partial(attention_kernel, heads, blocks), out_sh...  4.05 us
    pallas_call x2, Pallas kernels, last_product(): pl.pallas_call(functools.partial(last_kernel, early, late, columns, offse...  3.96 us
    pallas_call x1, Pallas kernels, turn_weights(): pl.pallas_call(functools.partial(turn_kernel, tile), out_shape=pltpu.VMEM...  3.44 us
    pallas_call x1, Pallas kernels, early_product(): pl.pallas_call(functools.partial(early_kernel, columns, tile), out_shape=...  3.31 us
    pallas_call x1, Pallas kernels, prepare(): pl.pallas_call(functools.partial(prepare_kernel, heads, blocks), out_shap...  2.25 us
  transfers between devices with their start and end apart: 20, of which 10 were waited for; matrix products, arithmetic and copies ran while one was open for 1% of the time, Pallas kernels for 38%

profile of v2, /device:TPU:0, one launch (start us, length us, event | category | flops | bytes accessed | tf_op | source)
XLA Modules:
  0.0 67.1 jit_solution(8132288898712364336)
XLA Ops:
  0.6 4.1 %collective-permute-start.7 = (bf16[80,2048]{1,0:T(8,128)(2,1)}, bf16[80,2048]{1,0:T(8,128)(2,1)S(1)}, u32[]{:S(2)}, u32[]{:S(2)}) collective-permute-start(bf16[80,2048]{1,0:T(8,128)(2,1)} %refs_0_.1), channel_id=1, source_target_pairs={{0,4},{1,5},{2,6},{3,7},{4,0},{5,1},{6,2},{7,3},{8,12},{9,13},{10,... | collective-permute-start | bytes 983048 | tf_op jit(solution)/shard_map/ppermute | solution.py:27
  4.7 0.8 %pack.1.refs_0_ = bf16[176,256]{1,0:T(8,128)(2,1)S(1)} custom-call(bf16[160,128]{1,0:T(8,128)(2,1)} %k_ref.1, bf16[160,128]{1,0:T(8,128)(2,1)} %v_ref.1, s32[1,160]{1,0:T(1,128)} %bitcast.5), custom_call_target="tpu_custom_call" | custom-call | bytes 163840 | tf_op jit(solution)/shard_map/pack/pallas_call | solution.py:71
  5.6 2.5 %collective-permute-start.2 = (bf16[176,256]{1,0:T(8,128)(2,1)S(1)}, bf16[176,256]{1,0:T(8,128)(2,1)S(1)}, u32[]{:S(2)}, u32[]{:S(2)}) collective-permute-start(bf16[176,256]{1,0:T(8,128)(2,1)S(1)} %pack.1.refs_0_), channel_id=1, source_target_pairs={{0,24},{8,16},{16,8},{24,0},{1,25},{9,17},{17,9},{25,1},{2,26},{10... | collective-permute-start | bytes 270344 | tf_op jit(solution)/shard_map/ppermute | solution.py:27
  8.1 0.5 collective-permute-start.1
  8.6 0.5 collective-permute-start
  9.1 2.2 %prepare.1 = (bf16[1280,128]{1,0:T(8,128)(2,1)S(1)}, bf16[1280,128]{1,0:T(8,128)(2,1)S(1)}, f32[640,128]{1,0:T(8,128)S(1)}, f32[640,128]{1,0:T(8,128)S(1)}) custom-call(s32[1]{0:T(128)} %bitcast.2.row_ref, bf16[160,1024]{1,0:T(8,128)(2,1)} %q_hbm.1, bf16[160,1024]{1,0:T(8,128)(2,1)} %o_hbm.1, s32[1,160]{1,0:T(1,128)} %bitcast.7, s32[1,160]{1,0:T(1,128)} %bitcast.6, ...), custom_call_target="tpu_custom_call" | custom-call | bytes 1310720 | tf_op jit(solution)/shard_map/prepare/pallas_call | solution.py:130
  11.4 1.5 %collective-permute-done.1.refs_2_ = bf16[176,256]{1,0:T(8,128)(2,1)S(1)} collective-permute-done((bf16[176,256]{1,0:T(8,128)(2,1)S(1)}, bf16[176,256]{1,0:T(8,128)(2,1)S(1)}, u32[]{:S(2)}, u32[]{:S(2)}) %collective-permute-start.1) | collective-permute-done | bytes 90144 | tf_op jit(solution)/shard_map/ppermute | solution.py:27
  12.8 0.3 collective-permute-done.refs_1_
  13.1 4.0 %attention_backward.1 = (bf16[160,512]{1,0:T(8,128)(2,1)S(1)}, bf16[160,512]{1,0:T(8,128)(2,1)}, bf16[160,1024]{1,0:T(8,128)(2,1)S(1)}, bf16[160,1024]{1,0:T(8,128)(2,1)S(1)}) custom-call(s32[1]{0:T(128)} %bitcast.2.row_ref, bf16[1280,128]{1,0:T(8,128)(2,1)S(1)} %get-tuple-element.26.q_all, bf16[1280,128]{1,0:T(8,128)(2,1)S(1)} %get-tuple-element.27.o_all, ...), custom_call_target="tpu_custom_call" | custom-call | flops 1048576000 | bytes 2621440 | tf_op jit(solution)/shard_map/attention_backward/pallas_call | solution.py:224
  17.2 1.0 %collective-permute-start.3 = (bf16[160,1024]{1,0:T(8,128)(2,1)S(1)}, bf16[160,1024]{1,0:T(8,128)(2,1)S(1)}, u32[]{:S(2)}, u32[]{:S(2)}) collective-permute-start(bf16[160,1024]{1,0:T(8,128)(2,1)S(1)} %get-tuple-element.31.refs_0_), channel_id=1, source_target_pairs={{0,8},{8,0},{16,24},{24,16},{1,9},{9,1},{17,25},{25,17},{2,10},{10... | collective-permute-start | bytes 983048 | tf_op jit(solution)/shard_map/ppermute | solution.py:27
  18.1 1.1 %collective-permute-start.6 = (bf16[160,1024]{1,0:T(8,128)(2,1)S(1)}, bf16[160,1024]{1,0:T(8,128)(2,1)S(1)}, u32[]{:S(2)}, u32[]{:S(2)}) collective-permute-start(bf16[160,1024]{1,0:T(8,128)(2,1)S(1)} %get-tuple-element.33.refs_0_), channel_id=1, source_target_pairs={{0,16},{8,24},{16,0},{24,8},{1,17},{9,25},{17,1},{25,9},{2,18},{10... | collective-permute-start | bytes 983048 | tf_op jit(solution)/shard_map/ppermute | solution.py:27
  19.2 0.5 collective-permute-done.7.refs_1_
  19.7 0.2 join_rows.1.refs_2_.refs_0_.refs_1_
  19.9 1.2 %collective-permute-start.8 = (bf16[160,2048]{1,0:T(8,128)(2,1)S(1)}, bf16[160,2048]{1,0:T(8,128)(2,1)S(1)}, u32[]{:S(2)}, u32[]{:S(2)}) collective-permute-start(bf16[160,2048]{1,0:T(8,128)(2,1)S(1)} %join_rows.1.refs_2_.refs_0_.refs_1_), channel_id=1, source_target_pairs={{0,2},{1,3},{2,0},{3,1},{4,6},{5,7},{6,4},{7,5},{8,10},{9,11},{10,... | collective-permute-start | bytes 1966088 | tf_op jit(solution)/shard_map/ppermute | solution.py:27
  21.1 1.5 %collective-permute-start.5 = (bf16[160,512]{1,0:T(8,128)(2,1)}, bf16[160,512]{1,0:T(8,128)(2,1)}, u32[]{:S(2)}, u32[]{:S(2)}) collective-permute-start(bf16[160,512]{1,0:T(8,128)(2,1)} %get-tuple-element.32.refs_3_.refs_4_), channel_id=1, source_target_pairs={{0,8},{8,0},{16,24},{24,16},{1,9},{9,1},{17,25},{25,17},{2,10},{10... | collective-permute-start | bytes 491528 | tf_op jit(solution)/shard_map/ppermute | solution.py:27
  22.6 1.2 %collective-permute-start.4 = (bf16[160,512]{1,0:T(8,128)(2,1)S(1)}, bf16[160,512]{1,0:T(8,128)(2,1)}, u32[]{:S(2)}, u32[]{:S(2)}) collective-permute-start(bf16[160,512]{1,0:T(8,128)(2,1)S(1)} %get-tuple-element.30.refs_0_.refs_2_), channel_id=1, source_target_pairs={{0,16},{8,24},{16,0},{24,8},{1,17},{9,25},{17,1},{25,9},{2,18},{10... | collective-permute-start | bytes 491528 | tf_op jit(solution)/shard_map/ppermute | solution.py:27
  23.8 4.0 %collective-permute-done.3.refs_1_.refs_2_ = bf16[160,1024]{1,0:T(8,128)(2,1)S(1)} collective-permute-done((bf16[160,1024]{1,0:T(8,128)(2,1)S(1)}, bf16[160,1024]{1,0:T(8,128)(2,1)S(1)}, u32[]{:S(2)}, u32[]{:S(2)}) %collective-permute-start.3) | collective-permute-done | bytes 327712 | tf_op jit(solution)/shard_map/ppermute | solution.py:27
  27.8 0.1 combine.2.refs_0_.refs_6_.refs_5_.refs_8_
  27.9 0.9 %collective-permute-start.9 = (bf16[160,1024]{1,0:T(8,128)(2,1)S(1)}, bf16[160,1024]{1,0:T(8,128)(2,1)S(1)}, u32[]{:S(2)}, u32[]{:S(2)}) collective-permute-start(bf16[160,1024]{1,0:T(8,128)(2,1)S(1)} %combine.2.refs_0_.refs_6_.refs_5_.refs_8_), channel_id=1, source_target_pairs={{0,16},{8,24},{16,0},{24,8},{1,17},{9,25},{17,1},{25,9},{2,18},{10... | collective-permute-start | bytes 983048 | tf_op jit(solution)/shard_map/ppermute | solution.py:27
  28.7 0.1 collective-permute-done.6.refs_5_.refs_1_.refs_2_.refs_6_
  28.8 0.1 combine.3.refs_8_.refs_7_.refs_10_
  28.9 1.1 %collective-permute-start.10 = (bf16[160,1024]{1,0:T(8,128)(2,1)S(1)}, bf16[160,1024]{1,0:T(8,128)(2,1)S(1)}, u32[]{:S(2)}, u32[]{:S(2)}) collective-permute-start(bf16[160,1024]{1,0:T(8,128)(2,1)S(1)} %combine.3.refs_8_.refs_7_.refs_10_), channel_id=1, source_target_pairs={{0,8},{8,0},{16,24},{24,16},{1,9},{9,1},{17,25},{25,17},{2,10},{10... | collective-permute-start | bytes 983048 | tf_op jit(solution)/shard_map/ppermute | solution.py:27
  30.0 0.1 pad_add_fusion.place_ref
  30.0 3.4 %turn_weights.1.refs_6_.refs_1_ = bf16[1280,2048]{1,0:T(8,128)(2,1)S(1)} custom-call(bf16[2048,1024]{1,0:T(8,128)(2,1)} %wq_hbm.1, bf16[2048,128]{1,0:T(8,128)(2,1)} %wk_hbm.1, bf16[2048,128]{1,0:T(8,128)(2,1)} %wv_hbm.1, bf16[160,1024]{1,0:T(8,128)(2,1)S(1)} %combine.2.refs_0_.refs_6_.refs_5_.refs_8_), custom_call_target="tpu_custom_call" | custom-call | bytes 10485760 | tf_op jit(solution)/shard_map/turn_weights/pallas_call | solution.py:335
  33.5 3.3 %early_product.1.refs_0_ = bf16[480,2048]{1,0:T(8,128)(2,1)S(1)} custom-call(bf16[160,512]{1,0:T(8,128)(2,1)S(1)} %get-tuple-element.30.refs_0_.refs_2_, bf16[160,1024]{1,0:T(8,128)(2,1)S(1)} %collective-permute-done.3.refs_1_.refs_2_, bf16[160,512]{1,0:T(8,128)(2,1)} %collective-permute-done.4.refs_2_, bf16[160,512]{1,0:T(8,128)(2,1)} %get-tuple-element.32.refs_3_.refs_4_, ...), custom_call_target="tpu_custom_call" | custom-call | flops 2013265920 | bytes 7143424 | tf_op jit(solution)/shard_map/early_product/pallas_call | solution.py:374
  36.8 0.3 collective-permute-done.9.refs_4_.refs_7_.refs_3_.refs_6_.refs_9_
  37.1 1.9 %last_product.2 = (bf16[80,1024]{1,0:T(8,128)(2,1)S(1)}, bf16[80,1024]{1,0:T(8,128)(2,1)S(1)}, bf16[80,1024]{1,0:T(8,128)(2,1)S(1)}, bf16[80,1024]{1,0:T(8,128)(2,1)S(1)}, bf16[320,1024]{1,0:T(8,128)(2,1)S(1)}) custom-call(s32[2]{0:T(128)S(1)} %pad_add_fusion.place_ref, bf16[480,2048]{1,0:T(8,128)(2,1)S(1)} %early_product.1.refs_0_, ...), custom_call_target="tpu_custom_call" | custom-call | flops 671088640 | bytes 7864320 | tf_op jit(solution)/shard_map/last_product/pallas_call | solution.py:466
  39.0 0.1 collective-permute-start.11
  39.1 2.1 %last_product.3 = (bf16[80,1024]{1,0:T(8,128)(2,1)S(1)}, bf16[80,1024]{1,0:T(8,128)(2,1)S(1)}, bf16[80,1024]{1,0:T(8,128)(2,1)S(1)}, bf16[80,1024]{1,0:T(8,128)(2,1)S(1)}, bf16[320,1024]{1,0:T(8,128)(2,1)S(1)}) custom-call(s32[2]{0:T(128)S(1)} %pad_add_fusion.place_ref, bf16[480,2048]{1,0:T(8,128)(2,1)S(1)} %early_product.1.refs_0_, ...), custom_call_target="tpu_custom_call" | custom-call | flops 671088640 | bytes 7864320 | tf_op jit(solution)/shard_map/last_product/pallas_call | solution.py:466
  41.2 0.6 collective-permute-start.14
  41.7 0.1 collective-permute-start.18
  41.8 0.4 collective-permute-start.19
  42.2 0.2 add_convert_fusion.1
  42.4 1.7 %collective-permute-start.12 = (bf16[80,1024]{1,0:T(8,128)(2,1)S(1)}, bf16[80,1024]{1,0:T(8,128)(2,1)S(1)}, u32[]{:S(2)}, u32[]{:S(2)}) collective-permute-start(bf16[80,1024]{1,0:T(8,128)(2,1)S(1)} %get-tuple-element.49), channel_id=1, source_target_pairs={{0,2},{1,3},{2,0},{3,1},{4,6},{5,7},{6,4},{7,5},{8,10},{9,11},{10,... | collective-permute-start | bytes 491528 | tf_op jit(solution)/shard_map/ppermute | solution.py:27
  44.1 0.2 add_convert_fusion
  44.3 1.0 %collective-permute-start.15 = (bf16[80,1024]{1,0:T(8,128)(2,1)S(1)}, bf16[80,1024]{1,0:T(8,128)(2,1)S(1)}, u32[]{:S(2)}, u32[]{:S(2)}) collective-permute-start(bf16[80,1024]{1,0:T(8,128)(2,1)S(1)} %get-tuple-element.52.refs_12_), channel_id=1, source_target_pairs={{0,2},{1,3},{2,0},{3,1},{4,6},{5,7},{6,4},{7,5},{8,10},{9,11},{10,... | collective-permute-start | bytes 491528 | tf_op jit(solution)/shard_map/ppermute | solution.py:27
  45.3 1.3 %order_rows.1.g_ref = bf16[640,1280]{1,0:T(8,128)(2,1)S(1)} custom-call(s32[2]{0:T(128)S(1)} %pad_add_fusion.place_ref, bf16[160,512]{1,0:T(8,128)(2,1)S(1)} %get-tuple-element.30.refs_0_.refs_2_, bf16[160,1024]{1,0:T(8,128)(2,1)S(1)} %collective-permute-done.3.refs_1_.refs_2_, bf16[160,512]{1,0:T(8,128)(2,1)} %collective-permute-done.4.refs_2_, ...), custom_call_target="tpu_custom_call" | custom-call | bytes 3276800 | tf_op jit(solution)/shard_map/order_rows/pallas_call | solution.py:515
  46.7 2.9 %collective-permute-done.12 = bf16[80,1024]{1,0:T(8,128)(2,1)S(1)} collective-permute-done((bf16[80,1024]{1,0:T(8,128)(2,1)S(1)}, bf16[80,1024]{1,0:T(8,128)(2,1)S(1)}, u32[]{:S(2)}, u32[]{:S(2)}) %collective-permute-start.12) | collective-permute-done | bytes 163872 | tf_op jit(solution)/shard_map/ppermute | solution.py:27
  49.5 0.1 add_convert_fusion.6
  49.6 1.9 %collective-permute-start.13 = (bf16[80,1024]{1,0:T(8,128)(2,1)S(1)}, bf16[80,1024]{1,0:T(8,128)(2,1)S(1)}, u32[]{:S(2)}, u32[]{:S(2)}) collective-permute-start(bf16[80,1024]{1,0:T(8,128)(2,1)S(1)} %add_convert_fusion.6), channel_id=1, source_target_pairs={{0,4},{1,5},{2,6},{3,7},{4,0},{5,1},{6,2},{7,3},{8,12},{9,13},{10,... | collective-permute-start | bytes 491528 | tf_op jit(solution)/shard_map/ppermute | solution.py:27
  51.6 1.8 %collective-permute-start.17 = (bf16[80,2048]{1,0:T(8,128)(2,1)S(1)}, bf16[80,2048]{1,0:T(8,128)(2,1)S(1)}, u32[]{:S(2)}, u32[]{:S(2)}) collective-permute-start(bf16[80,2048]{1,0:T(8,128)(2,1)S(1)} %pad_maximum_fusion), channel_id=1, source_target_pairs={{0,2},{1,3},{2,0},{3,1},{4,6},{5,7},{6,4},{7,5},{8,10},{9,11},{10,... | collective-permute-start | bytes 983048 | tf_op jit(solution)/shard_map/ppermute | solution.py:27
  53.3 1.3 %collective-permute-done.15 = bf16[80,1024]{1,0:T(8,128)(2,1)S(1)} collective-permute-done((bf16[80,1024]{1,0:T(8,128)(2,1)S(1)}, bf16[80,1024]{1,0:T(8,128)(2,1)S(1)}, u32[]{:S(2)}, u32[]{:S(2)}) %collective-permute-start.15) | collective-permute-done | bytes 163872 | tf_op jit(solution)/shard_map/ppermute | solution.py:27
  54.6 0.1 add_convert_fusion.2
  54.7 0.6 collective-permute-start.16
  55.3 8.1 %weight_grads.1 = (f32[2048,1024]{1,0:T(8,128)}, f32[2048,128]{1,0:T(8,128)}, f32[2048,128]{1,0:T(8,128)}) custom-call(bf16[640,1280]{1,0:T(8,128)(2,1)S(1)} %order_rows.1.g_ref, bf16[160,2048]{1,0:T(8,128)(2,1)S(1)} %join_rows.1.refs_2_.refs_0_.refs_1_, bf16[160,2048]{1,0:T(8,128)(2,1)S(1)} %join_rows.1.refs_2_.refs_0_.refs_1_, ...), custom_call_target="tpu_custom_call" | custom-call | flops 3355443200 | bytes 14745600 | tf_op jit(solution)/shard_map/weight_grads/pallas_call | solution.py:583
  63.4 2.0 %collective-permute-done.16.refs_3_ = bf16[80,1024]{1,0:T(8,128)(2,1)S(1)} collective-permute-done((bf16[80,1024]{1,0:T(8,128)(2,1)S(1)}, bf16[80,1024]{1,0:T(8,128)(2,1)S(1)}, u32[]{:S(2)}, u32[]{:S(2)}) %collective-permute-start.16) | collective-permute-done | bytes 163872 | tf_op jit(solution)/shard_map/ppermute | solution.py:27
  65.4 0.8 %collective-permute-done.17.refs_4_ = bf16[80,2048]{1,0:T(8,128)(2,1)S(1)} collective-permute-done((bf16[80,2048]{1,0:T(8,128)(2,1)S(1)}, bf16[80,2048]{1,0:T(8,128)(2,1)S(1)}, u32[]{:S(2)}, u32[]{:S(2)}) %collective-permute-start.17) | collective-permute-done | bytes 327712 | tf_op jit(solution)/shard_map/ppermute | solution.py:27
  66.2 0.8 %sum_rows.1 = bf16[80,2048]{1,0:T(8,128)(2,1)} custom-call(bf16[80,1024]{1,0:T(8,128)(2,1)S(1)} %get-tuple-element.50.refs_0_, bf16[80,1024]{1,0:T(8,128)(2,1)S(1)} %collective-permute-done.13.refs_1_, bf16[80,1024]{1,0:T(8,128)(2,1)S(1)} %get-tuple-element.53.refs_2_, bf16[80,1024]{1,0:T(8,128)(2,1)S(1)} %collective-permute-done.16.refs_3_, ...), custom_call_target="tpu_custom_call" | custom-call | flops 409600 | bytes 1638400 | tf_op jit(solution)/shard_map/sum_rows/pallas_call | solution.py:631
  (13 shorter events, 0.1 us)
Async XLA Ops:
  0.6 19.1 %copy-start = (bf16[80,2048]{1,0:T(8,128)(2,1)S(1)}, bf16[80,2048]{1,0:T(8,128)(2,1)}, u32[]{:S(2)}) copy-start(bf16[80,2048]{1,0:T(8,128)(2,1)} %refs_0_.1) | copy-start | bytes 983044
  0.6 19.0 %collective-permute-start.7 = (bf16[80,2048]{1,0:T(8,128)(2,1)}, bf16[80,2048]{1,0:T(8,128)(2,1)S(1)}, u32[]{:S(2)}, u32[]{:S(2)}) collective-permute-start(bf16[80,2048]{1,0:T(8,128)(2,1)} %refs_0_.1), channel_id=1, source_target_pairs={{0,4},{1,5},{2,6},{3,7},{4,0},{5,1},{6,2},{7,3},{8,12},{9,13},{10,... | collective-permute-start | bytes 983048 | tf_op jit(solution)/shard_map/ppermute | solution.py:27
  5.6 5.8 %collective-permute-start.2 = (bf16[176,256]{1,0:T(8,128)(2,1)S(1)}, bf16[176,256]{1,0:T(8,128)(2,1)S(1)}, u32[]{:S(2)}, u32[]{:S(2)}) collective-permute-start(bf16[176,256]{1,0:T(8,128)(2,1)S(1)} %pack.1.refs_0_), channel_id=1, source_target_pairs={{0,24},{8,16},{16,8},{24,0},{1,25},{9,17},{17,9},{25,1},{2,26},{10... | collective-permute-start | bytes 270344 | tf_op jit(solution)/shard_map/ppermute | solution.py:27
  8.1 4.8 %collective-permute-start.1 = (bf16[176,256]{1,0:T(8,128)(2,1)S(1)}, bf16[176,256]{1,0:T(8,128)(2,1)S(1)}, u32[]{:S(2)}, u32[]{:S(2)}) collective-permute-start(bf16[176,256]{1,0:T(8,128)(2,1)S(1)} %pack.1.refs_0_), channel_id=1, source_target_pairs={{0,16},{8,24},{16,0},{24,8},{1,17},{9,25},{17,1},{25,9},{2,18},{10... | collective-permute-start | bytes 270344 | tf_op jit(solution)/shard_map/ppermute | solution.py:27
  8.6 4.5 %collective-permute-start = (bf16[176,256]{1,0:T(8,128)(2,1)S(1)}, bf16[176,256]{1,0:T(8,128)(2,1)S(1)}, u32[]{:S(2)}, u32[]{:S(2)}) collective-permute-start(bf16[176,256]{1,0:T(8,128)(2,1)S(1)} %pack.1.refs_0_), channel_id=1, source_target_pairs={{0,8},{8,0},{16,24},{24,16},{1,9},{9,1},{17,25},{25,17},{2,10},{10... | collective-permute-start | bytes 270344 | tf_op jit(solution)/shard_map/ppermute | solution.py:27
  17.2 10.6 %collective-permute-start.3 = (bf16[160,1024]{1,0:T(8,128)(2,1)S(1)}, bf16[160,1024]{1,0:T(8,128)(2,1)S(1)}, u32[]{:S(2)}, u32[]{:S(2)}) collective-permute-start(bf16[160,1024]{1,0:T(8,128)(2,1)S(1)} %get-tuple-element.31.refs_0_), channel_id=1, source_target_pairs={{0,8},{8,0},{16,24},{24,16},{1,9},{9,1},{17,25},{25,17},{2,10},{10... | collective-permute-start | bytes 983048 | tf_op jit(solution)/shard_map/ppermute | solution.py:27
  18.1 10.7 %collective-permute-start.6 = (bf16[160,1024]{1,0:T(8,128)(2,1)S(1)}, bf16[160,1024]{1,0:T(8,128)(2,1)S(1)}, u32[]{:S(2)}, u32[]{:S(2)}) collective-permute-start(bf16[160,1024]{1,0:T(8,128)(2,1)S(1)} %get-tuple-element.33.refs_0_), channel_id=1, source_target_pairs={{0,16},{8,24},{16,0},{24,8},{1,17},{9,25},{17,1},{25,9},{2,18},{10... | collective-permute-start | bytes 983048 | tf_op jit(solution)/shard_map/ppermute | solution.py:27
  19.9 17.2 %collective-permute-start.8 = (bf16[160,2048]{1,0:T(8,128)(2,1)S(1)}, bf16[160,2048]{1,0:T(8,128)(2,1)S(1)}, u32[]{:S(2)}, u32[]{:S(2)}) collective-permute-start(bf16[160,2048]{1,0:T(8,128)(2,1)S(1)} %join_rows.1.refs_2_.refs_0_.refs_1_), channel_id=1, source_target_pairs={{0,2},{1,3},{2,0},{3,1},{4,6},{5,7},{6,4},{7,5},{8,10},{9,11},{10,... | collective-permute-start | bytes 1966088 | tf_op jit(solution)/shard_map/ppermute | solution.py:27
  21.1 12.4 %collective-permute-start.5 = (bf16[160,512]{1,0:T(8,128)(2,1)}, bf16[160,512]{1,0:T(8,128)(2,1)}, u32[]{:S(2)}, u32[]{:S(2)}) collective-permute-start(bf16[160,512]{1,0:T(8,128)(2,1)} %get-tuple-element.32.refs_3_.refs_4_), channel_id=1, source_target_pairs={{0,8},{8,0},{16,24},{24,16},{1,9},{9,1},{17,25},{25,17},{2,10},{10... | collective-permute-start | bytes 491528 | tf_op jit(solution)/shard_map/ppermute | solution.py:27
  22.6 10.9 %collective-permute-start.4 = (bf16[160,512]{1,0:T(8,128)(2,1)S(1)}, bf16[160,512]{1,0:T(8,128)(2,1)}, u32[]{:S(2)}, u32[]{:S(2)}) collective-permute-start(bf16[160,512]{1,0:T(8,128)(2,1)S(1)} %get-tuple-element.30.refs_0_.refs_2_), channel_id=1, source_target_pairs={{0,16},{8,24},{16,0},{24,8},{1,17},{9,25},{17,1},{25,9},{2,18},{10... | collective-permute-start | bytes 491528 | tf_op jit(solution)/shard_map/ppermute | solution.py:27
  27.9 9.2 %collective-permute-start.9 = (bf16[160,1024]{1,0:T(8,128)(2,1)S(1)}, bf16[160,1024]{1,0:T(8,128)(2,1)S(1)}, u32[]{:S(2)}, u32[]{:S(2)}) collective-permute-start(bf16[160,1024]{1,0:T(8,128)(2,1)S(1)} %combine.2.refs_0_.refs_6_.refs_5_.refs_8_), channel_id=1, source_target_pairs={{0,16},{8,24},{16,0},{24,8},{1,17},{9,25},{17,1},{25,9},{2,18},{10... | collective-permute-start | bytes 983048 | tf_op jit(solution)/shard_map/ppermute | solution.py:27
  28.9 8.3 %collective-permute-start.10 = (bf16[160,1024]{1,0:T(8,128)(2,1)S(1)}, bf16[160,1024]{1,0:T(8,128)(2,1)S(1)}, u32[]{:S(2)}, u32[]{:S(2)}) collective-permute-start(bf16[160,1024]{1,0:T(8,128)(2,1)S(1)} %combine.3.refs_8_.refs_7_.refs_10_), channel_id=1, source_target_pairs={{0,8},{8,0},{16,24},{24,16},{1,9},{9,1},{17,25},{25,17},{2,10},{10... | collective-permute-start | bytes 983048 | tf_op jit(solution)/shard_map/ppermute | solution.py:27
  39.0 3.2 %collective-permute-start.11 = (bf16[320,1024]{1,0:T(8,128)(2,1)S(1)}, bf16[320,1024]{1,0:T(8,128)(2,1)S(1)}, u32[]{:S(2)}, u32[]{:S(2)}) collective-permute-start(bf16[320,1024]{1,0:T(8,128)(2,1)S(1)} %get-tuple-element.35), channel_id=1, source_target_pairs={{0,1},{1,0},{2,3},{3,2},{4,5},{5,4},{6,7},{7,6},{8,9},{9,8},{10,11... | collective-permute-start | bytes 1966088 | tf_op jit(solution)/shard_map/ppermute | solution.py:27
  41.2 2.9 %collective-permute-start.14 = (bf16[320,1024]{1,0:T(8,128)(2,1)S(1)}, bf16[320,1024]{1,0:T(8,128)(2,1)S(1)}, u32[]{:S(2)}, u32[]{:S(2)}) collective-permute-start(bf16[320,1024]{1,0:T(8,128)(2,1)S(1)} %get-tuple-element.39), channel_id=1, source_target_pairs={{0,1},{1,0},{2,3},{3,2},{4,5},{5,4},{6,7},{7,6},{8,9},{9,8},{10,11... | collective-permute-start | bytes 1966088 | tf_op jit(solution)/shard_map/ppermute | solution.py:27
  41.7 13.5 %collective-permute-start.18 = (bf16[160,2048]{1,0:T(8,128)(2,1)S(1)}, bf16[160,2048]{1,0:T(8,128)(2,1)S(1)}, u32[]{:S(2)}, u32[]{:S(2)}) collective-permute-start(bf16[160,2048]{1,0:T(8,128)(2,1)S(1)} %join_rows.1.refs_2_.refs_0_.refs_1_), channel_id=1, source_target_pairs={{0,1},{1,0},{2,3},{3,2},{4,5},{5,4},{6,7},{7,6},{8,9},{9,8},{10,11... | collective-permute-start | bytes 1966088 | tf_op jit(solution)/shard_map/ppermute | solution.py:27
  41.8 13.5 %collective-permute-start.19 = (bf16[160,2048]{1,0:T(8,128)(2,1)S(1)}, bf16[160,2048]{1,0:T(8,128)(2,1)S(1)}, u32[]{:S(2)}, u32[]{:S(2)}) collective-permute-start(bf16[160,2048]{1,0:T(8,128)(2,1)S(1)} %collective-permute-done.8.refs_3_.refs_2_), channel_id=1, source_target_pairs={{0,1},{1,0},{2,3},{3,2},{4,5},{5,4},{6,7},{7,6},{8,9},{9,8},{10,11... | collective-permute-start | bytes 1966088 | tf_op jit(solution)/shard_map/ppermute | solution.py:27
  42.4 7.1 %collective-permute-start.12 = (bf16[80,1024]{1,0:T(8,128)(2,1)S(1)}, bf16[80,1024]{1,0:T(8,128)(2,1)S(1)}, u32[]{:S(2)}, u32[]{:S(2)}) collective-permute-start(bf16[80,1024]{1,0:T(8,128)(2,1)S(1)} %get-tuple-element.49), channel_id=1, source_target_pairs={{0,2},{1,3},{2,0},{3,1},{4,6},{5,7},{6,4},{7,5},{8,10},{9,11},{10,... | collective-permute-start | bytes 491528 | tf_op jit(solution)/shard_map/ppermute | solution.py:27
  44.3 10.4 %collective-permute-start.15 = (bf16[80,1024]{1,0:T(8,128)(2,1)S(1)}, bf16[80,1024]{1,0:T(8,128)(2,1)S(1)}, u32[]{:S(2)}, u32[]{:S(2)}) collective-permute-start(bf16[80,1024]{1,0:T(8,128)(2,1)S(1)} %get-tuple-element.52.refs_12_), channel_id=1, source_target_pairs={{0,2},{1,3},{2,0},{3,1},{4,6},{5,7},{6,4},{7,5},{8,10},{9,11},{10,... | collective-permute-start | bytes 491528 | tf_op jit(solution)/shard_map/ppermute | solution.py:27
  49.6 13.8 %collective-permute-start.13 = (bf16[80,1024]{1,0:T(8,128)(2,1)S(1)}, bf16[80,1024]{1,0:T(8,128)(2,1)S(1)}, u32[]{:S(2)}, u32[]{:S(2)}) collective-permute-start(bf16[80,1024]{1,0:T(8,128)(2,1)S(1)} %add_convert_fusion.6), channel_id=1, source_target_pairs={{0,4},{1,5},{2,6},{3,7},{4,0},{5,1},{6,2},{7,3},{8,12},{9,13},{10,... | collective-permute-start | bytes 491528 | tf_op jit(solution)/shard_map/ppermute | solution.py:27
  51.6 14.7 %collective-permute-start.17 = (bf16[80,2048]{1,0:T(8,128)(2,1)S(1)}, bf16[80,2048]{1,0:T(8,128)(2,1)S(1)}, u32[]{:S(2)}, u32[]{:S(2)}) collective-permute-start(bf16[80,2048]{1,0:T(8,128)(2,1)S(1)} %pad_maximum_fusion), channel_id=1, source_target_pairs={{0,2},{1,3},{2,0},{3,1},{4,6},{5,7},{6,4},{7,5},{8,10},{9,11},{10,... | collective-permute-start | bytes 983048 | tf_op jit(solution)/shard_map/ppermute | solution.py:27
  54.7 10.7 %collective-permute-start.16 = (bf16[80,1024]{1,0:T(8,128)(2,1)S(1)}, bf16[80,1024]{1,0:T(8,128)(2,1)S(1)}, u32[]{:S(2)}, u32[]{:S(2)}) collective-permute-start(bf16[80,1024]{1,0:T(8,128)(2,1)S(1)} %add_convert_fusion.2), channel_id=1, source_target_pairs={{0,4},{1,5},{2,6},{3,7},{4,0},{5,1},{6,2},{7,3},{8,12},{9,13},{10,... | collective-permute-start | bytes 491528 | tf_op jit(solution)/shard_map/ppermute | solution.py:27

commit v3 on v1

--- a/solution.py
+++ b/solution.py
@@ -258,10 +258,13 @@
 
 
 def summed_block(packet_ref, other_ref, blocks, b, offset, rows):
-    first = packet_ref.shape[1] - (blocks - b) * HEAD_SIZE
-    total = packet_ref[rows, first : first + HEAD_SIZE].astype(jnp.float32)
-    first = other_ref.shape[1] - (blocks - (b ^ offset)) * HEAD_SIZE
-    total += other_ref[rows, first : first + HEAD_SIZE].astype(jnp.float32)
+    def block_of(ref, index):
+        first = ref.shape[1] - (blocks - index) * HEAD_SIZE
+        if not isinstance(index, int):
+            first = pl.multiple_of(first, HEAD_SIZE)
+        return ref[rows, pl.ds(first, HEAD_SIZE)].astype(jnp.float32)
+
+    total = block_of(packet_ref, b) + block_of(other_ref, b ^ offset)
     return total.astype(jnp.bfloat16)
 
 
@@ -414,6 +417,14 @@
                     put(q, side, slice(first, first + half), b, (core ^ side) * half)
 
 
+def place_in(members, b):
+    place, found = jnp.int32(0), jnp.bool_(False)
+    for i, member in enumerate(members):
+        place = jnp.where(b == member, i, place)
+        found = found | (b == member)
+    return place, found
+
+
 def last_kernel(early, late, columns, offsets, part, width, spare, place_ref, *refs):
     blocks = len(early) + len(late)
     early_ref, w_ref, refs = refs[0], refs[1], refs[2 + spare :]
@@ -432,27 +443,30 @@
                 :, first : first + width
             ]
 
-    def put_rows(q, side, target, b, start):
-        put_pair(gkv, target, 0, sums, offsets, blocks, b, start)
-
-    by_destination(blocks, half, place_ref, put_rows)
+    core, turn = place_ref[0], place_ref[1]
+    targets = [
+        (q, side, slice((side * blocks + q) * half, (side * blocks + q + 1) * half))
+        for q in range(blocks)
+        for side in range(2)
+    ]
+    for q, side, target in targets:
+        put_pair(gkv, target, 0, sums, offsets, blocks, q ^ turn, (core ^ side) * half)
     query[...] = contract(gq[...], w_ref[: 2 * width, cols], 1, 0).astype(jnp.bfloat16)
     pair[...] = contract(gkv[...], w_ref[2 * width :, cols], 1, 0)
 
-    def put_sum(q, side, target, b, start):
-        if b in late:
-            rows = pl.ds(pl.multiple_of(late.index(b) * tokens + start, 16), half)
-            part_sum = query[rows, :]
-        else:
-            rows = pl.ds(pl.multiple_of(early.index(b) * tokens + start, 16), half)
-            part_sum = early_ref[rows, cols]
-        total = (pair[target, :] + part_sum.astype(jnp.float32)).astype(jnp.bfloat16)
-        if side:
-            other_ref[q * half : (q + 1) * half, :] = total
-        else:
-            mine_refs[q][...] = total
-
-    by_destination(blocks, half, place_ref, put_sum)
+    for q, side, target in targets:
+        early_place, in_early = place_in(early, q ^ turn)
+        late_place, in_late = place_in(late, q ^ turn)
+        out_ref = other_ref.at[q * half : (q + 1) * half, :] if side else mine_refs[q]
+
+        def put(part_ref, place, part_cols):
+            start = place * tokens + (core ^ side) * half
+            rows = pl.ds(pl.multiple_of(start, 16), half)
+            total = pair[target, :] + part_ref[rows, part_cols].astype(jnp.float32)
+            out_ref[...] = total.astype(jnp.bfloat16)
+
+        pl.when(in_early)(functools.partial(put, early_ref, early_place, cols))
+        pl.when(in_late)(functools.partial(put, query, late_place, slice(None)))
 
 
 def last_product(place, early, late, early_part, pieces, sums, offsets, weights, width, part, after):

time: 67.4 us -> 67.2 us (level)
  no operation moved by 1% of the time
where the time goes in v3:
time: 67.2 us; the launch traced here: 66.9 us
  Pallas kernels  28.3 us (42%)
  starting transfers between devices  24.2 us (36%)
  waiting for transfers between devices  13.1 us (19%)
  between operations  0.78 us (1%)
    ppermute x20, starting transfers between devices, swap(): return lax.ppermute(value, axis, pairs)  24.2 us
    ppermute x20, waiting for transfers between devices, swap(): return lax.ppermute(value, axis, pairs)  13.1 us
    pallas_call x1, Pallas kernels, weight_grads(): pl.pallas_call(functools.partial(weight_grad_kernel, places), grid=(featu...  8.14 us
    pallas_call x1, Pallas kernels, attention_backward(): pl.pallas_call(functools.partial(attention_kernel, heads, blocks), out_sh...  4.05 us
    pallas_call x2, Pallas kernels, last_product(): pl.pallas_call(functools.partial(last_kernel, early, late, columns, offse...  3.73 us
    pallas_call x1, Pallas kernels, turn_weights(): pl.pallas_call(functools.partial(turn_kernel, tile), out_shape=pltpu.VMEM...  3.44 us
    pallas_call x1, Pallas kernels, early_product(): pl.pallas_call(functools.partial(early_kernel, columns, tile), out_shape=...  3.31 us
    pallas_call x1, Pallas kernels, prepare(): pl.pallas_call(functools.partial(prepare_kernel, heads, blocks), out_shap...  2.25 us
  transfers between devices with their start and end apart: 20, of which 10 were waited for; matrix products, arithmetic and copies ran while one was open for 1% of the time, Pallas kernels for 38%

profile of v3, /device:TPU:0, one launch (start us, length us, event | category | flops | bytes accessed | tf_op | source)
XLA Modules:
  0.0 66.9 jit_solution(4553379558045638868)
XLA Ops:
  0.6 4.1 %collective-permute-start.7 = (bf16[80,2048]{1,0:T(8,128)(2,1)}, bf16[80,2048]{1,0:T(8,128)(2,1)S(1)}, u32[]{:S(2)}, u32[]{:S(2)}) collective-permute-start(bf16[80,2048]{1,0:T(8,128)(2,1)} %refs_0_.1), channel_id=1, source_target_pairs={{0,4},{1,5},{2,6},{3,7},{4,0},{5,1},{6,2},{7,3},{8,12},{9,13},{10,... | collective-permute-start | bytes 983048 | tf_op jit(solution)/shard_map/ppermute | solution.py:27
  4.7 0.8 %pack.1.refs_0_ = bf16[176,256]{1,0:T(8,128)(2,1)S(1)} custom-call(bf16[160,128]{1,0:T(8,128)(2,1)} %k_ref.1, bf16[160,128]{1,0:T(8,128)(2,1)} %v_ref.1, s32[1,160]{1,0:T(1,128)} %bitcast.5), custom_call_target="tpu_custom_call" | custom-call | bytes 163840 | tf_op jit(solution)/shard_map/pack/pallas_call | solution.py:71
  5.6 2.5 %collective-permute-start.2 = (bf16[176,256]{1,0:T(8,128)(2,1)S(1)}, bf16[176,256]{1,0:T(8,128)(2,1)S(1)}, u32[]{:S(2)}, u32[]{:S(2)}) collective-permute-start(bf16[176,256]{1,0:T(8,128)(2,1)S(1)} %pack.1.refs_0_), channel_id=1, source_target_pairs={{0,24},{8,16},{16,8},{24,0},{1,25},{9,17},{17,9},{25,1},{2,26},{10... | collective-permute-start | bytes 270344 | tf_op jit(solution)/shard_map/ppermute | solution.py:27
  8.1 0.5 collective-permute-start.1
  8.6 0.5 collective-permute-start
  9.1 2.2 %prepare.1 = (bf16[1280,128]{1,0:T(8,128)(2,1)S(1)}, bf16[1280,128]{1,0:T(8,128)(2,1)S(1)}, f32[640,128]{1,0:T(8,128)S(1)}, f32[640,128]{1,0:T(8,128)S(1)}) custom-call(s32[1]{0:T(128)} %bitcast.2.row_ref, bf16[160,1024]{1,0:T(8,128)(2,1)} %q_hbm.1, bf16[160,1024]{1,0:T(8,128)(2,1)} %o_hbm.1, s32[1,160]{1,0:T(1,128)} %bitcast.7, s32[1,160]{1,0:T(1,128)} %bitcast.6, ...), custom_call_target="tpu_custom_call" | custom-call | bytes 1310720 | tf_op jit(solution)/shard_map/prepare/pallas_call | solution.py:130
  11.4 1.5 %collective-permute-done.1.refs_2_ = bf16[176,256]{1,0:T(8,128)(2,1)S(1)} collective-permute-done((bf16[176,256]{1,0:T(8,128)(2,1)S(1)}, bf16[176,256]{1,0:T(8,128)(2,1)S(1)}, u32[]{:S(2)}, u32[]{:S(2)}) %collective-permute-start.1) | collective-permute-done | bytes 90144 | tf_op jit(solution)/shard_map/ppermute | solution.py:27
  12.8 0.3 collective-permute-done.refs_1_
  13.1 4.0 %attention_backward.1 = (bf16[160,512]{1,0:T(8,128)(2,1)S(1)}, bf16[160,512]{1,0:T(8,128)(2,1)}, bf16[160,1024]{1,0:T(8,128)(2,1)S(1)}, bf16[160,1024]{1,0:T(8,128)(2,1)S(1)}) custom-call(s32[1]{0:T(128)} %bitcast.2.row_ref, bf16[1280,128]{1,0:T(8,128)(2,1)S(1)} %get-tuple-element.26.q_all, bf16[1280,128]{1,0:T(8,128)(2,1)S(1)} %get-tuple-element.27.o_all, ...), custom_call_target="tpu_custom_call" | custom-call | flops 1048576000 | bytes 2621440 | tf_op jit(solution)/shard_map/attention_backward/pallas_call | solution.py:224
  17.2 1.0 %collective-permute-start.3 = (bf16[160,1024]{1,0:T(8,128)(2,1)S(1)}, bf16[160,1024]{1,0:T(8,128)(2,1)S(1)}, u32[]{:S(2)}, u32[]{:S(2)}) collective-permute-start(bf16[160,1024]{1,0:T(8,128)(2,1)S(1)} %get-tuple-element.31.refs_0_), channel_id=1, source_target_pairs={{0,8},{8,0},{16,24},{24,16},{1,9},{9,1},{17,25},{25,17},{2,10},{10... | collective-permute-start | bytes 983048 | tf_op jit(solution)/shard_map/ppermute | solution.py:27
  18.1 1.1 %collective-permute-start.6 = (bf16[160,1024]{1,0:T(8,128)(2,1)S(1)}, bf16[160,1024]{1,0:T(8,128)(2,1)S(1)}, u32[]{:S(2)}, u32[]{:S(2)}) collective-permute-start(bf16[160,1024]{1,0:T(8,128)(2,1)S(1)} %get-tuple-element.33.refs_0_), channel_id=1, source_target_pairs={{0,16},{8,24},{16,0},{24,8},{1,17},{9,25},{17,1},{25,9},{2,18},{10... | collective-permute-start | bytes 983048 | tf_op jit(solution)/shard_map/ppermute | solution.py:27
  19.2 0.5 collective-permute-done.7.refs_1_
  19.7 0.2 join_rows.1.refs_2_.refs_0_.refs_1_
  19.9 1.2 %collective-permute-start.8 = (bf16[160,2048]{1,0:T(8,128)(2,1)S(1)}, bf16[160,2048]{1,0:T(8,128)(2,1)S(1)}, u32[]{:S(2)}, u32[]{:S(2)}) collective-permute-start(bf16[160,2048]{1,0:T(8,128)(2,1)S(1)} %join_rows.1.refs_2_.refs_0_.refs_1_), channel_id=1, source_target_pairs={{0,2},{1,3},{2,0},{3,1},{4,6},{5,7},{6,4},{7,5},{8,10},{9,11},{10,... | collective-permute-start | bytes 1966088 | tf_op jit(solution)/shard_map/ppermute | solution.py:27
  21.1 1.5 %collective-permute-start.5 = (bf16[160,512]{1,0:T(8,128)(2,1)}, bf16[160,512]{1,0:T(8,128)(2,1)}, u32[]{:S(2)}, u32[]{:S(2)}) collective-permute-start(bf16[160,512]{1,0:T(8,128)(2,1)} %get-tuple-element.32.refs_3_.refs_4_), channel_id=1, source_target_pairs={{0,8},{8,0},{16,24},{24,16},{1,9},{9,1},{17,25},{25,17},{2,10},{10... | collective-permute-start | bytes 491528 | tf_op jit(solution)/shard_map/ppermute | solution.py:27
  22.6 1.2 %collective-permute-start.4 = (bf16[160,512]{1,0:T(8,128)(2,1)S(1)}, bf16[160,512]{1,0:T(8,128)(2,1)}, u32[]{:S(2)}, u32[]{:S(2)}) collective-permute-start(bf16[160,512]{1,0:T(8,128)(2,1)S(1)} %get-tuple-element.30.refs_0_.refs_2_), channel_id=1, source_target_pairs={{0,16},{8,24},{16,0},{24,8},{1,17},{9,25},{17,1},{25,9},{2,18},{10... | collective-permute-start | bytes 491528 | tf_op jit(solution)/shard_map/ppermute | solution.py:27
  23.8 4.0 %collective-permute-done.3.refs_1_.refs_2_ = bf16[160,1024]{1,0:T(8,128)(2,1)S(1)} collective-permute-done((bf16[160,1024]{1,0:T(8,128)(2,1)S(1)}, bf16[160,1024]{1,0:T(8,128)(2,1)S(1)}, u32[]{:S(2)}, u32[]{:S(2)}) %collective-permute-start.3) | collective-permute-done | bytes 327712 | tf_op jit(solution)/shard_map/ppermute | solution.py:27
  27.8 0.1 combine.2.refs_0_.refs_6_.refs_5_.refs_8_
  27.9 0.9 %collective-permute-start.9 = (bf16[160,1024]{1,0:T(8,128)(2,1)S(1)}, bf16[160,1024]{1,0:T(8,128)(2,1)S(1)}, u32[]{:S(2)}, u32[]{:S(2)}) collective-permute-start(bf16[160,1024]{1,0:T(8,128)(2,1)S(1)} %combine.2.refs_0_.refs_6_.refs_5_.refs_8_), channel_id=1, source_target_pairs={{0,16},{8,24},{16,0},{24,8},{1,17},{9,25},{17,1},{25,9},{2,18},{10... | collective-permute-start | bytes 983048 | tf_op jit(solution)/shard_map/ppermute | solution.py:27
  28.7 0.1 collective-permute-done.6.refs_5_.refs_1_.refs_2_.refs_6_
  28.8 0.1 combine.3.refs_8_.refs_7_.refs_10_
  28.9 1.1 %collective-permute-start.10 = (bf16[160,1024]{1,0:T(8,128)(2,1)S(1)}, bf16[160,1024]{1,0:T(8,128)(2,1)S(1)}, u32[]{:S(2)}, u32[]{:S(2)}) collective-permute-start(bf16[160,1024]{1,0:T(8,128)(2,1)S(1)} %combine.3.refs_8_.refs_7_.refs_10_), channel_id=1, source_target_pairs={{0,8},{8,0},{16,24},{24,16},{1,9},{9,1},{17,25},{25,17},{2,10},{10... | collective-permute-start | bytes 983048 | tf_op jit(solution)/shard_map/ppermute | solution.py:27
  30.0 0.1 pad_add_fusion.place_ref
  30.0 3.4 %turn_weights.1.refs_6_.refs_1_ = bf16[1280,2048]{1,0:T(8,128)(2,1)S(1)} custom-call(bf16[2048,1024]{1,0:T(8,128)(2,1)} %wq_hbm.1, bf16[2048,128]{1,0:T(8,128)(2,1)} %wk_hbm.1, bf16[2048,128]{1,0:T(8,128)(2,1)} %wv_hbm.1, bf16[160,1024]{1,0:T(8,128)(2,1)S(1)} %combine.2.refs_0_.refs_6_.refs_5_.refs_8_), custom_call_target="tpu_custom_call" | custom-call | bytes 10485760 | tf_op jit(solution)/shard_map/turn_weights/pallas_call | solution.py:338
  33.5 3.3 %early_product.1.refs_0_ = bf16[480,2048]{1,0:T(8,128)(2,1)S(1)} custom-call(bf16[160,512]{1,0:T(8,128)(2,1)S(1)} %get-tuple-element.30.refs_0_.refs_2_, bf16[160,1024]{1,0:T(8,128)(2,1)S(1)} %collective-permute-done.3.refs_1_.refs_2_, bf16[160,512]{1,0:T(8,128)(2,1)} %collective-permute-done.4.refs_2_, bf16[160,512]{1,0:T(8,128)(2,1)} %get-tuple-element.32.refs_3_.refs_4_, ...), custom_call_target="tpu_custom_call" | custom-call | flops 2013265920 | bytes 7143424 | tf_op jit(solution)/shard_map/early_product/pallas_call | solution.py:377
  36.8 0.3 collective-permute-done.9.refs_4_.refs_7_.refs_3_.refs_6_.refs_9_
  37.1 1.8 %last_product.2 = (bf16[80,1024]{1,0:T(8,128)(2,1)S(1)}, bf16[80,1024]{1,0:T(8,128)(2,1)S(1)}, bf16[80,1024]{1,0:T(8,128)(2,1)S(1)}, bf16[80,1024]{1,0:T(8,128)(2,1)S(1)}, bf16[320,1024]{1,0:T(8,128)(2,1)S(1)}) custom-call(s32[2]{0:T(128)S(1)} %pad_add_fusion.place_ref, bf16[480,2048]{1,0:T(8,128)(2,1)S(1)} %early_product.1.refs_0_, ...), custom_call_target="tpu_custom_call" | custom-call | flops 671088640 | bytes 7864320 | tf_op jit(solution)/shard_map/last_product/pallas_call | solution.py:480
  38.9 0.1 collective-permute-start.11
  39.0 2.0 %last_product.3 = (bf16[80,1024]{1,0:T(8,128)(2,1)S(1)}, bf16[80,1024]{1,0:T(8,128)(2,1)S(1)}, bf16[80,1024]{1,0:T(8,128)(2,1)S(1)}, bf16[80,1024]{1,0:T(8,128)(2,1)S(1)}, bf16[320,1024]{1,0:T(8,128)(2,1)S(1)}) custom-call(s32[2]{0:T(128)S(1)} %pad_add_fusion.place_ref, bf16[480,2048]{1,0:T(8,128)(2,1)S(1)} %early_product.1.refs_0_, ...), custom_call_target="tpu_custom_call" | custom-call | flops 671088640 | bytes 7864320 | tf_op jit(solution)/shard_map/last_product/pallas_call | solution.py:480
  40.9 0.6 collective-permute-start.14
  41.5 0.1 collective-permute-start.18
  41.6 0.4 collective-permute-start.19
  42.0 0.2 add_convert_fusion.1
  42.2 1.7 %collective-permute-start.12 = (bf16[80,1024]{1,0:T(8,128)(2,1)S(1)}, bf16[80,1024]{1,0:T(8,128)(2,1)S(1)}, u32[]{:S(2)}, u32[]{:S(2)}) collective-permute-start(bf16[80,1024]{1,0:T(8,128)(2,1)S(1)} %get-tuple-element.49), channel_id=1, source_target_pairs={{0,2},{1,3},{2,0},{3,1},{4,6},{5,7},{6,4},{7,5},{8,10},{9,11},{10,... | collective-permute-start | bytes 491528 | tf_op jit(solution)/shard_map/ppermute | solution.py:27
  43.9 0.2 add_convert_fusion
  44.1 1.0 %collective-permute-start.15 = (bf16[80,1024]{1,0:T(8,128)(2,1)S(1)}, bf16[80,1024]{1,0:T(8,128)(2,1)S(1)}, u32[]{:S(2)}, u32[]{:S(2)}) collective-permute-start(bf16[80,1024]{1,0:T(8,128)(2,1)S(1)} %get-tuple-element.52.refs_12_), channel_id=1, source_target_pairs={{0,2},{1,3},{2,0},{3,1},{4,6},{5,7},{6,4},{7,5},{8,10},{9,11},{10,... | collective-permute-start | bytes 491528 | tf_op jit(solution)/shard_map/ppermute | solution.py:27
  45.1 1.3 %order_rows.1.g_ref = bf16[640,1280]{1,0:T(8,128)(2,1)S(1)} custom-call(s32[2]{0:T(128)S(1)} %pad_add_fusion.place_ref, bf16[160,512]{1,0:T(8,128)(2,1)S(1)} %get-tuple-element.30.refs_0_.refs_2_, bf16[160,1024]{1,0:T(8,128)(2,1)S(1)} %collective-permute-done.3.refs_1_.refs_2_, bf16[160,512]{1,0:T(8,128)(2,1)} %collective-permute-done.4.refs_2_, ...), custom_call_target="tpu_custom_call" | custom-call | bytes 3276800 | tf_op jit(solution)/shard_map/order_rows/pallas_call | solution.py:529
  46.5 2.8 %collective-permute-done.12 = bf16[80,1024]{1,0:T(8,128)(2,1)S(1)} collective-permute-done((bf16[80,1024]{1,0:T(8,128)(2,1)S(1)}, bf16[80,1024]{1,0:T(8,128)(2,1)S(1)}, u32[]{:S(2)}, u32[]{:S(2)}) %collective-permute-start.12) | collective-permute-done | bytes 163872 | tf_op jit(solution)/shard_map/ppermute | solution.py:27
  49.3 0.1 add_convert_fusion.6
  49.4 1.9 %collective-permute-start.13 = (bf16[80,1024]{1,0:T(8,128)(2,1)S(1)}, bf16[80,1024]{1,0:T(8,128)(2,1)S(1)}, u32[]{:S(2)}, u32[]{:S(2)}) collective-permute-start(bf16[80,1024]{1,0:T(8,128)(2,1)S(1)} %add_convert_fusion.6), channel_id=1, source_target_pairs={{0,4},{1,5},{2,6},{3,7},{4,0},{5,1},{6,2},{7,3},{8,12},{9,13},{10,... | collective-permute-start | bytes 491528 | tf_op jit(solution)/shard_map/ppermute | solution.py:27
  51.3 2.3 %collective-permute-done.15 = bf16[80,1024]{1,0:T(8,128)(2,1)S(1)} collective-permute-done((bf16[80,1024]{1,0:T(8,128)(2,1)S(1)}, bf16[80,1024]{1,0:T(8,128)(2,1)S(1)}, u32[]{:S(2)}, u32[]{:S(2)}) %collective-permute-start.15) | collective-permute-done | bytes 163872 | tf_op jit(solution)/shard_map/ppermute | solution.py:27
  53.6 0.8 %collective-permute-start.17 = (bf16[80,2048]{1,0:T(8,128)(2,1)S(1)}, bf16[80,2048]{1,0:T(8,128)(2,1)S(1)}, u32[]{:S(2)}, u32[]{:S(2)}) collective-permute-start(bf16[80,2048]{1,0:T(8,128)(2,1)S(1)} %pad_maximum_fusion), channel_id=1, source_target_pairs={{0,2},{1,3},{2,0},{3,1},{4,6},{5,7},{6,4},{7,5},{8,10},{9,11},{10,... | collective-permute-start | bytes 983048 | tf_op jit(solution)/shard_map/ppermute | solution.py:27
  54.5 0.1 add_convert_fusion.2
  54.5 2.0 %collective-permute-start.16 = (bf16[80,1024]{1,0:T(8,128)(2,1)S(1)}, bf16[80,1024]{1,0:T(8,128)(2,1)S(1)}, u32[]{:S(2)}, u32[]{:S(2)}) collective-permute-start(bf16[80,1024]{1,0:T(8,128)(2,1)S(1)} %add_convert_fusion.2), channel_id=1, source_target_pairs={{0,4},{1,5},{2,6},{3,7},{4,0},{5,1},{6,2},{7,3},{8,12},{9,13},{10,... | collective-permute-start | bytes 491528 | tf_op jit(solution)/shard_map/ppermute | solution.py:27
  56.5 8.1 %weight_grads.1 = (f32[2048,1024]{1,0:T(8,128)}, f32[2048,128]{1,0:T(8,128)}, f32[2048,128]{1,0:T(8,128)}) custom-call(bf16[640,1280]{1,0:T(8,128)(2,1)S(1)} %order_rows.1.g_ref, bf16[160,2048]{1,0:T(8,128)(2,1)S(1)} %join_rows.1.refs_2_.refs_0_.refs_1_, bf16[160,2048]{1,0:T(8,128)(2,1)S(1)} %join_rows.1.refs_2_.refs_0_.refs_1_, ...), custom_call_target="tpu_custom_call" | custom-call | flops 3355443200 | bytes 14745600 | tf_op jit(solution)/shard_map/weight_grads/pallas_call | solution.py:597
  64.6 0.5 collective-permute-done.16.refs_3_
  65.2 0.9 %collective-permute-done.17.refs_4_ = bf16[80,2048]{1,0:T(8,128)(2,1)S(1)} collective-permute-done((bf16[80,2048]{1,0:T(8,128)(2,1)S(1)}, bf16[80,2048]{1,0:T(8,128)(2,1)S(1)}, u32[]{:S(2)}, u32[]{:S(2)}) %collective-permute-start.17) | collective-permute-done | bytes 327712 | tf_op jit(solution)/shard_map/ppermute | solution.py:27
  66.1 0.8 %sum_rows.1 = bf16[80,2048]{1,0:T(8,128)(2,1)} custom-call(bf16[80,1024]{1,0:T(8,128)(2,1)S(1)} %get-tuple-element.50.refs_0_, bf16[80,1024]{1,0:T(8,128)(2,1)S(1)} %collective-permute-done.13.refs_1_, bf16[80,1024]{1,0:T(8,128)(2,1)S(1)} %get-tuple-element.53.refs_2_, bf16[80,1024]{1,0:T(8,128)(2,1)S(1)} %collective-permute-done.16.refs_3_, ...), custom_call_target="tpu_custom_call" | custom-call | flops 409600 | bytes 1638400 | tf_op jit(solution)/shard_map/sum_rows/pallas_call | solution.py:645
  (13 shorter events, 0.1 us)
Async XLA Ops:
  0.6 19.1 %copy-start = (bf16[80,2048]{1,0:T(8,128)(2,1)S(1)}, bf16[80,2048]{1,0:T(8,128)(2,1)}, u32[]{:S(2)}) copy-start(bf16[80,2048]{1,0:T(8,128)(2,1)} %refs_0_.1) | copy-start | bytes 983044
  0.6 19.0 %collective-permute-start.7 = (bf16[80,2048]{1,0:T(8,128)(2,1)}, bf16[80,2048]{1,0:T(8,128)(2,1)S(1)}, u32[]{:S(2)}, u32[]{:S(2)}) collective-permute-start(bf16[80,2048]{1,0:T(8,128)(2,1)} %refs_0_.1), channel_id=1, source_target_pairs={{0,4},{1,5},{2,6},{3,7},{4,0},{5,1},{6,2},{7,3},{8,12},{9,13},{10,... | collective-permute-start | bytes 983048 | tf_op jit(solution)/shard_map/ppermute | solution.py:27
  5.6 5.8 %collective-permute-start.2 = (bf16[176,256]{1,0:T(8,128)(2,1)S(1)}, bf16[176,256]{1,0:T(8,128)(2,1)S(1)}, u32[]{:S(2)}, u32[]{:S(2)}) collective-permute-start(bf16[176,256]{1,0:T(8,128)(2,1)S(1)} %pack.1.refs_0_), channel_id=1, source_target_pairs={{0,24},{8,16},{16,8},{24,0},{1,25},{9,17},{17,9},{25,1},{2,26},{10... | collective-permute-start | bytes 270344 | tf_op jit(solution)/shard_map/ppermute | solution.py:27
  8.1 4.8 %collective-permute-start.1 = (bf16[176,256]{1,0:T(8,128)(2,1)S(1)}, bf16[176,256]{1,0:T(8,128)(2,1)S(1)}, u32[]{:S(2)}, u32[]{:S(2)}) collective-permute-start(bf16[176,256]{1,0:T(8,128)(2,1)S(1)} %pack.1.refs_0_), channel_id=1, source_target_pairs={{0,16},{8,24},{16,0},{24,8},{1,17},{9,25},{17,1},{25,9},{2,18},{10... | collective-permute-start | bytes 270344 | tf_op jit(solution)/shard_map/ppermute | solution.py:27
  8.6 4.5 %collective-permute-start = (bf16[176,256]{1,0:T(8,128)(2,1)S(1)}, bf16[176,256]{1,0:T(8,128)(2,1)S(1)}, u32[]{:S(2)}, u32[]{:S(2)}) collective-permute-start(bf16[176,256]{1,0:T(8,128)(2,1)S(1)} %pack.1.refs_0_), channel_id=1, source_target_pairs={{0,8},{8,0},{16,24},{24,16},{1,9},{9,1},{17,25},{25,17},{2,10},{10... | collective-permute-start | bytes 270344 | tf_op jit(solution)/shard_map/ppermute | solution.py:27
  17.2 10.6 %collective-permute-start.3 = (bf16[160,1024]{1,0:T(8,128)(2,1)S(1)}, bf16[160,1024]{1,0:T(8,128)(2,1)S(1)}, u32[]{:S(2)}, u32[]{:S(2)}) collective-permute-start(bf16[160,1024]{1,0:T(8,128)(2,1)S(1)} %get-tuple-element.31.refs_0_), channel_id=1, source_target_pairs={{0,8},{8,0},{16,24},{24,16},{1,9},{9,1},{17,25},{25,17},{2,10},{10... | collective-permute-start | bytes 983048 | tf_op jit(solution)/shard_map/ppermute | solution.py:27
  18.1 10.7 %collective-permute-start.6 = (bf16[160,1024]{1,0:T(8,128)(2,1)S(1)}, bf16[160,1024]{1,0:T(8,128)(2,1)S(1)}, u32[]{:S(2)}, u32[]{:S(2)}) collective-permute-start(bf16[160,1024]{1,0:T(8,128)(2,1)S(1)} %get-tuple-element.33.refs_0_), channel_id=1, source_target_pairs={{0,16},{8,24},{16,0},{24,8},{1,17},{9,25},{17,1},{25,9},{2,18},{10... | collective-permute-start | bytes 983048 | tf_op jit(solution)/shard_map/ppermute | solution.py:27
  19.9 17.2 %collective-permute-start.8 = (bf16[160,2048]{1,0:T(8,128)(2,1)S(1)}, bf16[160,2048]{1,0:T(8,128)(2,1)S(1)}, u32[]{:S(2)}, u32[]{:S(2)}) collective-permute-start(bf16[160,2048]{1,0:T(8,128)(2,1)S(1)} %join_rows.1.refs_2_.refs_0_.refs_1_), channel_id=1, source_target_pairs={{0,2},{1,3},{2,0},{3,1},{4,6},{5,7},{6,4},{7,5},{8,10},{9,11},{10,... | collective-permute-start | bytes 1966088 | tf_op jit(solution)/shard_map/ppermute | solution.py:27
  21.1 12.4 %collective-permute-start.5 = (bf16[160,512]{1,0:T(8,128)(2,1)}, bf16[160,512]{1,0:T(8,128)(2,1)}, u32[]{:S(2)}, u32[]{:S(2)}) collective-permute-start(bf16[160,512]{1,0:T(8,128)(2,1)} %get-tuple-element.32.refs_3_.refs_4_), channel_id=1, source_target_pairs={{0,8},{8,0},{16,24},{24,16},{1,9},{9,1},{17,25},{25,17},{2,10},{10... | collective-permute-start | bytes 491528 | tf_op jit(solution)/shard_map/ppermute | solution.py:27
  22.6 10.9 %collective-permute-start.4 = (bf16[160,512]{1,0:T(8,128)(2,1)S(1)}, bf16[160,512]{1,0:T(8,128)(2,1)}, u32[]{:S(2)}, u32[]{:S(2)}) collective-permute-start(bf16[160,512]{1,0:T(8,128)(2,1)S(1)} %get-tuple-element.30.refs_0_.refs_2_), channel_id=1, source_target_pairs={{0,16},{8,24},{16,0},{24,8},{1,17},{9,25},{17,1},{25,9},{2,18},{10... | collective-permute-start | bytes 491528 | tf_op jit(solution)/shard_map/ppermute | solution.py:27
  27.9 9.2 %collective-permute-start.9 = (bf16[160,1024]{1,0:T(8,128)(2,1)S(1)}, bf16[160,1024]{1,0:T(8,128)(2,1)S(1)}, u32[]{:S(2)}, u32[]{:S(2)}) collective-permute-start(bf16[160,1024]{1,0:T(8,128)(2,1)S(1)} %combine.2.refs_0_.refs_6_.refs_5_.refs_8_), channel_id=1, source_target_pairs={{0,16},{8,24},{16,0},{24,8},{1,17},{9,25},{17,1},{25,9},{2,18},{10... | collective-permute-start | bytes 983048 | tf_op jit(solution)/shard_map/ppermute | solution.py:27
  28.9 8.3 %collective-permute-start.10 = (bf16[160,1024]{1,0:T(8,128)(2,1)S(1)}, bf16[160,1024]{1,0:T(8,128)(2,1)S(1)}, u32[]{:S(2)}, u32[]{:S(2)}) collective-permute-start(bf16[160,1024]{1,0:T(8,128)(2,1)S(1)} %combine.3.refs_8_.refs_7_.refs_10_), channel_id=1, source_target_pairs={{0,8},{8,0},{16,24},{24,16},{1,9},{9,1},{17,25},{25,17},{2,10},{10... | collective-permute-start | bytes 983048 | tf_op jit(solution)/shard_map/ppermute | solution.py:27
  38.9 3.1 %collective-permute-start.11 = (bf16[320,1024]{1,0:T(8,128)(2,1)S(1)}, bf16[320,1024]{1,0:T(8,128)(2,1)S(1)}, u32[]{:S(2)}, u32[]{:S(2)}) collective-permute-start(bf16[320,1024]{1,0:T(8,128)(2,1)S(1)} %get-tuple-element.35), channel_id=1, source_target_pairs={{0,1},{1,0},{2,3},{3,2},{4,5},{5,4},{6,7},{7,6},{8,9},{9,8},{10,11... | collective-permute-start | bytes 1966088 | tf_op jit(solution)/shard_map/ppermute | solution.py:27
  40.9 2.9 %collective-permute-start.14 = (bf16[320,1024]{1,0:T(8,128)(2,1)S(1)}, bf16[320,1024]{1,0:T(8,128)(2,1)S(1)}, u32[]{:S(2)}, u32[]{:S(2)}) collective-permute-start(bf16[320,1024]{1,0:T(8,128)(2,1)S(1)} %get-tuple-element.39), channel_id=1, source_target_pairs={{0,1},{1,0},{2,3},{3,2},{4,5},{5,4},{6,7},{7,6},{8,9},{9,8},{10,11... | collective-permute-start | bytes 1966088 | tf_op jit(solution)/shard_map/ppermute | solution.py:27
  41.5 15.0 %collective-permute-start.18 = (bf16[160,2048]{1,0:T(8,128)(2,1)S(1)}, bf16[160,2048]{1,0:T(8,128)(2,1)S(1)}, u32[]{:S(2)}, u32[]{:S(2)}) collective-permute-start(bf16[160,2048]{1,0:T(8,128)(2,1)S(1)} %join_rows.1.refs_2_.refs_0_.refs_1_), channel_id=1, source_target_pairs={{0,1},{1,0},{2,3},{3,2},{4,5},{5,4},{6,7},{7,6},{8,9},{9,8},{10,11... | collective-permute-start | bytes 1966088 | tf_op jit(solution)/shard_map/ppermute | solution.py:27
  41.6 14.9 %collective-permute-start.19 = (bf16[160,2048]{1,0:T(8,128)(2,1)S(1)}, bf16[160,2048]{1,0:T(8,128)(2,1)S(1)}, u32[]{:S(2)}, u32[]{:S(2)}) collective-permute-start(bf16[160,2048]{1,0:T(8,128)(2,1)S(1)} %collective-permute-done.8.refs_3_.refs_2_), channel_id=1, source_target_pairs={{0,1},{1,0},{2,3},{3,2},{4,5},{5,4},{6,7},{7,6},{8,9},{9,8},{10,11... | collective-permute-start | bytes 1966088 | tf_op jit(solution)/shard_map/ppermute | solution.py:27
  42.2 7.1 %collective-permute-start.12 = (bf16[80,1024]{1,0:T(8,128)(2,1)S(1)}, bf16[80,1024]{1,0:T(8,128)(2,1)S(1)}, u32[]{:S(2)}, u32[]{:S(2)}) collective-permute-start(bf16[80,1024]{1,0:T(8,128)(2,1)S(1)} %get-tuple-element.49), channel_id=1, source_target_pairs={{0,2},{1,3},{2,0},{3,1},{4,6},{5,7},{6,4},{7,5},{8,10},{9,11},{10,... | collective-permute-start | bytes 491528 | tf_op jit(solution)/shard_map/ppermute | solution.py:27
  44.1 9.6 %collective-permute-start.15 = (bf16[80,1024]{1,0:T(8,128)(2,1)S(1)}, bf16[80,1024]{1,0:T(8,128)(2,1)S(1)}, u32[]{:S(2)}, u32[]{:S(2)}) collective-permute-start(bf16[80,1024]{1,0:T(8,128)(2,1)S(1)} %get-tuple-element.52.refs_12_), channel_id=1, source_target_pairs={{0,2},{1,3},{2,0},{3,1},{4,6},{5,7},{6,4},{7,5},{8,10},{9,11},{10,... | collective-permute-start | bytes 491528 | tf_op jit(solution)/shard_map/ppermute | solution.py:27
  49.4 15.3 %collective-permute-start.13 = (bf16[80,1024]{1,0:T(8,128)(2,1)S(1)}, bf16[80,1024]{1,0:T(8,128)(2,1)S(1)}, u32[]{:S(2)}, u32[]{:S(2)}) collective-permute-start(bf16[80,1024]{1,0:T(8,128)(2,1)S(1)} %add_convert_fusion.6), channel_id=1, source_target_pairs={{0,4},{1,5},{2,6},{3,7},{4,0},{5,1},{6,2},{7,3},{8,12},{9,13},{10,... | collective-permute-start | bytes 491528 | tf_op jit(solution)/shard_map/ppermute | solution.py:27
  53.6 12.4 %collective-permute-start.17 = (bf16[80,2048]{1,0:T(8,128)(2,1)S(1)}, bf16[80,2048]{1,0:T(8,128)(2,1)S(1)}, u32[]{:S(2)}, u32[]{:S(2)}) collective-permute-start(bf16[80,2048]{1,0:T(8,128)(2,1)S(1)} %pad_maximum_fusion), channel_id=1, source_target_pairs={{0,2},{1,3},{2,0},{3,1},{4,6},{5,7},{6,4},{7,5},{8,10},{9,11},{10,... | collective-permute-start | bytes 983048 | tf_op jit(solution)/shard_map/ppermute | solution.py:27
  54.5 10.7 %collective-permute-start.16 = (bf16[80,1024]{1,0:T(8,128)(2,1)S(1)}, bf16[80,1024]{1,0:T(8,128)(2,1)S(1)}, u32[]{:S(2)}, u32[]{:S(2)}) collective-permute-start(bf16[80,1024]{1,0:T(8,128)(2,1)S(1)} %add_convert_fusion.2), channel_id=1, source_target_pairs={{0,4},{1,5},{2,6},{3,7},{4,0},{5,1},{6,2},{7,3},{8,12},{9,13},{10,... | collective-permute-start | bytes 491528 | tf_op jit(solution)/shard_map/ppermute | solution.py:27

commit v4 on v3

--- a/solution.py
+++ b/solution.py
@@ -156,7 +156,7 @@
     cos_ref, sin_ref = refs[blocks : blocks + 2]
     dq_refs, packet_refs = refs[blocks + 2 : blocks + 4], refs[blocks + 4 : blocks + 6]
     k_all, v_all, ds_all, w_all, bias_ref, scores_ref, dweights_ref = refs[blocks + 6 :]
-    together = scores_ref.shape[0] // bias_ref.shape[0]
+    together = min(4, heads)
     tokens = q_all.shape[0] // heads
     width = dq_refs[0].shape[1]
     keys = tokens * blocks
@@ -182,9 +182,9 @@
     for h in range(heads):
         if h % together == 0:
             rows = slice(h * tokens, (h + together) * tokens)
-            scores_ref[...] = contract(q_all[rows, :], k_all[...], 1, 1)
-            dweights_ref[...] = contract(o_all[rows, :], v_all[...], 1, 1)
-        rows = slice(h % together * tokens, (h % together + 1) * tokens)
+            scores_ref[rows, :] = contract(q_all[rows, :], k_all[...], 1, 1)
+            dweights_ref[rows, :] = contract(o_all[rows, :], v_all[...], 1, 1)
+        rows = slice(h * tokens, (h + 1) * tokens)
         scores = scores_ref[rows, :] + bias_ref[...]
         peak = jnp.max(scores, axis=1, keepdims=True)
         terms = jnp.exp2((scores - peak) * (scale * math.log2(math.e)))
@@ -193,7 +193,6 @@
         weights = terms * inverse
         delta = jnp.sum(weights * dweights, axis=1, keepdims=True)
         dscores = (weights * (dweights - delta) * scale).astype(jnp.bfloat16)
-        rows = slice(h * tokens, (h + 1) * tokens)
         w_all[rows, :] = weights.astype(jnp.bfloat16)
         ds_all[rows, :] = dscores
     dq = contract(ds_all[...], k_all[...], 1, 0)
@@ -233,8 +232,8 @@
             pltpu.VMEM((heads * tokens, keys), jnp.bfloat16),
             pltpu.VMEM((heads * tokens, keys), jnp.bfloat16),
             pltpu.VMEM((tokens, keys), jnp.float32),
-            pltpu.VMEM((min(4, heads) * tokens, keys), jnp.float32),
-            pltpu.VMEM((min(4, heads) * tokens, keys), jnp.float32),
+            pltpu.VMEM((heads * tokens, keys), jnp.float32),
+            pltpu.VMEM((heads * tokens, keys), jnp.float32),
         ],
         compiler_params=pltpu.CompilerParams(vmem_limit_bytes=32 * MIB),
         cost_estimate=pl.CostEstimate(

time: 67.2 us -> 67.2 us (level)
  no operation moved by 1% of the time
where the time goes in v4:
time: 67.2 us; the launch traced here: 66.9 us
  Pallas kernels  28.3 us (42%)
  starting transfers between devices  24.2 us (36%)
  waiting for transfers between devices  13.1 us (19%)
  between operations  0.78 us (1%)
    ppermute x20, starting transfers between devices, swap(): return lax.ppermute(value, axis, pairs)  24.2 us
    ppermute x20, waiting for transfers between devices, swap(): return lax.ppermute(value, axis, pairs)  13.1 us
    pallas_call x1, Pallas kernels, weight_grads(): pl.pallas_call(functools.partial(weight_grad_kernel, places), grid=(featu...  8.14 us
    pallas_call x1, Pallas kernels, attention_backward(): pl.pallas_call(functools.partial(attention_kernel, heads, blocks), out_sh...  4.05 us
    pallas_call x2, Pallas kernels, last_product(): pl.pallas_call(functools.partial(last_kernel, early, late, columns, offse...  3.73 us
    pallas_call x1, Pallas kernels, turn_weights(): pl.pallas_call(functools.partial(turn_kernel, tile), out_shape=pltpu.VMEM...  3.44 us
    pallas_call x1, Pallas kernels, early_product(): pl.pallas_call(functools.partial(early_kernel, columns, tile), out_shape=...  3.31 us
    pallas_call x1, Pallas kernels, prepare(): pl.pallas_call(functools.partial(prepare_kernel, heads, blocks), out_shap...  2.25 us
  transfers between devices with their start and end apart: 20, of which 10 were waited for; matrix products, arithmetic and copies ran while one was open for 1% of the time, Pallas kernels for 38%

profile of v4, /device:TPU:0, one launch (start us, length us, event | category | flops | bytes accessed | tf_op | source)
XLA Modules:
  0.0 66.9 jit_solution(4553379558045638868)
XLA Ops:
  0.6 4.1 %collective-permute-start.7 = (bf16[80,2048]{1,0:T(8,128)(2,1)}, bf16[80,2048]{1,0:T(8,128)(2,1)S(1)}, u32[]{:S(2)}, u32[]{:S(2)}) collective-permute-start(bf16[80,2048]{1,0:T(8,128)(2,1)} %refs_0_.1), channel_id=1, source_target_pairs={{0,4},{1,5},{2,6},{3,7},{4,0},{5,1},{6,2},{7,3},{8,12},{9,13},{10,... | collective-permute-start | bytes 983048 | tf_op jit(solution)/shard_map/ppermute | solution.py:27
  4.7 0.8 %pack.1.refs_0_ = bf16[176,256]{1,0:T(8,128)(2,1)S(1)} custom-call(bf16[160,128]{1,0:T(8,128)(2,1)} %k_ref.1, bf16[160,128]{1,0:T(8,128)(2,1)} %v_ref.1, s32[1,160]{1,0:T(1,128)} %bitcast.5), custom_call_target="tpu_custom_call" | custom-call | bytes 163840 | tf_op jit(solution)/shard_map/pack/pallas_call | solution.py:71
  5.6 2.5 %collective-permute-start.2 = (bf16[176,256]{1,0:T(8,128)(2,1)S(1)}, bf16[176,256]{1,0:T(8,128)(2,1)S(1)}, u32[]{:S(2)}, u32[]{:S(2)}) collective-permute-start(bf16[176,256]{1,0:T(8,128)(2,1)S(1)} %pack.1.refs_0_), channel_id=1, source_target_pairs={{0,24},{8,16},{16,8},{24,0},{1,25},{9,17},{17,9},{25,1},{2,26},{10... | collective-permute-start | bytes 270344 | tf_op jit(solution)/shard_map/ppermute | solution.py:27
  8.1 0.5 collective-permute-start.1
  8.6 0.5 collective-permute-start
  9.1 2.2 %prepare.1 = (bf16[1280,128]{1,0:T(8,128)(2,1)S(1)}, bf16[1280,128]{1,0:T(8,128)(2,1)S(1)}, f32[640,128]{1,0:T(8,128)S(1)}, f32[640,128]{1,0:T(8,128)S(1)}) custom-call(s32[1]{0:T(128)} %bitcast.2.row_ref, bf16[160,1024]{1,0:T(8,128)(2,1)} %q_hbm.1, bf16[160,1024]{1,0:T(8,128)(2,1)} %o_hbm.1, s32[1,160]{1,0:T(1,128)} %bitcast.7, s32[1,160]{1,0:T(1,128)} %bitcast.6, ...), custom_call_target="tpu_custom_call" | custom-call | bytes 1310720 | tf_op jit(solution)/shard_map/prepare/pallas_call | solution.py:130
  11.4 1.5 %collective-permute-done.1.refs_2_ = bf16[176,256]{1,0:T(8,128)(2,1)S(1)} collective-permute-done((bf16[176,256]{1,0:T(8,128)(2,1)S(1)}, bf16[176,256]{1,0:T(8,128)(2,1)S(1)}, u32[]{:S(2)}, u32[]{:S(2)}) %collective-permute-start.1) | collective-permute-done | bytes 90144 | tf_op jit(solution)/shard_map/ppermute | solution.py:27
  12.8 0.3 collective-permute-done.refs_1_
  13.1 4.0 %attention_backward.1 = (bf16[160,512]{1,0:T(8,128)(2,1)S(1)}, bf16[160,512]{1,0:T(8,128)(2,1)}, bf16[160,1024]{1,0:T(8,128)(2,1)S(1)}, bf16[160,1024]{1,0:T(8,128)(2,1)S(1)}) custom-call(s32[1]{0:T(128)} %bitcast.2.row_ref, bf16[1280,128]{1,0:T(8,128)(2,1)S(1)} %get-tuple-element.26.q_all, bf16[1280,128]{1,0:T(8,128)(2,1)S(1)} %get-tuple-element.27.o_all, ...), custom_call_target="tpu_custom_call" | custom-call | flops 1048576000 | bytes 2621440 | tf_op jit(solution)/shard_map/attention_backward/pallas_call | solution.py:223
  17.2 1.0 %collective-permute-start.3 = (bf16[160,1024]{1,0:T(8,128)(2,1)S(1)}, bf16[160,1024]{1,0:T(8,128)(2,1)S(1)}, u32[]{:S(2)}, u32[]{:S(2)}) collective-permute-start(bf16[160,1024]{1,0:T(8,128)(2,1)S(1)} %get-tuple-element.31.refs_0_), channel_id=1, source_target_pairs={{0,8},{8,0},{16,24},{24,16},{1,9},{9,1},{17,25},{25,17},{2,10},{10... | collective-permute-start | bytes 983048 | tf_op jit(solution)/shard_map/ppermute | solution.py:27
  18.1 1.1 %collective-permute-start.6 = (bf16[160,1024]{1,0:T(8,128)(2,1)S(1)}, bf16[160,1024]{1,0:T(8,128)(2,1)S(1)}, u32[]{:S(2)}, u32[]{:S(2)}) collective-permute-start(bf16[160,1024]{1,0:T(8,128)(2,1)S(1)} %get-tuple-element.33.refs_0_), channel_id=1, source_target_pairs={{0,16},{8,24},{16,0},{24,8},{1,17},{9,25},{17,1},{25,9},{2,18},{10... | collective-permute-start | bytes 983048 | tf_op jit(solution)/shard_map/ppermute | solution.py:27
  19.2 0.5 collective-permute-done.7.refs_1_
  19.7 0.2 join_rows.1.refs_2_.refs_0_.refs_1_
  19.9 1.2 %collective-permute-start.8 = (bf16[160,2048]{1,0:T(8,128)(2,1)S(1)}, bf16[160,2048]{1,0:T(8,128)(2,1)S(1)}, u32[]{:S(2)}, u32[]{:S(2)}) collective-permute-start(bf16[160,2048]{1,0:T(8,128)(2,1)S(1)} %join_rows.1.refs_2_.refs_0_.refs_1_), channel_id=1, source_target_pairs={{0,2},{1,3},{2,0},{3,1},{4,6},{5,7},{6,4},{7,5},{8,10},{9,11},{10,... | collective-permute-start | bytes 1966088 | tf_op jit(solution)/shard_map/ppermute | solution.py:27
  21.1 1.5 %collective-permute-start.5 = (bf16[160,512]{1,0:T(8,128)(2,1)}, bf16[160,512]{1,0:T(8,128)(2,1)}, u32[]{:S(2)}, u32[]{:S(2)}) collective-permute-start(bf16[160,512]{1,0:T(8,128)(2,1)} %get-tuple-element.32.refs_3_.refs_4_), channel_id=1, source_target_pairs={{0,8},{8,0},{16,24},{24,16},{1,9},{9,1},{17,25},{25,17},{2,10},{10... | collective-permute-start | bytes 491528 | tf_op jit(solution)/shard_map/ppermute | solution.py:27
  22.6 1.2 %collective-permute-start.4 = (bf16[160,512]{1,0:T(8,128)(2,1)S(1)}, bf16[160,512]{1,0:T(8,128)(2,1)}, u32[]{:S(2)}, u32[]{:S(2)}) collective-permute-start(bf16[160,512]{1,0:T(8,128)(2,1)S(1)} %get-tuple-element.30.refs_0_.refs_2_), channel_id=1, source_target_pairs={{0,16},{8,24},{16,0},{24,8},{1,17},{9,25},{17,1},{25,9},{2,18},{10... | collective-permute-start | bytes 491528 | tf_op jit(solution)/shard_map/ppermute | solution.py:27
  23.8 4.0 %collective-permute-done.3.refs_1_.refs_2_ = bf16[160,1024]{1,0:T(8,128)(2,1)S(1)} collective-permute-done((bf16[160,1024]{1,0:T(8,128)(2,1)S(1)}, bf16[160,1024]{1,0:T(8,128)(2,1)S(1)}, u32[]{:S(2)}, u32[]{:S(2)}) %collective-permute-start.3) | collective-permute-done | bytes 327712 | tf_op jit(solution)/shard_map/ppermute | solution.py:27
  27.8 0.1 combine.2.refs_0_.refs_6_.refs_5_.refs_8_
  27.9 0.9 %collective-permute-start.9 = (bf16[160,1024]{1,0:T(8,128)(2,1)S(1)}, bf16[160,1024]{1,0:T(8,128)(2,1)S(1)}, u32[]{:S(2)}, u32[]{:S(2)}) collective-permute-start(bf16[160,1024]{1,0:T(8,128)(2,1)S(1)} %combine.2.refs_0_.refs_6_.refs_5_.refs_8_), channel_id=1, source_target_pairs={{0,16},{8,24},{16,0},{24,8},{1,17},{9,25},{17,1},{25,9},{2,18},{10... | collective-permute-start | bytes 983048 | tf_op jit(solution)/shard_map/ppermute | solution.py:27
  28.7 0.1 collective-permute-done.6.refs_5_.refs_1_.refs_2_.refs_6_
  28.8 0.1 combine.3.refs_8_.refs_7_.refs_10_
  28.9 1.1 %collective-permute-start.10 = (bf16[160,1024]{1,0:T(8,128)(2,1)S(1)}, bf16[160,1024]{1,0:T(8,128)(2,1)S(1)}, u32[]{:S(2)}, u32[]{:S(2)}) collective-permute-start(bf16[160,1024]{1,0:T(8,128)(2,1)S(1)} %combine.3.refs_8_.refs_7_.refs_10_), channel_id=1, source_target_pairs={{0,8},{8,0},{16,24},{24,16},{1,9},{9,1},{17,25},{25,17},{2,10},{10... | collective-permute-start | bytes 983048 | tf_op jit(solution)/shard_map/ppermute | solution.py:27
  30.0 0.1 pad_add_fusion.place_ref
  30.0 3.4 %turn_weights.1.refs_6_.refs_1_ = bf16[1280,2048]{1,0:T(8,128)(2,1)S(1)} custom-call(bf16[2048,1024]{1,0:T(8,128)(2,1)} %wq_hbm.1, bf16[2048,128]{1,0:T(8,128)(2,1)} %wk_hbm.1, bf16[2048,128]{1,0:T(8,128)(2,1)} %wv_hbm.1, bf16[160,1024]{1,0:T(8,128)(2,1)S(1)} %combine.2.refs_0_.refs_6_.refs_5_.refs_8_), custom_call_target="tpu_custom_call" | custom-call | bytes 10485760 | tf_op jit(solution)/shard_map/turn_weights/pallas_call | solution.py:337
  33.5 3.3 %early_product.1.refs_0_ = bf16[480,2048]{1,0:T(8,128)(2,1)S(1)} custom-call(bf16[160,512]{1,0:T(8,128)(2,1)S(1)} %get-tuple-element.30.refs_0_.refs_2_, bf16[160,1024]{1,0:T(8,128)(2,1)S(1)} %collective-permute-done.3.refs_1_.refs_2_, bf16[160,512]{1,0:T(8,128)(2,1)} %collective-permute-done.4.refs_2_, bf16[160,512]{1,0:T(8,128)(2,1)} %get-tuple-element.32.refs_3_.refs_4_, ...), custom_call_target="tpu_custom_call" | custom-call | flops 2013265920 | bytes 7143424 | tf_op jit(solution)/shard_map/early_product/pallas_call | solution.py:376
  36.8 0.3 collective-permute-done.9.refs_4_.refs_7_.refs_3_.refs_6_.refs_9_
  37.1 1.8 %last_product.2 = (bf16[80,1024]{1,0:T(8,128)(2,1)S(1)}, bf16[80,1024]{1,0:T(8,128)(2,1)S(1)}, bf16[80,1024]{1,0:T(8,128)(2,1)S(1)}, bf16[80,1024]{1,0:T(8,128)(2,1)S(1)}, bf16[320,1024]{1,0:T(8,128)(2,1)S(1)}) custom-call(s32[2]{0:T(128)S(1)} %pad_add_fusion.place_ref, bf16[480,2048]{1,0:T(8,128)(2,1)S(1)} %early_product.1.refs_0_, ...), custom_call_target="tpu_custom_call" | custom-call | flops 671088640 | bytes 7864320 | tf_op jit(solution)/shard_map/last_product/pallas_call | solution.py:479
  38.9 0.1 collective-permute-start.11
  39.0 2.0 %last_product.3 = (bf16[80,1024]{1,0:T(8,128)(2,1)S(1)}, bf16[80,1024]{1,0:T(8,128)(2,1)S(1)}, bf16[80,1024]{1,0:T(8,128)(2,1)S(1)}, bf16[80,1024]{1,0:T(8,128)(2,1)S(1)}, bf16[320,1024]{1,0:T(8,128)(2,1)S(1)}) custom-call(s32[2]{0:T(128)S(1)} %pad_add_fusion.place_ref, bf16[480,2048]{1,0:T(8,128)(2,1)S(1)} %early_product.1.refs_0_, ...), custom_call_target="tpu_custom_call" | custom-call | flops 671088640 | bytes 7864320 | tf_op jit(solution)/shard_map/last_product/pallas_call | solution.py:479
  40.9 0.6 collective-permute-start.14
  41.5 0.1 collective-permute-start.18
  41.6 0.4 collective-permute-start.19
  42.0 0.2 add_convert_fusion.1
  42.2 1.7 %collective-permute-start.12 = (bf16[80,1024]{1,0:T(8,128)(2,1)S(1)}, bf16[80,1024]{1,0:T(8,128)(2,1)S(1)}, u32[]{:S(2)}, u32[]{:S(2)}) collective-permute-start(bf16[80,1024]{1,0:T(8,128)(2,1)S(1)} %get-tuple-element.49), channel_id=1, source_target_pairs={{0,2},{1,3},{2,0},{3,1},{4,6},{5,7},{6,4},{7,5},{8,10},{9,11},{10,... | collective-permute-start | bytes 491528 | tf_op jit(solution)/shard_map/ppermute | solution.py:27
  43.9 0.2 add_convert_fusion
  44.1 1.0 %collective-permute-start.15 = (bf16[80,1024]{1,0:T(8,128)(2,1)S(1)}, bf16[80,1024]{1,0:T(8,128)(2,1)S(1)}, u32[]{:S(2)}, u32[]{:S(2)}) collective-permute-start(bf16[80,1024]{1,0:T(8,128)(2,1)S(1)} %get-tuple-element.52.refs_12_), channel_id=1, source_target_pairs={{0,2},{1,3},{2,0},{3,1},{4,6},{5,7},{6,4},{7,5},{8,10},{9,11},{10,... | collective-permute-start | bytes 491528 | tf_op jit(solution)/shard_map/ppermute | solution.py:27
  45.1 1.3 %order_rows.1.g_ref = bf16[640,1280]{1,0:T(8,128)(2,1)S(1)} custom-call(s32[2]{0:T(128)S(1)} %pad_add_fusion.place_ref, bf16[160,512]{1,0:T(8,128)(2,1)S(1)} %get-tuple-element.30.refs_0_.refs_2_, bf16[160,1024]{1,0:T(8,128)(2,1)S(1)} %collective-permute-done.3.refs_1_.refs_2_, bf16[160,512]{1,0:T(8,128)(2,1)} %collective-permute-done.4.refs_2_, ...), custom_call_target="tpu_custom_call" | custom-call | bytes 3276800 | tf_op jit(solution)/shard_map/order_rows/pallas_call | solution.py:528
  46.5 2.8 %collective-permute-done.12 = bf16[80,1024]{1,0:T(8,128)(2,1)S(1)} collective-permute-done((bf16[80,1024]{1,0:T(8,128)(2,1)S(1)}, bf16[80,1024]{1,0:T(8,128)(2,1)S(1)}, u32[]{:S(2)}, u32[]{:S(2)}) %collective-permute-start.12) | collective-permute-done | bytes 163872 | tf_op jit(solution)/shard_map/ppermute | solution.py:27
  49.3 0.1 add_convert_fusion.6
  49.4 1.9 %collective-permute-start.13 = (bf16[80,1024]{1,0:T(8,128)(2,1)S(1)}, bf16[80,1024]{1,0:T(8,128)(2,1)S(1)}, u32[]{:S(2)}, u32[]{:S(2)}) collective-permute-start(bf16[80,1024]{1,0:T(8,128)(2,1)S(1)} %add_convert_fusion.6), channel_id=1, source_target_pairs={{0,4},{1,5},{2,6},{3,7},{4,0},{5,1},{6,2},{7,3},{8,12},{9,13},{10,... | collective-permute-start | bytes 491528 | tf_op jit(solution)/shard_map/ppermute | solution.py:27
  51.3 2.3 %collective-permute-done.15 = bf16[80,1024]{1,0:T(8,128)(2,1)S(1)} collective-permute-done((bf16[80,1024]{1,0:T(8,128)(2,1)S(1)}, bf16[80,1024]{1,0:T(8,128)(2,1)S(1)}, u32[]{:S(2)}, u32[]{:S(2)}) %collective-permute-start.15) | collective-permute-done | bytes 163872 | tf_op jit(solution)/shard_map/ppermute | solution.py:27
  53.6 0.8 %collective-permute-start.17 = (bf16[80,2048]{1,0:T(8,128)(2,1)S(1)}, bf16[80,2048]{1,0:T(8,128)(2,1)S(1)}, u32[]{:S(2)}, u32[]{:S(2)}) collective-permute-start(bf16[80,2048]{1,0:T(8,128)(2,1)S(1)} %pad_maximum_fusion), channel_id=1, source_target_pairs={{0,2},{1,3},{2,0},{3,1},{4,6},{5,7},{6,4},{7,5},{8,10},{9,11},{10,... | collective-permute-start | bytes 983048 | tf_op jit(solution)/shard_map/ppermute | solution.py:27
  54.5 0.1 add_convert_fusion.2
  54.5 2.0 %collective-permute-start.16 = (bf16[80,1024]{1,0:T(8,128)(2,1)S(1)}, bf16[80,1024]{1,0:T(8,128)(2,1)S(1)}, u32[]{:S(2)}, u32[]{:S(2)}) collective-permute-start(bf16[80,1024]{1,0:T(8,128)(2,1)S(1)} %add_convert_fusion.2), channel_id=1, source_target_pairs={{0,4},{1,5},{2,6},{3,7},{4,0},{5,1},{6,2},{7,3},{8,12},{9,13},{10,... | collective-permute-start | bytes 491528 | tf_op jit(solution)/shard_map/ppermute | solution.py:27
  56.5 8.1 %weight_grads.1 = (f32[2048,1024]{1,0:T(8,128)}, f32[2048,128]{1,0:T(8,128)}, f32[2048,128]{1,0:T(8,128)}) custom-call(bf16[640,1280]{1,0:T(8,128)(2,1)S(1)} %order_rows.1.g_ref, bf16[160,2048]{1,0:T(8,128)(2,1)S(1)} %join_rows.1.refs_2_.refs_0_.refs_1_, bf16[160,2048]{1,0:T(8,128)(2,1)S(1)} %join_rows.1.refs_2_.refs_0_.refs_1_, ...), custom_call_target="tpu_custom_call" | custom-call | flops 3355443200 | bytes 14745600 | tf_op jit(solution)/shard_map/weight_grads/pallas_call | solution.py:596
  64.6 0.5 collective-permute-done.16.refs_3_
  65.2 0.9 %collective-permute-done.17.refs_4_ = bf16[80,2048]{1,0:T(8,128)(2,1)S(1)} collective-permute-done((bf16[80,2048]{1,0:T(8,128)(2,1)S(1)}, bf16[80,2048]{1,0:T(8,128)(2,1)S(1)}, u32[]{:S(2)}, u32[]{:S(2)}) %collective-permute-start.17) | collective-permute-done | bytes 327712 | tf_op jit(solution)/shard_map/ppermute | solution.py:27
  66.1 0.8 %sum_rows.1 = bf16[80,2048]{1,0:T(8,128)(2,1)} custom-call(bf16[80,1024]{1,0:T(8,128)(2,1)S(1)} %get-tuple-element.50.refs_0_, bf16[80,1024]{1,0:T(8,128)(2,1)S(1)} %collective-permute-done.13.refs_1_, bf16[80,1024]{1,0:T(8,128)(2,1)S(1)} %get-tuple-element.53.refs_2_, bf16[80,1024]{1,0:T(8,128)(2,1)S(1)} %collective-permute-done.16.refs_3_, ...), custom_call_target="tpu_custom_call" | custom-call | flops 409600 | bytes 1638400 | tf_op jit(solution)/shard_map/sum_rows/pallas_call | solution.py:644
  (13 shorter events, 0.1 us)
Async XLA Ops:
  0.6 19.1 %copy-start = (bf16[80,2048]{1,0:T(8,128)(2,1)S(1)}, bf16[80,2048]{1,0:T(8,128)(2,1)}, u32[]{:S(2)}) copy-start(bf16[80,2048]{1,0:T(8,128)(2,1)} %refs_0_.1) | copy-start | bytes 983044
  0.6 19.0 %collective-permute-start.7 = (bf16[80,2048]{1,0:T(8,128)(2,1)}, bf16[80,2048]{1,0:T(8,128)(2,1)S(1)}, u32[]{:S(2)}, u32[]{:S(2)}) collective-permute-start(bf16[80,2048]{1,0:T(8,128)(2,1)} %refs_0_.1), channel_id=1, source_target_pairs={{0,4},{1,5},{2,6},{3,7},{4,0},{5,1},{6,2},{7,3},{8,12},{9,13},{10,... | collective-permute-start | bytes 983048 | tf_op jit(solution)/shard_map/ppermute | solution.py:27
  5.6 5.8 %collective-permute-start.2 = (bf16[176,256]{1,0:T(8,128)(2,1)S(1)}, bf16[176,256]{1,0:T(8,128)(2,1)S(1)}, u32[]{:S(2)}, u32[]{:S(2)}) collective-permute-start(bf16[176,256]{1,0:T(8,128)(2,1)S(1)} %pack.1.refs_0_), channel_id=1, source_target_pairs={{0,24},{8,16},{16,8},{24,0},{1,25},{9,17},{17,9},{25,1},{2,26},{10... | collective-permute-start | bytes 270344 | tf_op jit(solution)/shard_map/ppermute | solution.py:27
  8.1 4.8 %collective-permute-start.1 = (bf16[176,256]{1,0:T(8,128)(2,1)S(1)}, bf16[176,256]{1,0:T(8,128)(2,1)S(1)}, u32[]{:S(2)}, u32[]{:S(2)}) collective-permute-start(bf16[176,256]{1,0:T(8,128)(2,1)S(1)} %pack.1.refs_0_), channel_id=1, source_target_pairs={{0,16},{8,24},{16,0},{24,8},{1,17},{9,25},{17,1},{25,9},{2,18},{10... | collective-permute-start | bytes 270344 | tf_op jit(solution)/shard_map/ppermute | solution.py:27
  8.6 4.5 %collective-permute-start = (bf16[176,256]{1,0:T(8,128)(2,1)S(1)}, bf16[176,256]{1,0:T(8,128)(2,1)S(1)}, u32[]{:S(2)}, u32[]{:S(2)}) collective-permute-start(bf16[176,256]{1,0:T(8,128)(2,1)S(1)} %pack.1.refs_0_), channel_id=1, source_target_pairs={{0,8},{8,0},{16,24},{24,16},{1,9},{9,1},{17,25},{25,17},{2,10},{10... | collective-permute-start | bytes 270344 | tf_op jit(solution)/shard_map/ppermute | solution.py:27
  17.2 10.6 %collective-permute-start.3 = (bf16[160,1024]{1,0:T(8,128)(2,1)S(1)}, bf16[160,1024]{1,0:T(8,128)(2,1)S(1)}, u32[]{:S(2)}, u32[]{:S(2)}) collective-permute-start(bf16[160,1024]{1,0:T(8,128)(2,1)S(1)} %get-tuple-element.31.refs_0_), channel_id=1, source_target_pairs={{0,8},{8,0},{16,24},{24,16},{1,9},{9,1},{17,25},{25,17},{2,10},{10... | collective-permute-start | bytes 983048 | tf_op jit(solution)/shard_map/ppermute | solution.py:27
  18.1 10.7 %collective-permute-start.6 = (bf16[160,1024]{1,0:T(8,128)(2,1)S(1)}, bf16[160,1024]{1,0:T(8,128)(2,1)S(1)}, u32[]{:S(2)}, u32[]{:S(2)}) collective-permute-start(bf16[160,1024]{1,0:T(8,128)(2,1)S(1)} %get-tuple-element.33.refs_0_), channel_id=1, source_target_pairs={{0,16},{8,24},{16,0},{24,8},{1,17},{9,25},{17,1},{25,9},{2,18},{10... | collective-permute-start | bytes 983048 | tf_op jit(solution)/shard_map/ppermute | solution.py:27
  19.9 17.2 %collective-permute-start.8 = (bf16[160,2048]{1,0:T(8,128)(2,1)S(1)}, bf16[160,2048]{1,0:T(8,128)(2,1)S(1)}, u32[]{:S(2)}, u32[]{:S(2)}) collective-permute-start(bf16[160,2048]{1,0:T(8,128)(2,1)S(1)} %join_rows.1.refs_2_.refs_0_.refs_1_), channel_id=1, source_target_pairs={{0,2},{1,3},{2,0},{3,1},{4,6},{5,7},{6,4},{7,5},{8,10},{9,11},{10,... | collective-permute-start | bytes 1966088 | tf_op jit(solution)/shard_map/ppermute | solution.py:27
  21.1 12.4 %collective-permute-start.5 = (bf16[160,512]{1,0:T(8,128)(2,1)}, bf16[160,512]{1,0:T(8,128)(2,1)}, u32[]{:S(2)}, u32[]{:S(2)}) collective-permute-start(bf16[160,512]{1,0:T(8,128)(2,1)} %get-tuple-element.32.refs_3_.refs_4_), channel_id=1, source_target_pairs={{0,8},{8,0},{16,24},{24,16},{1,9},{9,1},{17,25},{25,17},{2,10},{10... | collective-permute-start | bytes 491528 | tf_op jit(solution)/shard_map/ppermute | solution.py:27
  22.6 10.9 %collective-permute-start.4 = (bf16[160,512]{1,0:T(8,128)(2,1)S(1)}, bf16[160,512]{1,0:T(8,128)(2,1)}, u32[]{:S(2)}, u32[]{:S(2)}) collective-permute-start(bf16[160,512]{1,0:T(8,128)(2,1)S(1)} %get-tuple-element.30.refs_0_.refs_2_), channel_id=1, source_target_pairs={{0,16},{8,24},{16,0},{24,8},{1,17},{9,25},{17,1},{25,9},{2,18},{10... | collective-permute-start | bytes 491528 | tf_op jit(solution)/shard_map/ppermute | solution.py:27
  27.9 9.2 %collective-permute-start.9 = (bf16[160,1024]{1,0:T(8,128)(2,1)S(1)}, bf16[160,1024]{1,0:T(8,128)(2,1)S(1)}, u32[]{:S(2)}, u32[]{:S(2)}) collective-permute-start(bf16[160,1024]{1,0:T(8,128)(2,1)S(1)} %combine.2.refs_0_.refs_6_.refs_5_.refs_8_), channel_id=1, source_target_pairs={{0,16},{8,24},{16,0},{24,8},{1,17},{9,25},{17,1},{25,9},{2,18},{10... | collective-permute-start | bytes 983048 | tf_op jit(solution)/shard_map/ppermute | solution.py:27
  28.9 8.3 %collective-permute-start.10 = (bf16[160,1024]{1,0:T(8,128)(2,1)S(1)}, bf16[160,1024]{1,0:T(8,128)(2,1)S(1)}, u32[]{:S(2)}, u32[]{:S(2)}) collective-permute-start(bf16[160,1024]{1,0:T(8,128)(2,1)S(1)} %combine.3.refs_8_.refs_7_.refs_10_), channel_id=1, source_target_pairs={{0,8},{8,0},{16,24},{24,16},{1,9},{9,1},{17,25},{25,17},{2,10},{10... | collective-permute-start | bytes 983048 | tf_op jit(solution)/shard_map/ppermute | solution.py:27
  38.9 3.1 %collective-permute-start.11 = (bf16[320,1024]{1,0:T(8,128)(2,1)S(1)}, bf16[320,1024]{1,0:T(8,128)(2,1)S(1)}, u32[]{:S(2)}, u32[]{:S(2)}) collective-permute-start(bf16[320,1024]{1,0:T(8,128)(2,1)S(1)} %get-tuple-element.35), channel_id=1, source_target_pairs={{0,1},{1,0},{2,3},{3,2},{4,5},{5,4},{6,7},{7,6},{8,9},{9,8},{10,11... | collective-permute-start | bytes 1966088 | tf_op jit(solution)/shard_map/ppermute | solution.py:27
  40.9 2.9 %collective-permute-start.14 = (bf16[320,1024]{1,0:T(8,128)(2,1)S(1)}, bf16[320,1024]{1,0:T(8,128)(2,1)S(1)}, u32[]{:S(2)}, u32[]{:S(2)}) collective-permute-start(bf16[320,1024]{1,0:T(8,128)(2,1)S(1)} %get-tuple-element.39), channel_id=1, source_target_pairs={{0,1},{1,0},{2,3},{3,2},{4,5},{5,4},{6,7},{7,6},{8,9},{9,8},{10,11... | collective-permute-start | bytes 1966088 | tf_op jit(solution)/shard_map/ppermute | solution.py:27
  41.5 15.0 %collective-permute-start.18 = (bf16[160,2048]{1,0:T(8,128)(2,1)S(1)}, bf16[160,2048]{1,0:T(8,128)(2,1)S(1)}, u32[]{:S(2)}, u32[]{:S(2)}) collective-permute-start(bf16[160,2048]{1,0:T(8,128)(2,1)S(1)} %join_rows.1.refs_2_.refs_0_.refs_1_), channel_id=1, source_target_pairs={{0,1},{1,0},{2,3},{3,2},{4,5},{5,4},{6,7},{7,6},{8,9},{9,8},{10,11... | collective-permute-start | bytes 1966088 | tf_op jit(solution)/shard_map/ppermute | solution.py:27
  41.6 14.9 %collective-permute-start.19 = (bf16[160,2048]{1,0:T(8,128)(2,1)S(1)}, bf16[160,2048]{1,0:T(8,128)(2,1)S(1)}, u32[]{:S(2)}, u32[]{:S(2)}) collective-permute-start(bf16[160,2048]{1,0:T(8,128)(2,1)S(1)} %collective-permute-done.8.refs_3_.refs_2_), channel_id=1, source_target_pairs={{0,1},{1,0},{2,3},{3,2},{4,5},{5,4},{6,7},{7,6},{8,9},{9,8},{10,11... | collective-permute-start | bytes 1966088 | tf_op jit(solution)/shard_map/ppermute | solution.py:27
  42.2 7.1 %collective-permute-start.12 = (bf16[80,1024]{1,0:T(8,128)(2,1)S(1)}, bf16[80,1024]{1,0:T(8,128)(2,1)S(1)}, u32[]{:S(2)}, u32[]{:S(2)}) collective-permute-start(bf16[80,1024]{1,0:T(8,128)(2,1)S(1)} %get-tuple-element.49), channel_id=1, source_target_pairs={{0,2},{1,3},{2,0},{3,1},{4,6},{5,7},{6,4},{7,5},{8,10},{9,11},{10,... | collective-permute-start | bytes 491528 | tf_op jit(solution)/shard_map/ppermute | solution.py:27
  44.1 9.6 %collective-permute-start.15 = (bf16[80,1024]{1,0:T(8,128)(2,1)S(1)}, bf16[80,1024]{1,0:T(8,128)(2,1)S(1)}, u32[]{:S(2)}, u32[]{:S(2)}) collective-permute-start(bf16[80,1024]{1,0:T(8,128)(2,1)S(1)} %get-tuple-element.52.refs_12_), channel_id=1, source_target_pairs={{0,2},{1,3},{2,0},{3,1},{4,6},{5,7},{6,4},{7,5},{8,10},{9,11},{10,... | collective-permute-start | bytes 491528 | tf_op jit(solution)/shard_map/ppermute | solution.py:27
  49.4 15.3 %collective-permute-start.13 = (bf16[80,1024]{1,0:T(8,128)(2,1)S(1)}, bf16[80,1024]{1,0:T(8,128)(2,1)S(1)}, u32[]{:S(2)}, u32[]{:S(2)}) collective-permute-start(bf16[80,1024]{1,0:T(8,128)(2,1)S(1)} %add_convert_fusion.6), channel_id=1, source_target_pairs={{0,4},{1,5},{2,6},{3,7},{4,0},{5,1},{6,2},{7,3},{8,12},{9,13},{10,... | collective-permute-start | bytes 491528 | tf_op jit(solution)/shard_map/ppermute | solution.py:27
  53.6 12.4 %collective-permute-start.17 = (bf16[80,2048]{1,0:T(8,128)(2,1)S(1)}, bf16[80,2048]{1,0:T(8,128)(2,1)S(1)}, u32[]{:S(2)}, u32[]{:S(2)}) collective-permute-start(bf16[80,2048]{1,0:T(8,128)(2,1)S(1)} %pad_maximum_fusion), channel_id=1, source_target_pairs={{0,2},{1,3},{2,0},{3,1},{4,6},{5,7},{6,4},{7,5},{8,10},{9,11},{10,... | collective-permute-start | bytes 983048 | tf_op jit(solution)/shard_map/ppermute | solution.py:27
  54.5 10.7 %collective-permute-start.16 = (bf16[80,1024]{1,0:T(8,128)(2,1)S(1)}, bf16[80,1024]{1,0:T(8,128)(2,1)S(1)}, u32[]{:S(2)}, u32[]{:S(2)}) collective-permute-start(bf16[80,1024]{1,0:T(8,128)(2,1)S(1)} %add_convert_fusion.2), channel_id=1, source_target_pairs={{0,4},{1,5},{2,6},{3,7},{4,0},{5,1},{6,2},{7,3},{8,12},{9,13},{10,... | collective-permute-start | bytes 491528 | tf_op jit(solution)/shard_map/ppermute | solution.py:27
